TPU v7x, 32 devices: a whole 2x2x4 slice. The times are simulated.
32 devices in a mesh: fsdp: 2 (over x), ctx: 4 (over z), tp: 4 (over y, core).
Axes of the slice: x: 2, y: 2, z: 4, core: 2. Of those that a mesh axis runs over, the one named last changes fastest.
Arguments:
- tokens: bfloat16 [4096, 2048], P(('fsdp', 'ctx')), may hold values from -6 to 6
- first_gain: bfloat16 [2048], P('fsdp'), may hold values from 0.099609375 to 1.8984375
- query_weight: bfloat16 [2048, 2048], P('fsdp', 'tp'), may hold values from -0.125 to 0.125
- keyval_weight: bfloat16 [2048, 512], P('fsdp', 'tp'), may hold values from -0.125 to 0.125
- output_weight: bfloat16 [2048, 2048], P('tp', 'fsdp'), may hold values from -2 to 2
- second_gain: bfloat16 [2048], P('fsdp'), may hold values from 0.099609375 to 1.8984375
- gate_weight: bfloat16 [2048, 5632], P('fsdp', 'tp'), may hold values from -0.125 to 0.125
- up_weight: bfloat16 [2048, 5632], P('fsdp', 'tp'), may hold values from -0.125 to 0.125
- down_weight: bfloat16 [5632, 2048], P('tp', 'fsdp'), may hold values from -0.078125 to 0.078125
- segment_ids: int32 [4096], P('fsdp'), may hold values from 0 to 2049, as said below
- positions: int32 [4096], P('fsdp'), may hold values from 0 to 1023, as said below
- cotangent: bfloat16 [4096, 2048], P(('fsdp', 'ctx')), may hold values from -6 to 6
Outputs:
- activations: bfloat16 [4096, 2048], P(('fsdp', 'ctx'))
- input_grad: float32 [4096, 2048], P(('fsdp', 'ctx'))
- first_gain_grad: float32 [2048], P('fsdp')
- query_grad: float32 [2048, 2048], P('fsdp', 'tp')
- keyval_grad: float32 [2048, 512], P('fsdp', 'tp')
- output_grad: float32 [2048, 2048], P('tp', 'fsdp')
- second_gain_grad: float32 [2048], P('fsdp')
- gate_grad: float32 [2048, 5632], P('fsdp', 'tp')
- up_grad: float32 [2048, 5632], P('fsdp', 'tp')
- down_grad: float32 [5632, 2048], P('tp', 'fsdp')
Inputs may be any that keep to these rules, and one draw needn't show every extreme that they name: `segment_ids`: each group of 2048 slots holds 2 sequences with ids 0 to 1, one of exactly 1024 tokens, the others of 512 to 1023; every other slot is padding whose id is 2 plus its slot's place in the virtual order of the group, an id of its own; the last slot of that order is always padding. Slots come in tiles of 128; the tiles of one group lie in sequence order dealt in turn over the devices of ctx, in an order within a device drawn from the seed. The tokens of a sequence carry positions 0 to its length - 1, each once; padding slots carry 0.
All inputs are finite; a program needn't handle non-finite values.
Results may differ from a plain program's by a relative error of at most 0.014.
Values may be sent and summed in bfloat16 or wider, within the bound.
No kernel may reach another device: no remote copies, remote signals or barrier semaphores. Data moves between devices by JAX's collectives and lax.ppermute only.
A program may use at most 192 MiB of HBM per device.

v0:
```python
import math

import jax
import jax.numpy as jnp
from jax import lax
from jax.sharding import PartitionSpec as P

HD = 64


epsilon = 1e-05


def rotate(values, places):
    half = values.shape[-1] // 2
    ladder = jnp.arange(half).astype(values.dtype)
    freqs = jnp.exp(ladder * (-2.0 * math.log(10000.0) / values.shape[-1]))
    angles = places.astype(values.dtype)[:, None] * freqs[None, :]
    cosine = jnp.cos(angles)[:, None, :]
    sine = jnp.sin(angles)[:, None, :]
    former = values[..., :half]
    latter = values[..., half:]
    return jnp.concatenate(
        [former * cosine - latter * sine, latter * cosine + former * sine], axis=-1
    )


def unrotate(values, places):
    half = values.shape[-1] // 2
    ladder = jnp.arange(half).astype(values.dtype)
    freqs = jnp.exp(ladder * (-2.0 * math.log(10000.0) / values.shape[-1]))
    angles = places.astype(values.dtype)[:, None] * freqs[None, :]
    cosine = jnp.cos(angles)[:, None, :]
    sine = jnp.sin(angles)[:, None, :]
    former = values[..., :half]
    latter = values[..., half:]
    return jnp.concatenate(
        [former * cosine + latter * sine, latter * cosine - former * sine], axis=-1
    )


def rms_scale(values):
    return lax.rsqrt(jnp.mean(values * values, axis=-1, keepdims=True) + epsilon)


def norm_back(values, scale, gain, upstream):
    weighted = upstream * gain
    return scale * weighted - values * scale**3 * jnp.mean(
        values * weighted, axis=-1, keepdims=True
    )


def per_device(
    tokens,
    first_gain,
    query_weight,
    keyval_weight,
    output_weight,
    second_gain,
    gate_weight,
    up_weight,
    down_weight,
    segment_ids,
    positions,
    cotangent,
):
    shards = (
        first_gain,
        query_weight,
        keyval_weight,
        output_weight,
        second_gain,
        gate_weight,
        up_weight,
        down_weight,
    )
    gathered = (
        lax.all_gather(shards[0], "fsdp", axis=0, tiled=True),
        lax.all_gather(shards[1], "fsdp", axis=0, tiled=True),
        lax.all_gather(shards[2], "fsdp", axis=0, tiled=True),
        lax.all_gather(shards[3], "fsdp", axis=1, tiled=True),
        lax.all_gather(shards[4], "fsdp", axis=0, tiled=True),
        lax.all_gather(shards[5], "fsdp", axis=0, tiled=True),
        lax.all_gather(shards[6], "fsdp", axis=0, tiled=True),
        lax.all_gather(shards[7], "fsdp", axis=1, tiled=True),
    )
    (
        full_gain_one,
        full_query,
        full_keyval,
        full_output,
        full_gain_two,
        full_gate,
        full_upper,
        full_down,
    ) = gathered
    token_rows = tokens.shape[0]
    group_rows = segment_ids.shape[0]
    offset = lax.axis_index("ctx") * token_rows
    own_segments = lax.dynamic_slice_in_dim(segment_ids, offset, token_rows)
    own_places = lax.dynamic_slice_in_dim(positions, offset, token_rows)
    inputs = tokens.astype(jnp.float32)
    gain_first = full_gain_one.astype(jnp.float32)
    gain_second = full_gain_two.astype(jnp.float32)
    scale_first = rms_scale(inputs)
    normed_first = (inputs * scale_first * gain_first).astype(jnp.bfloat16)
    query_pre = jnp.dot(normed_first, full_query, preferred_element_type=jnp.float32)
    keyval_pre = jnp.dot(normed_first, full_keyval, preferred_element_type=jnp.float32)
    head_local = query_pre.shape[1] // HD
    pair_local = keyval_pre.shape[1] // (2 * HD)
    group_size = head_local // pair_local
    queries = rotate(query_pre.reshape(token_rows, head_local, HD), own_places).astype(jnp.bfloat16)
    keyval_split = keyval_pre.reshape(token_rows, pair_local, 2, HD)
    keys_own = rotate(keyval_split[:, :, 0], own_places).astype(jnp.bfloat16)
    values_own = keyval_split[:, :, 1].astype(jnp.bfloat16)
    packed = jnp.stack([keys_own, values_own], axis=2).reshape(token_rows, pair_local * 2 * HD)
    group_pairs = lax.all_gather(packed, "ctx", axis=0, tiled=True).reshape(
        group_rows, pair_local, 2, HD
    )
    keys_head = jnp.transpose(group_pairs[:, :, 0], (1, 0, 2))
    values_head = jnp.transpose(group_pairs[:, :, 1], (1, 0, 2))
    query_head = jnp.transpose(queries, (1, 0, 2))
    block_rows = min(512, token_rows)
    blocks = token_rows // block_rows
    steps_total = blocks * head_local

    def take_rows(stack, head_index):
        chosen = lax.dynamic_index_in_dim(stack, head_index, 0, False)
        return chosen

    def scores_for(index):
        block_index = index // head_local
        head_index = index % head_local
        pair_index = head_index // group_size
        query_block = take_rows(query_head, head_index)
        keys_pair = lax.dynamic_index_in_dim(keys_head, pair_index, 0, False)
        values_pair = lax.dynamic_index_in_dim(values_head, pair_index, 0, False)
        allowed = (own_segments[:, None] == segment_ids[None, :]) & (
            positions[None, :] <= own_places[:, None]
        )
        raw = (
            jnp.einsum("qd,kd->qk", query_block, keys_pair, preferred_element_type=jnp.float32)
            * 0.125
        )
        return (
            jnp.where(allowed, raw, -1e30),
            query_block,
            keys_pair,
            values_pair,
            pair_index,
            head_index,
            block_index,
        )

    def forward_step(index):
        scores, query_block, keys_pair, values_pair, pair_index, head_index, block_index = (
            scores_for(index)
        )
        highest = jnp.max(scores, axis=-1, keepdims=True)
        expos = jnp.exp(scores - highest)
        totals = jnp.sum(expos, axis=-1, keepdims=True)
        probs = (expos / totals).astype(jnp.bfloat16)
        mixed = jnp.einsum("qk,kd->qd", probs, values_pair, preferred_element_type=jnp.float32)
        return (mixed, (highest + jnp.log(totals))[:, 0])

    mixed_all, logsum = lax.map(forward_step, jnp.arange(steps_total))
    mixed_rows = jnp.transpose(mixed_all.reshape(blocks, head_local, block_rows, HD), (0, 2, 1, 3))
    mixed_low = mixed_rows.reshape(token_rows, head_local * HD).astype(jnp.bfloat16)
    attn_part = jnp.dot(mixed_low, full_output, preferred_element_type=jnp.float32)
    attn_whole = lax.psum(attn_part, "tp")
    hidden_one = inputs + attn_whole
    scale_second = rms_scale(hidden_one)
    normed_second = (hidden_one * scale_second * gain_second).astype(jnp.bfloat16)
    gate = jnp.dot(normed_second, full_gate, preferred_element_type=jnp.float32)
    upper = jnp.dot(normed_second, full_upper, preferred_element_type=jnp.float32)
    sigma = jax.nn.sigmoid(gate)
    swish = gate * sigma
    hidden = (swish * upper).astype(jnp.bfloat16)
    ffn_part = jnp.dot(hidden, full_down, preferred_element_type=jnp.float32)
    ffn_whole = lax.psum(ffn_part.astype(jnp.bfloat16), "tp").astype(jnp.float32)
    output_rows = (hidden_one + ffn_whole).astype(jnp.bfloat16)
    upstream = cotangent.astype(jnp.float32)
    down_full = jnp.einsum("rf,rd->fd", hidden, cotangent, preferred_element_type=jnp.float32)
    grad_hidden = jnp.einsum("rd,fd->rf", cotangent, full_down, preferred_element_type=jnp.float32)
    grad_gate = (grad_hidden * upper * sigma * (1.0 + gate * (1.0 - sigma))).astype(jnp.bfloat16)
    grad_upper = (grad_hidden * swish).astype(jnp.bfloat16)
    gate_full = jnp.einsum(
        "rd,rf->df", normed_second, grad_gate, preferred_element_type=jnp.float32
    )
    upper_full = jnp.einsum(
        "rd,rf->df", normed_second, grad_upper, preferred_element_type=jnp.float32
    )
    second_part = jnp.einsum("rf,df->rd", grad_gate, full_gate, preferred_element_type=jnp.float32)
    second_part = second_part + jnp.einsum(
        "rf,df->rd", grad_upper, full_upper, preferred_element_type=jnp.float32
    )
    grad_second = lax.psum(second_part, "tp")
    gain_two_full = jnp.sum(grad_second * hidden_one * scale_second, axis=0)
    grad_hidden_one = upstream + norm_back(hidden_one, scale_second, gain_second, grad_second)
    grad_attn = grad_hidden_one.astype(jnp.bfloat16)
    output_full = jnp.einsum("rh,rd->hd", mixed_low, grad_attn, preferred_element_type=jnp.float32)
    grad_mixed = jnp.einsum(
        "rd,hd->rh", grad_attn, full_output, preferred_element_type=jnp.float32
    ).astype(jnp.bfloat16)
    grad_head = jnp.transpose(grad_mixed.reshape(token_rows, head_local, HD), (1, 0, 2))

    def backward_step(carry, member):
        index, lse_rows = member
        scores, query_block, keys_pair, values_pair, pair_index, head_index, block_index = (
            scores_for(index)
        )
        probs = jnp.exp(scores - lse_rows[:, None])
        grad_block = take_rows(grad_head, head_index)
        grad_probs = jnp.einsum(
            "qd,kd->qk", grad_block, values_pair, preferred_element_type=jnp.float32
        )
        centre = jnp.sum(probs * grad_probs, axis=-1, keepdims=True)
        grad_scores = (probs * (grad_probs - centre)).astype(jnp.bfloat16)
        grad_query = 0.125 * jnp.einsum(
            "qk,kd->qd", grad_scores, keys_pair, preferred_element_type=jnp.float32
        )
        key_term = 0.125 * jnp.einsum(
            "qk,qd->kd", grad_scores, query_block, preferred_element_type=jnp.float32
        )
        value_term = jnp.einsum(
            "qk,qd->kd", probs.astype(jnp.bfloat16), grad_block, preferred_element_type=jnp.float32
        )
        keys_acc, values_acc = carry
        keys_acc = lax.dynamic_update_index_in_dim(
            keys_acc,
            lax.dynamic_index_in_dim(keys_acc, pair_index, 0, False) + key_term,
            pair_index,
            0,
        )
        values_acc = lax.dynamic_update_index_in_dim(
            values_acc,
            lax.dynamic_index_in_dim(values_acc, pair_index, 0, False) + value_term,
            pair_index,
            0,
        )
        return ((keys_acc, values_acc), grad_query)

    empty_pairs = jnp.zeros((pair_local, group_rows, HD), jnp.float32)
    (keys_acc, values_acc), query_rot = lax.scan(
        backward_step, (empty_pairs, empty_pairs), (jnp.arange(steps_total), logsum)
    )
    pair_terms = jnp.transpose(jnp.stack([keys_acc, values_acc], axis=2), (1, 0, 2, 3)).reshape(
        group_rows, pair_local * 2 * HD
    )
    pair_own = lax.psum_scatter(pair_terms, "ctx", scatter_dimension=0, tiled=True).reshape(
        token_rows, pair_local, 2, HD
    )
    grad_keys = unrotate(pair_own[:, :, 0], own_places).astype(jnp.bfloat16)
    grad_values = pair_own[:, :, 1].astype(jnp.bfloat16)
    grad_keyval = jnp.stack([grad_keys, grad_values], axis=2).reshape(
        token_rows, pair_local * 2 * HD
    )
    query_rows = jnp.transpose(
        query_rot.reshape(blocks, head_local, block_rows, HD), (0, 2, 1, 3)
    ).reshape(token_rows, head_local, HD)
    grad_query_low = (
        unrotate(query_rows, own_places).reshape(token_rows, head_local * HD).astype(jnp.bfloat16)
    )
    query_full = jnp.einsum(
        "rd,rh->dh", normed_first, grad_query_low, preferred_element_type=jnp.float32
    )
    keyval_full = jnp.einsum(
        "rd,rh->dh", normed_first, grad_keyval, preferred_element_type=jnp.float32
    )
    first_part = jnp.einsum(
        "rh,dh->rd", grad_query_low, full_query, preferred_element_type=jnp.float32
    )
    first_part = first_part + jnp.einsum(
        "rh,dh->rd", grad_keyval, full_keyval, preferred_element_type=jnp.float32
    )
    grad_first = lax.psum(first_part, "tp")
    gain_one_full = jnp.sum(grad_first * inputs * scale_first, axis=0)
    input_grad = grad_hidden_one + norm_back(inputs, scale_first, gain_first, grad_first)
    gradients = (
        gain_one_full,
        query_full,
        keyval_full,
        output_full,
        gain_two_full,
        gate_full,
        upper_full,
        down_full,
    )
    pieces = (
        lax.psum_scatter(gradients[0], ("fsdp", "ctx"), scatter_dimension=0, tiled=True),
        lax.psum_scatter(gradients[1], ("fsdp", "ctx"), scatter_dimension=0, tiled=True),
        lax.psum_scatter(gradients[2], ("fsdp", "ctx"), scatter_dimension=0, tiled=True),
        lax.psum_scatter(gradients[3], ("fsdp", "ctx"), scatter_dimension=1, tiled=True),
        lax.psum_scatter(gradients[4], ("fsdp", "ctx"), scatter_dimension=0, tiled=True),
        lax.psum_scatter(gradients[5], ("fsdp", "ctx"), scatter_dimension=0, tiled=True),
        lax.psum_scatter(gradients[6], ("fsdp", "ctx"), scatter_dimension=0, tiled=True),
        lax.psum_scatter(gradients[7], ("fsdp", "ctx"), scatter_dimension=1, tiled=True),
    )
    reduced = (
        lax.all_gather(pieces[0], "ctx", axis=0, tiled=True),
        lax.all_gather(pieces[1], "ctx", axis=0, tiled=True),
        lax.all_gather(pieces[2], "ctx", axis=0, tiled=True),
        lax.all_gather(pieces[3], "ctx", axis=1, tiled=True),
        lax.all_gather(pieces[4], "ctx", axis=0, tiled=True),
        lax.all_gather(pieces[5], "ctx", axis=0, tiled=True),
        lax.all_gather(pieces[6], "ctx", axis=0, tiled=True),
        lax.all_gather(pieces[7], "ctx", axis=1, tiled=True),
    )
    return (
        output_rows,
        input_grad,
        reduced[0],
        reduced[1],
        reduced[2],
        reduced[3],
        reduced[4],
        reduced[5],
        reduced[6],
        reduced[7],
    )


def solution(mesh):
    placed = (
        P(("fsdp", "ctx"), None),
        P("fsdp"),
        P("fsdp", "tp"),
        P("fsdp", "tp"),
        P("tp", "fsdp"),
        P("fsdp"),
        P("fsdp", "tp"),
        P("fsdp", "tp"),
        P("tp", "fsdp"),
        P("fsdp"),
        P("fsdp"),
        P(("fsdp", "ctx"), None),
    )
    return jax.shard_map(
        per_device,
        mesh=mesh,
        in_specs=placed,
        out_specs=(
            P(("fsdp", "ctx"), None),
            P(("fsdp", "ctx"), None),
            P("fsdp"),
            P("fsdp", "tp"),
            P("fsdp", "tp"),
            P("tp", "fsdp"),
            P("fsdp"),
            P("fsdp", "tp"),
            P("fsdp", "tp"),
            P("tp", "fsdp"),
        ),
        check_vma=False,
    )
```

profile of v0, /device:TPU:8, one launch (start us, length us, event | category | flops | bytes accessed | tf_op | source)
XLA Modules:
  0.0 2142.4 jit_solution(7321478418355437070)
XLA Ops:
  11.4 4.3 all_gather.51
  15.8 12.0 all_gather.53
  31.8 15.2 all_gather.54
  54.8 99.8 %while.32 = (s32[]{:T(128)}, bf16[8,512,64]{1,2,0:T(8,128)(2,1)}, f32[8,512]{1,0:T(8,128)}, s32[512]{0:T(512)S(1)}, s32[2048]{0:T(1024)S(1)}, /*index=5*/s32[204...) while((s32[]{:T(128)}, bf16[8,512,64]{1,2,0:T(8,128)(2,1)}, ...), condition=%wide.region_4.5_spmd.clone, body=%wide.region_1.4_spmd.sunk.clone | while | flops 279969280 | bytes 30188332 | solution.py:166
  76.0 3.8 fusion.149
  100.9 3.8 fusion.149
  125.9 3.8 fusion.149
  150.8 3.8 fusion.149
  154.6 5.4 fusion.74
  161.9 5.2 all_gather.56
  167.1 80.7 %all-reduce.8.cloned.1.call-done = f32[512,2048]{1,0:T(8,128)} async-done(((f32[512,2048]{1,0:T(8,128)}), f32[512,2048]{1,0:T(8,128)}) %all-reduce.8.cloned.1.call-update) | async-done | bytes 4194320 | tf_op jit(solution)/shard_map/psum | solution.py:170
  254.4 69.5 %all-gather.17.cloned.1.call-done = bf16[2048,1408]{1,0:T(8,128)(2,1)} async-done(((bf16[1024,1408]{1,0:T(8,128)(2,1)}), bf16[2048,1408]{1,0:T(8,128)(2,1)}) %all-gather.17.cloned.1.call-update) | async-done | bytes 5767184 | tf_op jit(solution)/shard_map/all_gather | solution.py:83
  323.9 8.3 fusion.75
  332.2 67.7 %all-gather.19.cloned.1.call-done = bf16[2048,1408]{1,0:T(8,128)(2,1)} async-done(((bf16[1024,1408]{1,0:T(8,128)(2,1)}), bf16[2048,1408]{1,0:T(8,128)(2,1)}) %all-gather.19.cloned.1.call-update) | async-done | bytes 5767184 | tf_op jit(solution)/shard_map/all_gather | solution.py:84
  399.9 8.3 fusion.76
  408.1 67.7 %all-gather.21.cloned.1.call-done = bf16[1408,2048]{1,0:T(8,128)(2,1)} async-done(((bf16[1408,1024]{1,0:T(8,128)(2,1)}), bf16[1408,2048]{1,0:T(8,128)(2,1)}) %all-gather.21.cloned.1.call-update) | async-done | bytes 5767184 | tf_op jit(solution)/shard_map/all_gather | solution.py:85
  475.8 10.4 multiply_convert_fusion.2
  486.2 6.6 fusion.77
  492.9 5.0 convolution_add_fusion.2
  498.1 7.8 convolution_convert_fusion
  506.0 77.5 %all-reduce.12.cloned.1.call-done = f32[512,2048]{1,0:T(8,128)} async-done(((f32[512,2048]{1,0:T(8,128)}), f32[512,2048]{1,0:T(8,128)}) %all-reduce.12.cloned.1.call-update) | async-done | bytes 4194320 | tf_op jit(solution)/shard_map/psum | solution.py:197
  583.5 4.5 multiply_reduce_fusion.1
  588.1 50.0 %all-reduce.10.cloned.1.call-done = bf16[512,2048]{1,0:T(8,128)(2,1)} async-done(((bf16[512,2048]{1,0:T(8,128)(2,1)}), bf16[512,2048]{1,0:T(8,128)(2,1)}) %all-reduce.10.cloned.1.call-update) | async-done | bytes 2097168 | tf_op jit(solution)/shard_map/psum | solution.py:180
  638.0 6.6 subtract_add_fusion
  649.4 103.3 %while.33 = (s32[]{:T(128)}, f32[1,2048,64]{1,2,0:T(8,128)S(1)}, f32[1,2048,64]{1,2,0:T(8,128)S(1)}, f32[8,512,64]{1,2,0:T(8,128)}, s32[512]{0:T(512)S(1)}, /*in...) while((s32[]{:T(128)}, f32[1,2048,64]{1,2,0:T(8,128)S(1)}, ...), condition=%wide.region_12.13_spmd.clone, body=%wide.region_10.12_spmd.sunk.clone | while | flops 684097024 | bytes 36338512 | solution.py:244
  753.8 5.6 fusion.41
  764.8 9.8 fusion.79
  774.6 9.7 fusion.80
  784.4 9.4 fusion.81
  793.9 5.0 fusion.78
  801.1 5.0 convolution_add_fusion.1
  808.4 64.0 %reduce-scatter.14.cloned.1.call-done = f32[512,256]{1,0:T(8,128)} async-done(((f32[512,2048]{1,0:T(8,128)}), f32[512,256]{1,0:T(8,128)}) %reduce-scatter.14.cloned.1.call-update) | async-done | bytes 524304 | tf_op jit(solution)/shard_map/reduce_scatter | solution.py:293
  872.5 92.3 %reduce-scatter.10.cloned.1.call-done = f32[256,512]{1,0:T(8,128)} async-done(((f32[2048,512]{1,0:T(8,128)}), f32[256,512]{1,0:T(8,128)}) %reduce-scatter.10.cloned.1.call-update) | async-done | bytes 524304 | tf_op jit(solution)/shard_map/reduce_scatter | solution.py:291
  964.9 193.9 %reduce-scatter.16.cloned.1.call-done = f32[256,1408]{1,0:T(8,128)} async-done(((f32[2048,1408]{1,0:T(8,128)}), f32[256,1408]{1,0:T(8,128)}) %reduce-scatter.16.cloned.1.call-update) | async-done | bytes 1441808 | tf_op jit(solution)/shard_map/reduce_scatter | solution.py:295
  1158.9 195.3 %reduce-scatter.18.cloned.1.call-done = f32[256,1408]{1,0:T(8,128)} async-done(((f32[2048,1408]{1,0:T(8,128)}), f32[256,1408]{1,0:T(8,128)}) %reduce-scatter.18.cloned.1.call-update) | async-done | bytes 1441808 | tf_op jit(solution)/shard_map/reduce_scatter | solution.py:296
  1354.3 195.6 %reduce-scatter.20.cloned.1.call-done = f32[1408,256]{1,0:T(8,128)} async-done(((f32[1408,2048]{1,0:T(8,128)}), f32[1408,256]{1,0:T(8,128)}) %reduce-scatter.20.cloned.1.call-update) | async-done | bytes 1441808 | tf_op jit(solution)/shard_map/reduce_scatter | solution.py:297
  1551.1 87.8 %all-reduce.14.cloned.1.call-done = f32[512,2048]{1,0:T(8,128)} async-done(((f32[512,2048]{1,0:T(8,128)}), f32[512,2048]{1,0:T(8,128)}) %all-reduce.14.cloned.1.call-update) | async-done | bytes 4194320 | tf_op jit(solution)/shard_map/psum | solution.py:276
  1642.4 32.9 %all-reduce.2 = (f32[2048]{0:T(1024)S(1)}, f32[2048]{0:T(1024)S(1)}) all-reduce(f32[2048]{0:T(1024)S(1)} %get-tuple-element.407, f32[2048]{0:T(1024)S(1)} %get-tuple-element.405), channel_id=3, replica_groups=mesh['fsdp'=2,'ctx'=4,'tp'=4] {'fsdp','ctx'}, use_global_device_ids=true, to_apply=%region_17.18.clone | all-reduce | flops 4096 | bytes 32768
  1675.4 12.5 all-gather
  1688.0 7.6 all-gather.1
  1695.5 11.2 reduce-scatter.12.cloned.1.call-done
  1706.7 16.8 all_gather.62
  1723.5 6.6 fusion.36
  1730.1 23.9 %all-gather.25.cloned.1.call-done = f32[512,1024]{1,0:T(8,128)} async-done(((f32[512,256]{1,0:T(8,128)}), f32[512,1024]{1,0:T(8,128)}) %all-gather.25.cloned.1.call-update) | async-done | bytes 2097168 | tf_op jit(solution)/shard_map/all_gather | solution.py:303
  1754.0 45.9 %all-gather.23.cloned.1.call-done = f32[1024,512]{1,0:T(8,128)} async-done(((f32[256,512]{1,0:T(8,128)}), f32[1024,512]{1,0:T(8,128)}) %all-gather.23.cloned.1.call-update) | async-done | bytes 2097168 | tf_op jit(solution)/shard_map/all_gather | solution.py:301
  1799.8 105.7 %all-gather.27.cloned.1.call-done = f32[1024,1408]{1,0:T(8,128)} async-done(((f32[256,1408]{1,0:T(8,128)}), f32[1024,1408]{1,0:T(8,128)}) %all-gather.27.cloned.1.call-update) | async-done | bytes 5767184 | tf_op jit(solution)/shard_map/all_gather | solution.py:305
  1905.6 106.5 %all-gather.29.cloned.1.call-done = f32[1024,1408]{1,0:T(8,128)} async-done(((f32[256,1408]{1,0:T(8,128)}), f32[1024,1408]{1,0:T(8,128)}) %all-gather.29.cloned.1.call-update) | async-done | bytes 5767184 | tf_op jit(solution)/shard_map/all_gather | solution.py:306
  2012.0 106.6 %all-gather.31.cloned.1.call-done = f32[1408,1024]{1,0:T(8,128)} async-done(((f32[1408,256]{1,0:T(8,128)}), f32[1408,1024]{1,0:T(8,128)}) %all-gather.31.cloned.1.call-update) | async-done | bytes 5767184 | tf_op jit(solution)/shard_map/all_gather | solution.py:307
  (316 shorter events, 217.1 us)
Async XLA Ops:
  7.2 21.4 copy-start.2
  7.2 4.2 copy-start.27
  7.2 8.6 copy-start.19
  7.2 41.2 %all-gather.13.cloned.1.call-start = ((), (), s32[]{:S(2)}) async-start(), calls=%async_computation.7 | async-start | bytes 3145728 | tf_op jit(solution)/shard_map/all_gather | solution.py:79
  7.9 146.7 %all-gather.15.cloned.1.call-start = ((), (), s32[]{:S(2)}) async-start(), calls=%async_computation.8 | async-start | bytes 3145728 | tf_op jit(solution)/shard_map/all_gather | solution.py:81
  8.7 239.1 %all-reduce.8.cloned.1.call-start = ((), (), s32[]{:S(2)}) async-start(), calls=%async_computation.9 | async-start | bytes 8388608 | tf_op jit(solution)/shard_map/psum | solution.py:170
  8.8 23.1 %copy-start.25 = (f32[32]{0:T(128)}, f32[32]{0:T(128)S(1)}, u32[]{:S(2)}) copy-start(f32[32]{0:T(128)S(1)} %multiply_exponential_fusion) | copy-start | bytes 388
  11.4 37.0 %copy-start.20 = (f32[512]{0:T(512)}, f32[512]{0:T(512)S(1)}, u32[]{:S(2)}) copy-start(f32[512]{0:T(512)S(1)} %get-tuple-element.487) | copy-start | bytes 6148
  15.8 32.6 %copy-start.17 = (f32[2048]{0:T(1024)}, f32[2048]{0:T(1024)S(1)}, u32[]{:S(2)}) copy-start(f32[2048]{0:T(1024)S(1)} %convert_element_type.124) | copy-start | bytes 24580
  31.1 16.2 copy-start.22
  31.5 19.9 copy-start.13
  31.5 19.9 copy-start.15
  51.4 3.4 copy-start.29
  51.4 3.4 copy-start.30
  154.6 5.5 copy-start.4
  154.6 5.5 copy-start.5
  160.1 163.8 %all-gather.17.cloned.1.call-start = ((), (), s32[]{:S(2)}) async-start(), calls=%async_computation.10 | async-start | bytes 8650752 | tf_op jit(solution)/shard_map/all_gather | solution.py:83
  160.7 239.2 %all-gather.19.cloned.1.call-start = ((), (), s32[]{:S(2)}) async-start(), calls=%async_computation.11 | async-start | bytes 8650752 | tf_op jit(solution)/shard_map/all_gather | solution.py:84
  161.3 314.6 %all-gather.21.cloned.1.call-start = ((), (), s32[]{:S(2)}) async-start(), calls=%async_computation.12 | async-start | bytes 8650752 | tf_op jit(solution)/shard_map/all_gather | solution.py:85
  161.9 421.7 %all-reduce.12.cloned.1.call-start = ((), (), s32[]{:S(2)}) async-start(), calls=%async_computation.14 | async-start | bytes 8388608 | tf_op jit(solution)/shard_map/psum | solution.py:197
  486.2 6.6 copy-start.34
  486.2 6.6 copy-start.33
  486.2 6.6 copy-start.31
  497.9 140.1 %all-reduce.10.cloned.1.call-start = ((), (), s32[]{:S(2)}) async-start(), calls=%async_computation.13 | async-start | bytes 4194304 | tf_op jit(solution)/shard_map/psum | solution.py:180
  506.0 292.9 %reduce-scatter.8.cloned.1.call-start = ((), (), s32[]{:S(2)}) async-start(), calls=%async_computation.15 | async-start | bytes 1310720 | tf_op jit(solution)/shard_map/reduce_scatter | solution.py:250
  638.0 8.7 copy-start.10
  753.7 118.7 %reduce-scatter.14.cloned.1.call-start = ((), (), s32[]{:S(2)}) async-start(), calls=%async_computation.20 | async-start | bytes 4718592 | tf_op jit(solution)/shard_map/reduce_scatter | solution.py:293
  759.5 205.3 %reduce-scatter.10.cloned.1.call-start = ((), (), s32[]{:S(2)}) async-start(), calls=%async_computation.17 | async-start | bytes 4718592 | tf_op jit(solution)/shard_map/reduce_scatter | solution.py:291
  764.5 394.3 %reduce-scatter.16.cloned.1.call-start = ((), (), s32[]{:S(2)}) async-start(), calls=%async_computation.22 | async-start | bytes 12976128 | tf_op jit(solution)/shard_map/reduce_scatter | solution.py:295
  774.6 579.6 %reduce-scatter.18.cloned.1.call-start = ((), (), s32[]{:S(2)}) async-start(), calls=%async_computation.24 | async-start | bytes 12976128 | tf_op jit(solution)/shard_map/reduce_scatter | solution.py:296
  784.3 765.5 %reduce-scatter.20.cloned.1.call-start = ((), (), s32[]{:S(2)}) async-start(), calls=%async_computation.26 | async-start | bytes 12976128 | tf_op jit(solution)/shard_map/reduce_scatter | solution.py:297
  793.8 6.9 copy-start.23
  793.9 6.9 copy-start.26
  793.9 7.2 copy-start.9
  793.9 845.0 %all-reduce.14.cloned.1.call-start = ((), (), s32[]{:S(2)}) async-start(), calls=%async_computation.16 | async-start | bytes 8388608 | tf_op jit(solution)/shard_map/psum | solution.py:276
  806.1 900.6 %reduce-scatter.12.cloned.1.call-start = ((), (), s32[]{:S(2)}) async-start(), calls=%async_computation.19 | async-start | bytes 1179648 | tf_op jit(solution)/shard_map/reduce_scatter | solution.py:292
  808.3 741.5 %copy-start.32 = (u32[32]{0:T(128)S(1)}, u32[32]{0:T(128)}, u32[]{:S(2)}) copy-start(u32[32]{0:T(128)} %constant.180) | copy-start | bytes 388
  808.4 945.6 %all-gather.25.cloned.1.call-start = ((), (), s32[]{:S(2)}) async-start(), calls=%async_computation.21 | async-start | bytes 2621440 | tf_op jit(solution)/shard_map/all_gather | solution.py:303
  872.5 927.4 %all-gather.23.cloned.1.call-start = ((), (), s32[]{:S(2)}) async-start(), calls=%async_computation.18 | async-start | bytes 2621440 | tf_op jit(solution)/shard_map/all_gather | solution.py:301
  964.8 940.7 %all-gather.27.cloned.1.call-start = ((), (), s32[]{:S(2)}) async-start(), calls=%async_computation.23 | async-start | bytes 7208960 | tf_op jit(solution)/shard_map/all_gather | solution.py:305
  1158.8 853.2 %all-gather.29.cloned.1.call-start = ((), (), s32[]{:S(2)}) async-start(), calls=%async_computation.25 | async-start | bytes 7208960 | tf_op jit(solution)/shard_map/all_gather | solution.py:306
  1354.2 764.4 %all-gather.31.cloned.1.call-start = ((), (), s32[]{:S(2)}) async-start(), calls=%async_computation.27 | async-start | bytes 7208960 | tf_op jit(solution)/shard_map/all_gather | solution.py:307
  1549.8 173.7 %copy-start.24 = (f32[512]{0:T(512)S(1)}, f32[512]{0:T(512)}, u32[]{:S(2)}) copy-start(f32[512]{0:T(512)} %get-tuple-element.486) | copy-start | bytes 6148
  1754.0 369.3 %copy-start.11 = (f32[512,1024]{1,0:T(8,128)S(1)}, f32[512,1024]{1,0:T(8,128)}, u32[]{:S(2)}) copy-start(f32[512,1024]{1,0:T(8,128)} %all-gather.25.cloned.1.call-done) | copy-start | bytes 6291460
  2119.2 6.0 copy-start.7
  2123.3 4.9 slice-start
  2125.2 6.9 slice-start.2
  2128.3 4.3 slice-start.3
  (26 other events, 54.0 us)
Sparse Core Ops, SparseCore 0:
  9.6 36.4 all-gather.12
  47.6 34.2 all-gather.14
  160.2 87.5 all-reduce.7
  249.3 74.5 all-gather.16
  325.4 74.4 all-gather.18
  401.3 74.4 all-gather.20
  498.0 85.4 all-reduce.11
  586.5 51.5 all-reduce.9
  753.8 25.0 reduce-scatter.7
  783.0 89.3 reduce-scatter.13
  877.1 87.6 reduce-scatter.9
  968.2 190.5 reduce-scatter.15
  1162.4 191.7 reduce-scatter.17
  1357.7 192.1 reduce-scatter.19
  1552.6 86.2 all-reduce.13
  1643.1 63.5 reduce-scatter.11
  1708.1 45.8 all-gather.24
  1755.4 44.3 all-gather.22
  1801.4 104.1 all-gather.26
  1907.0 104.9 all-gather.28
  2013.6 104.9 all-gather.30
where the time goes:
time: 2160 us; the launch traced here: 2140 us
  waiting for transfers between devices  1640 us (76%)
  matrix products  227 us (11%)
  blocking collectives  107 us (5%)
  local copies, waits for them, and re-layouts  72.3 us (3%)
  other arithmetic  42.3 us (2%)
  loops' own time  32 us (1%)
    reduce_scatter x1, waiting for transfers between devices, per_device(): lax.psum_scatter(gradients[7], ('fsdp', 'ctx'), scatter_dimension=1, tile...  196 us
    reduce_scatter x1, waiting for transfers between devices, per_device(): lax.psum_scatter(gradients[6], ('fsdp', 'ctx'), scatter_dimension=0, tile...  195 us
    reduce_scatter x1, waiting for transfers between devices, per_device(): lax.psum_scatter(gradients[5], ('fsdp', 'ctx'), scatter_dimension=0, tile...  194 us
    all_gather x1, waiting for transfers between devices, per_device(): lax.all_gather(pieces[7], 'ctx', axis=1, tiled=True)  107 us
    all_gather x1, waiting for transfers between devices, per_device(): lax.all_gather(pieces[6], 'ctx', axis=0, tiled=True)  106 us
    all_gather x1, waiting for transfers between devices, per_device(): lax.all_gather(pieces[5], 'ctx', axis=0, tiled=True)  106 us
    reduce_scatter x1, waiting for transfers between devices, per_device(): lax.psum_scatter(gradients[1], ('fsdp', 'ctx'), scatter_dimension=0, tile...  92.3 us
    psum x1, waiting for transfers between devices, per_device(): grad_first = lax.psum(first_part, 'tp')  87.8 us
  transfers between devices with their start and end apart: 21, of which 18 were waited for; matrix products, arithmetic and copies ran while one was open for 8% of the time, Pallas kernels for 0%

commit v1 on v0

v1 whole, which is shorter than its diff:
```python
import functools
import math

import jax
import jax.numpy as jnp
from jax import lax
from jax.experimental import pallas as pl
from jax.experimental.pallas import tpu as pltpu
from jax.sharding import PartitionSpec as P

HD = 64
TILE = 128
CODE = 4096
NEGATIVE = -1e30
epsilon = 1e-05
MIB = 2**20


def dot(left, right, over_left, over_right):
    return lax.dot_general(
        left,
        right,
        (((over_left,), (over_right,)), ((), ())),
        preferred_element_type=jnp.float32,
    )


def swap(value, axis, size, distance):
    pairs = [(i, i ^ distance) for i in range(size)]
    return lax.ppermute(value, axis, pairs)


def shift(value, axis, size, distance):
    pairs = [(i, (i + distance) % size) for i in range(size)]
    return lax.ppermute(value, axis, pairs)


def bit_of(axis, distance):
    return (lax.axis_index(axis) // distance) % 2


def scatter_rows(part, axis, size):
    distance = 1
    while distance < size:
        halves = part.reshape((2, part.shape[0] // 2) + part.shape[1:])
        bit = bit_of(axis, distance)
        give = lax.dynamic_index_in_dim(halves, 1 - bit, 0, False).astype(jnp.bfloat16)
        keep = lax.dynamic_index_in_dim(halves, bit, 0, False)
        part = keep.astype(jnp.float32) + swap(give, axis, size, distance).astype(jnp.float32)
        distance *= 2
    return part


def own_rows(whole, axis, size):
    distance = 1
    while distance < size:
        halves = whole.reshape((2, whole.shape[0] // 2) + whole.shape[1:])
        whole = lax.dynamic_index_in_dim(halves, bit_of(axis, distance), 0, False)
        distance *= 2
    return whole


def in_order(bit, mine, other, dim):
    return jnp.where(
        bit == 0,
        jnp.concatenate([mine, other], axis=dim),
        jnp.concatenate([other, mine], axis=dim),
    )


def gather_rows(rows, axis, size):
    distance = size // 2
    while distance >= 1:
        other = swap(rows, axis, size, distance)
        rows = in_order(bit_of(axis, distance), rows, other, 0)
        distance //= 2
    return rows


def sum_all(value, axis, size):
    distance = 1
    while distance < size:
        value = value + swap(value, axis, size, distance)
        distance *= 2
    return value


def gather_weight(shard, size, dim):
    if size != 2:
        return lax.all_gather(shard, "fsdp", axis=dim, tiled=True)
    return in_order(lax.axis_index("fsdp"), shard, swap(shard, "fsdp", 2, 1), dim)


def line_sum(pieces, size):
    if size != 4:
        return [lax.psum(piece.astype(jnp.float32), "ctx") for piece in pieces]
    place = lax.axis_index("ctx")
    inner = (place == 1) | (place == 2)
    done = []
    for piece in pieces:
        low = piece.astype(jnp.bfloat16)
        low = low + lax.ppermute(low, "ctx", [(0, 1), (3, 2)])
        low = low + lax.ppermute(low, "ctx", [(1, 2), (2, 1)])
        final = lax.ppermute(low, "ctx", [(1, 0), (2, 3)])
        done.append(jnp.where(inner, low, final).astype(jnp.float32))
    return done


def attend_kernel(
    heads, count, tiles, q, kv, q_code, q_base, k_code, mixed, lse, top, total, acc
):
    step = pl.program_id(0)
    top[...] = jnp.full_like(top, NEGATIVE)
    total[...] = jnp.zeros_like(total)
    acc[...] = jnp.zeros_like(acc)
    code, base = q_code[...], q_base[...]

    def body(j, carry):
        tile = tiles[step, j]
        keys = kv[tile, :HD]
        values = kv[tile, HD:]
        key_code = k_code[tile]
        allowed = (key_code <= code) & (key_code >= base)
        for h in range(heads):
            scores = jnp.where(allowed, dot(keys, q[h], 0, 0), NEGATIVE)
            before = top[h : h + 1]
            highest = jnp.maximum(before, jnp.max(scores, axis=0, keepdims=True))
            probs = jnp.exp(scores - highest)
            fade = jnp.exp(before - highest)
            top[h : h + 1] = highest
            total[h : h + 1] = total[h : h + 1] * fade + jnp.sum(probs, axis=0, keepdims=True)
            acc[h] = acc[h] * fade + dot(values, probs.astype(jnp.bfloat16), 1, 0)
        return carry

    lax.fori_loop(0, count[step], body, 0)
    sums = total[...]
    lse[...] = top[...] + jnp.log(sums)
    inverse = 1.0 / sums
    for h in range(heads):
        mixed[h] = acc[h] * inverse[h : h + 1]


def attend(count, tiles, q, kv, q_code, q_base, k_code):
    heads, _, rows = q.shape
    stack = pl.BlockSpec(kv.shape, lambda i, *_: (0, 0, 0))
    codes = pl.BlockSpec(k_code.shape, lambda i, *_: (0, 0, 0))
    line = pl.BlockSpec((1, TILE), lambda i, *_: (0, i))
    block = pl.BlockSpec((heads, HD, TILE), lambda i, *_: (0, 0, i))
    return pl.pallas_call(
        functools.partial(attend_kernel, heads),
        grid_spec=pltpu.PrefetchScalarGridSpec(
            num_scalar_prefetch=2,
            grid=(rows // TILE,),
            in_specs=[block, stack, line, line, codes],
            out_specs=[block, pl.BlockSpec((heads, TILE), lambda i, *_: (0, i))],
            scratch_shapes=[
                pltpu.VMEM((heads, TILE), jnp.float32),
                pltpu.VMEM((heads, TILE), jnp.float32),
                pltpu.VMEM((heads, HD, TILE), jnp.float32),
            ],
        ),
        out_shape=[
            jax.ShapeDtypeStruct((heads, HD, rows), jnp.float32),
            jax.ShapeDtypeStruct((heads, rows), jnp.float32),
        ],
        compiler_params=pltpu.CompilerParams(vmem_limit_bytes=32 * MIB),
        cost_estimate=pl.CostEstimate(
            flops=10 * 10**9, bytes_accessed=4 * MIB, transcendentals=4 * MIB
        ),
    )(count, tiles, q, kv, q_code, q_base, k_code)


def attend_back_kernel(
    heads, count, tiles, q, kv, q_code, q_base, k_code, mixed, lse, upstream, dq, dkv, centre
):
    step = pl.program_id(0)

    @pl.when(step == 0)
    def _():
        dkv[...] = jnp.zeros_like(dkv)

    dq[...] = jnp.zeros_like(dq)
    code, base = q_code[...], q_base[...]
    for h in range(heads):
        centre[h : h + 1] = jnp.sum(
            mixed[h] * upstream[h].astype(jnp.float32), axis=0, keepdims=True
        )

    def body(j, carry):
        tile = tiles[step, j]
        keys = kv[tile, :HD]
        values = kv[tile, HD:]
        key_code = k_code[tile]
        allowed = (key_code <= code) & (key_code >= base)
        key_term = dkv[tile, :HD]
        value_term = dkv[tile, HD:]
        for h in range(heads):
            scores = dot(keys, q[h], 0, 0) - lse[h : h + 1]
            probs = jnp.exp(jnp.where(allowed, scores, NEGATIVE))
            grad_probs = dot(values, upstream[h], 0, 0)
            grad_scores = (probs * (grad_probs - centre[h : h + 1])).astype(jnp.bfloat16)
            value_term = value_term + dot(upstream[h], probs.astype(jnp.bfloat16), 1, 1)
            key_term = key_term + dot(q[h], grad_scores, 1, 1)
            dq[h] += dot(keys, grad_scores, 1, 0)
        dkv[tile, :HD] = key_term
        dkv[tile, HD:] = value_term
        return carry

    lax.fori_loop(0, count[step], body, 0)


def attend_back(count, tiles, q, kv, q_code, q_base, k_code, mixed, lse, upstream):
    heads, _, rows = q.shape
    stack = pl.BlockSpec(kv.shape, lambda i, *_: (0, 0, 0))
    codes = pl.BlockSpec(k_code.shape, lambda i, *_: (0, 0, 0))
    line = pl.BlockSpec((1, TILE), lambda i, *_: (0, i))
    block = pl.BlockSpec((heads, HD, TILE), lambda i, *_: (0, 0, i))
    return pl.pallas_call(
        functools.partial(attend_back_kernel, heads),
        grid_spec=pltpu.PrefetchScalarGridSpec(
            num_scalar_prefetch=2,
            grid=(rows // TILE,),
            in_specs=[
                block,
                stack,
                line,
                line,
                codes,
                block,
                pl.BlockSpec((heads, TILE), lambda i, *_: (0, i)),
                block,
            ],
            out_specs=[block, stack],
            scratch_shapes=[pltpu.VMEM((heads, TILE), jnp.float32)],
        ),
        out_shape=[
            jax.ShapeDtypeStruct((heads, HD, rows), jnp.float32),
            jax.ShapeDtypeStruct(kv.shape, jnp.float32),
        ],
        compiler_params=pltpu.CompilerParams(vmem_limit_bytes=32 * MIB),
        cost_estimate=pl.CostEstimate(
            flops=30 * 10**9, bytes_accessed=6 * MIB, transcendentals=4 * MIB
        ),
    )(count, tiles, q, kv, q_code, q_base, k_code, mixed, lse, upstream)


def plan_tiles(q_code, q_base, k_code):
    rows, keys = q_code.shape[0], k_code.shape[0]
    allowed = (k_code[None, :] <= q_code[:, None]) & (k_code[None, :] >= q_base[:, None])
    used = jnp.any(allowed.reshape(rows // TILE, TILE, keys // TILE, TILE), axis=(1, 3))
    place = jnp.cumsum(used.astype(jnp.int32), axis=1) - 1
    ladder = jnp.arange(keys // TILE)
    hit = used[:, :, None] & (place[:, :, None] == ladder[None, None, :])
    tiles = jnp.sum(jnp.where(hit, ladder[None, :, None], 0), axis=1).astype(jnp.int32)
    return jnp.sum(used.astype(jnp.int32), axis=1), tiles


def middle_kernel(rows, upstream, gate_w, upper_w, down_w, hidden, dgate, dupper):
    gate = dot(rows[...], gate_w[...], 1, 0)
    upper = dot(rows[...], upper_w[...], 1, 0)
    grad = dot(upstream[...], down_w[...], 1, 1)
    sigma = 1.0 / (1.0 + jnp.exp(-gate))
    swish = gate * sigma
    hidden[...] = (swish * upper).astype(jnp.bfloat16)
    dgate[...] = (grad * upper * sigma * (1.0 + gate * (1.0 - sigma))).astype(jnp.bfloat16)
    dupper[...] = (grad * swish).astype(jnp.bfloat16)


def middle(rows, upstream, gate_w, upper_w, down_w):
    count, width = rows.shape
    units = gate_w.shape[1]
    block = 256
    whole = pl.BlockSpec((count, width), lambda i: (0, 0))
    tall = pl.BlockSpec((width, block), lambda i: (0, i))
    out = pl.BlockSpec((count, block), lambda i: (0, i))
    return pl.pallas_call(
        middle_kernel,
        grid=(pl.cdiv(units, block),),
        in_specs=[whole, whole, tall, tall, pl.BlockSpec((block, width), lambda i: (i, 0))],
        out_specs=[out, out, out],
        out_shape=[jax.ShapeDtypeStruct((count, units), jnp.bfloat16)] * 3,
        compiler_params=pltpu.CompilerParams(vmem_limit_bytes=40 * MIB),
        cost_estimate=pl.CostEstimate(
            flops=6 * count * width * units,
            bytes_accessed=6 * width * units + 4 * count * width + 6 * count * units,
            transcendentals=count * units,
        ),
    )(rows, upstream, gate_w, upper_w, down_w)


def rms_scale(values):
    return lax.rsqrt(jnp.mean(values * values, axis=-1, keepdims=True) + epsilon)


def norm_back(values, scale, gain, upstream):
    weighted = upstream * gain
    return scale * weighted - values * scale**3 * jnp.mean(
        values * weighted, axis=-1, keepdims=True
    )


def turn(values, cosine, sine):
    half = HD // 2
    former, latter = values[:, :half], values[:, half:]
    return jnp.concatenate(
        [former * cosine - latter * sine, latter * cosine + former * sine], axis=1
    )


def per_device(
    sizes,
    tokens,
    first_gain,
    query_weight,
    keyval_weight,
    output_weight,
    second_gain,
    gate_weight,
    up_weight,
    down_weight,
    segment_ids,
    positions,
    cotangent,
):
    nx, nz, nt = sizes
    low, high = jnp.bfloat16, jnp.float32
    rows, width = tokens.shape
    half = width // nx
    here_x = lax.axis_index("fsdp")
    here_z = lax.axis_index("ctx")
    paired = nx == 2

    def mine(whole):
        return lax.dynamic_slice_in_dim(whole, here_x * half, half, 1)

    def theirs(whole):
        return lax.dynamic_slice_in_dim(whole, (1 - here_x) * half, half, 1)

    heads = query_weight.shape[1] // HD
    pairs_low = keyval_weight.shape[1] // (2 * HD)
    assert pairs_low == 1
    query_width = heads * HD
    qkv_w = gather_weight(jnp.concatenate([query_weight, keyval_weight], axis=1), nx, 0)
    gains = gather_weight(jnp.stack([first_gain, second_gain]), nx, 1).astype(high)
    output_w = gather_weight(output_weight, nx, 1)
    gate_w = gather_weight(gate_weight, nx, 0)
    upper_w = gather_weight(up_weight, nx, 0)
    down_w = gather_weight(down_weight, nx, 1)
    gain_one, gain_two = gains[0], gains[1]

    codes = (segment_ids * CODE + positions).reshape(nz, rows)
    bases = (segment_ids * CODE).reshape(nz, rows)
    q_code = lax.dynamic_index_in_dim(codes, here_z, 0, False)
    q_base = lax.dynamic_index_in_dim(bases, here_z, 0, False)
    k_code = jnp.concatenate(
        [
            lax.dynamic_index_in_dim(codes, (here_z + nz - d) % nz, 0, False)
            for d in range(nz)
        ]
    )
    count, tiles = plan_tiles(q_code, q_base, k_code)
    k_wide = jnp.broadcast_to(k_code.reshape(-1, TILE, 1), (nz * rows // TILE, TILE, TILE))
    masks = (q_code[None], q_base[None], k_wide)
    places = (q_code - q_base).astype(high)
    freqs = jnp.exp(jnp.arange(HD // 2).astype(high) * (-2.0 * math.log(10000.0) / HD))
    angles = freqs[:, None] * places[None, :]
    cosine, sine = jnp.cos(angles)[None], jnp.sin(angles)[None]

    inputs = tokens.astype(high)
    scale_one = rms_scale(inputs)
    normed_one = (inputs * scale_one * gain_one).astype(low)
    qkv = dot(qkv_w, normed_one, 0, 1)
    q = turn(qkv[:query_width].reshape(heads, HD, rows), cosine, sine).astype(low) * 0.125
    k = turn(qkv[query_width : query_width + HD][None], cosine, sine)[0].astype(low)
    kv = jnp.concatenate([k, qkv[query_width + HD :].astype(low)], axis=0)
    kv = jnp.transpose(kv.reshape(2 * HD, rows // TILE, TILE), (1, 0, 2))
    kv = jnp.concatenate(
        [kv] + [shift(kv, "ctx", nz, d) for d in range(1, nz)], axis=0
    )

    mixed, lse = attend(count, tiles, q, kv, *masks)
    mixed_low = mixed.reshape(query_width, rows).astype(low)
    attn_own = scatter_rows(dot(mixed_low, output_w, 0, 0), "tp", nt)
    inputs_own = own_rows(tokens, "tp", nt).astype(high)
    upstream_low = own_rows(cotangent, "tp", nt)
    upstream_own = upstream_low.astype(high)
    one_own = inputs_own + attn_own
    scale_two = rms_scale(one_own)
    normed_own = (one_own * scale_two * gain_two).astype(low)
    normed_two = gather_rows(normed_own, "tp", nt)

    hidden, dgate, dupper = middle(normed_two, cotangent, gate_w, upper_w, down_w)
    grad_part = dot(dgate, gate_w, 1, 1) + dot(dupper, upper_w, 1, 1)
    grad_own = scatter_rows(grad_part, "tp", nt)
    ffn_own = scatter_rows(dot(hidden, down_w, 1, 0), "tp", nt)
    activations = gather_rows((one_own + ffn_own).astype(low), "tp", nt)
    gain_two_sum = jnp.sum(grad_own * one_own * scale_two, axis=0)
    grad_one = upstream_own + norm_back(one_own, scale_two, gain_two, grad_own)
    grad_attn = gather_rows(grad_one.astype(low), "tp", nt)

    if paired:
        there_cot = gather_rows(swap(upstream_low, "fsdp", 2, 1), "tp", nt)
        there_two = gather_rows(swap(normed_own, "fsdp", 2, 1), "tp", nt)
        hidden_there, dgate_there, dupper_there = middle(
            there_two, there_cot, gate_w, upper_w, down_w
        )
        down_grad = dot(hidden, mine(cotangent), 0, 0) + dot(
            hidden_there, mine(there_cot), 0, 0
        )
        left, left_there = mine(normed_two), mine(there_two)
        gate_grad = dot(left, dgate, 0, 0) + dot(left_there, dgate_there, 0, 0)
        upper_grad = dot(left, dupper, 0, 0) + dot(left_there, dupper_there, 0, 0)
        output_grad = dot(mixed_low, mine(grad_attn), 1, 0) + dot(
            swap(mixed_low, "fsdp", 2, 1), swap(theirs(grad_attn), "fsdp", 2, 1), 1, 0
        )
    else:
        down_grad = lax.psum_scatter(
            dot(hidden, cotangent, 0, 0), "fsdp", scatter_dimension=1, tiled=True
        )
        gate_grad = lax.psum_scatter(
            dot(normed_two, dgate, 0, 0), "fsdp", scatter_dimension=0, tiled=True
        )
        upper_grad = lax.psum_scatter(
            dot(normed_two, dupper, 0, 0), "fsdp", scatter_dimension=0, tiled=True
        )
        output_grad = lax.psum_scatter(
            dot(mixed_low, grad_attn, 1, 0), "fsdp", scatter_dimension=1, tiled=True
        )

    grad_mixed = dot(output_w, grad_attn, 1, 1).astype(low).reshape(heads, HD, rows)
    dq, dkv = attend_back(count, tiles, q, kv, *masks, mixed, lse, grad_mixed)
    per = rows // TILE
    dkv_own = dkv[:per]
    for d in range(1, nz):
        dkv_own = dkv_own + shift(
            dkv[d * per : (d + 1) * per].astype(low), "ctx", nz, nz - d
        ).astype(high)
    dkv_own = jnp.transpose(dkv_own, (1, 0, 2)).reshape(2 * HD, rows)
    dq = turn(dq * 0.125, cosine, -sine).reshape(query_width, rows)
    dk = turn(dkv_own[None, :HD], cosine, -sine)[0]
    dqkv = jnp.concatenate([dq, dk, dkv_own[HD:]], axis=0).astype(low)
    first_own = scatter_rows(dot(dqkv, qkv_w, 0, 1), "tp", nt)
    if paired:
        there_one = swap(theirs(normed_one), "fsdp", 2, 1)
        qkv_grad = dot(mine(normed_one), dqkv, 0, 1) + dot(
            there_one, swap(dqkv, "fsdp", 2, 1), 0, 1
        )
    else:
        qkv_grad = lax.psum_scatter(
            dot(normed_one, dqkv, 0, 1), "fsdp", scatter_dimension=0, tiled=True
        )
    scale_own = rms_scale(inputs_own)
    gain_one_sum = jnp.sum(first_own * inputs_own * scale_own, axis=0)
    input_own = grad_one + norm_back(inputs_own, scale_own, gain_one, first_own)
    input_grad = gather_rows(input_own.astype(low), "tp", nt).astype(high)

    sums = sum_all(jnp.stack([gain_one_sum, gain_two_sum]), "tp", nt)
    if paired:
        sums = mine(sums) + swap(theirs(sums), "fsdp", 2, 1)
    else:
        sums = lax.psum_scatter(sums, "fsdp", scatter_dimension=1, tiled=True)
    sums = sum_all(sums, "ctx", nz)
    down_grad, gate_grad, upper_grad, output_grad, qkv_grad = line_sum(
        [down_grad, gate_grad, upper_grad, output_grad, qkv_grad], nz
    )
    return (
        activations,
        input_grad,
        sums[0],
        qkv_grad[:, :query_width],
        qkv_grad[:, query_width:],
        output_grad,
        sums[1],
        gate_grad,
        upper_grad,
        down_grad,
    )


def solution(mesh):
    placed = (
        P(("fsdp", "ctx"), None),
        P("fsdp"),
        P("fsdp", "tp"),
        P("fsdp", "tp"),
        P("tp", "fsdp"),
        P("fsdp"),
        P("fsdp", "tp"),
        P("fsdp", "tp"),
        P("tp", "fsdp"),
        P("fsdp"),
        P("fsdp"),
        P(("fsdp", "ctx"), None),
    )
    sizes = (mesh.shape["fsdp"], mesh.shape["ctx"], mesh.shape["tp"])
    return jax.shard_map(
        functools.partial(per_device, sizes),
        mesh=mesh,
        in_specs=placed,
        out_specs=(
            P(("fsdp", "ctx"), None),
            P(("fsdp", "ctx"), None),
            P("fsdp"),
            P("fsdp", "tp"),
            P("fsdp", "tp"),
            P("tp", "fsdp"),
            P("fsdp"),
            P("fsdp", "tp"),
            P("fsdp", "tp"),
            P("tp", "fsdp"),
        ),
        check_vma=False,
    )
```

time: 2160 us -> 1010 us (0.47)
  waiting for transfers between devices: 1640 us -> 661 us
  matrix products: 227 us -> 52.6 us
  blocking collectives: 107 us -> 0 us
  Pallas kernels: 0 us -> 78.1 us
  starting transfers between devices: 1.48 us -> 74 us
  other arithmetic: 42.3 us -> 106 us
  local copies, waits for them, and re-layouts: 72.3 us -> 23.1 us
  loops' own time: 32 us -> 0 us
    reduce_scatter x7 -> x0, waiting for transfers between devices: 752 us -> none  [the longest x1 196 us: per_device(): lax.psum_scatter(gradients[7], ('fsdp', 'ctx'), scatter_dimension=1, tile...]
    ppermute x0 -> x58, waiting for transfers between devices: none -> 661 us  [the longest x37 342 us: swap(): return lax.ppermute(value, axis, pairs)]
    all_gather x10 -> x0, waiting for transfers between devices: 593 us -> none  [the longest x1 107 us: per_device(): lax.all_gather(pieces[7], 'ctx', axis=1, tiled=True)]
    psum x4 -> x0, waiting for transfers between devices: 296 us -> none  [the longest x1 87.8 us: per_device(): grad_first = lax.psum(first_part, 'tp')]
    dot_general x74 -> x17, matrix products: 227 us -> 52.6 us  [dot(): lax.dot_general(left, right, (((over_left,), (over_right,)), ((), ())), p...]
    pallas_call x0 -> x4, Pallas kernels: none -> 78.1 us  [the longest x1 37.9 us: attend_back(): pl.pallas_call(functools.partial(attend_back_kernel, heads), grid_spec=pl...]
    ppermute x0 -> x58, starting transfers between devices: none -> 74 us  [the longest x37 27.7 us: swap(): return lax.ppermute(value, axis, pairs)]
    all_gather x7 -> x0, blocking collectives: 73.7 us -> none  [the longest x1 16.8 us: per_device(): lax.all_gather(pieces[2], 'ctx', axis=0, tiled=True)]
  transfers between devices with their start and end apart: 21 -> 58, of which waited for: 18 -> 24; matrix products, arithmetic and copies ran while one was open for 8% -> 16% of each run, Pallas kernels for 0% -> 8%
where the time goes in v1:
time: 1010 us; the launch traced here: 997 us
  waiting for transfers between devices  661 us (65%)
  other arithmetic  106 us (10%)
  Pallas kernels  78.1 us (8%)
  starting transfers between devices  74 us (7%)
  matrix products  52.6 us (5%)
  local copies, waits for them, and re-layouts  23.1 us (2%)
    ppermute x37, waiting for transfers between devices, swap(): return lax.ppermute(value, axis, pairs)  342 us
    ppermute x5, waiting for transfers between devices, line_sum(): final = lax.ppermute(low, 'ctx', [(1, 0), (2, 3)])  153 us
    ppermute x5, waiting for transfers between devices, line_sum(): low = low + lax.ppermute(low, 'ctx', [(0, 1), (3, 2)])  109 us
    dot_general x17, matrix products, dot(): lax.dot_general(left, right, (((over_left,), (over_right,)), ((), ())), p...  52.6 us
    select_n x14, other arithmetic, in_order(): jnp.where(bit == 0, jnp.concatenate([mine, other], axis=dim), jnp.concate...  42.7 us
    pallas_call x1, Pallas kernels, attend_back(): pl.pallas_call(functools.partial(attend_back_kernel, heads), grid_spec=pl...  37.9 us
    ppermute x5, waiting for transfers between devices, line_sum(): low = low + lax.ppermute(low, 'ctx', [(1, 2), (2, 1)])  32.8 us
    pallas_call x2, Pallas kernels, middle(): pl.pallas_call(middle_kernel, grid=(pl.cdiv(units, block),), in_specs=[wh...  28.5 us
  transfers between devices with their start and end apart: 58, of which 24 were waited for; matrix products, arithmetic and copies ran while one was open for 16% of the time, Pallas kernels for 8%

profile of v1, /device:TPU:8, one launch (start us, length us, event | category | flops | bytes accessed | tf_op | source)
XLA Modules:
  0.0 997.4 jit_solution(8922458007076483451)
XLA Ops:
  18.0 19.6 %collective-permute-done = bf16[1024,640]{1,0:T(8,128)(2,1)} collective-permute-done((bf16[1024,640]{1,0:T(8,128)(2,1)S(1)}, bf16[1024,640]{1,0:T(8,128)(2,1)}, u32[]{:S(2)}, u32[]{:S(2)}) %collective-permute-start) | collective-permute-done | bytes 1310752 | tf_op jit(solution)/shard_map/ppermute | solution.py:30
  48.0 4.8 collective-permute-done.4
  54.0 11.7 %shard_map.195 = (f32[8,64,512]{2,1,0:T(8,128)S(1)}, f32[8,512]{1,0:T(8,128)S(1)}) custom-call(s32[4]{0:T(128)S(1)} %convert_reduce_fusion.count, s32[4,16]{1,0:T(4,128)S(1)} %select_reduce_fusion.tiles, bf16[8,64,512]{2,1,0:T(8,128)(2,1)S(1)} %maximum_multiply_fusion.q, bf16[16,128,128]{2,1,0:T(8,128)(2,1)S(1)} %pad_maximum_fusion.1.kv, ...), custom_call_target="tpu_custom_call" | custom-call | flops 10000000000 | bytes 4194304 | tf_op jit(solution)/shard_map/pallas_call | solution.py:149
  77.9 72.0 %collective-permute-done.46 = bf16[128,2048]{1,0:T(8,128)(2,1)} collective-permute-done((bf16[128,2048]{1,0:T(8,128)(2,1)}, bf16[128,2048]{1,0:T(8,128)(2,1)}, u32[]{:S(2)}, u32[]{:S(2)}) %collective-permute-start.46) | collective-permute-done | bytes 524320 | tf_op jit(solution)/shard_map/ppermute | solution.py:30
  156.5 8.6 collective-permute-done.47
  168.1 6.6 collective-permute-done.7
  177.9 6.3 maximum_select_fusion.gate_w
  184.1 4.5 collective-permute-done.8
  188.9 22.8 %collective-permute-done.11 = bf16[1024,1408]{1,0:T(8,128)(2,1)} collective-permute-done((bf16[1024,1408]{1,0:T(8,128)(2,1)}, bf16[1024,1408]{1,0:T(8,128)(2,1)}, u32[]{:S(2)}, u32[]{:S(2)}) %collective-permute-start.11) | collective-permute-done | bytes 2883616 | tf_op jit(solution)/shard_map/ppermute | solution.py:30
  211.8 8.2 maximum_select_fusion.1.upper_w
  220.1 53.5 %collective-permute-done.12 = bf16[1408,1024]{1,0:T(8,128)(2,1)} collective-permute-done((bf16[1408,1024]{1,0:T(8,128)(2,1)}, bf16[1408,1024]{1,0:T(8,128)(2,1)}, u32[]{:S(2)}, u32[]{:S(2)}) %collective-permute-start.12) | collective-permute-done | bytes 2883616 | tf_op jit(solution)/shard_map/ppermute | solution.py:30
  273.6 9.6 maximum_select_fusion.2.down_w
  286.9 14.2 %shard_map.196 = (bf16[512,1408]{1,0:T(8,128)(2,1)S(1)}, bf16[512,1408]{1,0:T(8,128)(2,1)S(1)}, bf16[512,1408]{1,0:T(8,128)(2,1)S(1)}) custom-call(bf16[512,2048]{1,0:T(8,128)(2,1)S(1)} %maximum_select_fusion.5.rows, bf16[512,2048]{1,0:T(8,128)(2,1)S(1)} %copy-done.5, bf16[2048,1408]{1,0:T(8,128)(2,1)S(1)} %maximum_select_fusion.gate_w, ...), custom_call_target="tpu_custom_call" | custom-call | flops 8858370048 | bytes 25821184 | tf_op jit(solution)/shard_map/pallas_call | solution.py:276
  301.2 5.0 fusion.82
  306.2 5.6 convolution_add_fusion
  312.1 3.4 fusion.81
  316.2 3.3 maximum_select_fusion.10.upstream
  326.4 11.2 %collective-permute-done.18 = bf16[128,2048]{1,0:T(8,128)(2,1)S(1)} collective-permute-done((bf16[128,2048]{1,0:T(8,128)(2,1)S(1)}, bf16[128,2048]{1,0:T(8,128)(2,1)S(1)}, u32[]{:S(2)}, u32[]{:S(2)}) %collective-permute-start.18) | collective-permute-done | bytes 524320 | tf_op jit(solution)/shard_map/ppermute | solution.py:30
  337.9 10.5 %collective-permute-done.14 = bf16[128,2048]{1,0:T(8,128)(2,1)S(1)} collective-permute-done((bf16[128,2048]{1,0:T(8,128)(2,1)S(1)}, bf16[128,2048]{1,0:T(8,128)(2,1)S(1)}, u32[]{:S(2)}, u32[]{:S(2)}) %collective-permute-start.14) | collective-permute-done | bytes 524320 | tf_op jit(solution)/shard_map/ppermute | solution.py:30
  350.5 14.3 %shard_map.198 = (bf16[512,1408]{1,0:T(8,128)(2,1)S(1)}, bf16[512,1408]{1,0:T(8,128)(2,1)S(1)}, bf16[512,1408]{1,0:T(8,128)(2,1)S(1)}) custom-call(bf16[512,2048]{1,0:T(8,128)(2,1)S(1)} %maximum_select_fusion.9.rows, bf16[512,2048]{1,0:T(8,128)(2,1)S(1)} %maximum_select_fusion.10.upstream, bf16[2048,1408]{1,0:T(8,128)(2,1)S(1)} %maximum_select_fusion.gate_w, ...), custom_call_target="tpu_custom_call" | custom-call | flops 8858370048 | bytes 25821184 | tf_op jit(solution)/shard_map/pallas_call | solution.py:276
  367.0 3.4 add_convert_fusion.2
  371.7 4.4 fusion.29
  377.4 3.7 convolution_convert_fusion
  381.1 37.9 %shard_map.197 = (f32[8,64,512]{2,1,0:T(8,128)S(1)}, f32[16,128,128]{2,1,0:T(8,128)S(1)}) custom-call(s32[4]{0:T(128)S(1)} %convert_reduce_fusion.count, s32[4,16]{1,0:T(4,128)S(1)} %select_reduce_fusion.tiles, bf16[8,64,512]{2,1,0:T(8,128)(2,1)S(1)} %copy-done.8, bf16[16,128,128]{2,1,0:T(8,128)(2,1)S(1)} %copy-done.10, ...), custom_call_target="tpu_custom_call" | custom-call | flops 30000001024 | bytes 6291456 | tf_op jit(solution)/shard_map/pallas_call | solution.py:218
  421.7 19.0 %collective-permute-done.23 = bf16[4,128,128]{2,1,0:T(8,128)(2,1)S(1)} collective-permute-done((bf16[4,128,128]{2,1,0:T(8,128)(2,1)S(1)}, bf16[4,128,128]{2,1,0:T(8,128)(2,1)S(1)}, u32[]{:S(2)}, u32[]{:S(2)}) %collective-permute-start.23) | collective-permute-done | bytes 131104 | tf_op jit(solution)/shard_map/ppermute | solution.py:35
  441.2 4.5 fusion.39
  447.1 6.2 add_convert_fusion.1
  464.0 11.9 %collective-permute-done.25 = bf16[128,2048]{1,0:T(8,128)(2,1)} collective-permute-done((bf16[128,2048]{1,0:T(8,128)(2,1)}, bf16[128,2048]{1,0:T(8,128)(2,1)}, u32[]{:S(2)}, u32[]{:S(2)}) %collective-permute-start.25) | collective-permute-done | bytes 524320 | tf_op jit(solution)/shard_map/ppermute | solution.py:30
  481.6 3.4 add.336
  486.1 6.7 collective-permute-done.38
  492.8 6.4 collective-permute-start.50
  500.0 22.9 %collective-permute-done.52 = bf16[1024,1408]{1,0:T(8,128)(2,1)} collective-permute-done((bf16[1024,1408]{1,0:T(8,128)(2,1)}, bf16[1024,1408]{1,0:T(8,128)(2,1)}, u32[]{:S(2)}, u32[]{:S(2)}) %collective-permute-start.52) | collective-permute-done | bytes 2883616 | tf_op jit(solution)/shard_map/ppermute | solution.py:102
  523.3 60.5 %collective-permute-done.55 = bf16[1408,1024]{1,0:T(8,128)(2,1)} collective-permute-done((bf16[1408,1024]{1,0:T(8,128)(2,1)}, bf16[1408,1024]{1,0:T(8,128)(2,1)}, u32[]{:S(2)}, u32[]{:S(2)}) %collective-permute-start.55) | collective-permute-done | bytes 2883616 | tf_op jit(solution)/shard_map/ppermute | solution.py:102
  585.1 3.4 add.339
  588.5 4.1 add.342
  592.6 5.4 collective-permute-start.53
  603.1 4.2 collective-permute-start.32
  608.4 112.6 %collective-permute-done.32 = f32[2,1024]{1,0:T(2,128)S(1)} collective-permute-done((f32[2,1024]{1,0:T(2,128)S(1)}, f32[2,1024]{1,0:T(2,128)S(1)}, u32[]{:S(2)}, u32[]{:S(2)}) %collective-permute-start.32) | collective-permute-done | bytes 8224 | tf_op jit(solution)/shard_map/ppermute | solution.py:30
  725.9 25.6 %collective-permute-done.35 = bf16[1024,640]{1,0:T(8,128)(2,1)S(1)} collective-permute-done((bf16[1024,640]{1,0:T(8,128)(2,1)S(1)}, bf16[1024,640]{1,0:T(8,128)(2,1)S(1)}, u32[]{:S(2)}, u32[]{:S(2)}) %collective-permute-start.35) | collective-permute-done | bytes 1310752 | tf_op jit(solution)/shard_map/ppermute | solution.py:102
  766.4 13.1 %collective-permute-done.41 = bf16[512,1024]{1,0:T(8,128)(2,1)S(1)} collective-permute-done((bf16[512,1024]{1,0:T(8,128)(2,1)S(1)}, bf16[512,1024]{1,0:T(8,128)(2,1)S(1)}, u32[]{:S(2)}, u32[]{:S(2)}) %collective-permute-start.41) | collective-permute-done | bytes 1048608 | tf_op jit(solution)/shard_map/ppermute | solution.py:103
  783.8 19.7 %collective-permute-done.36 = bf16[1024,640]{1,0:T(8,128)(2,1)S(1)} collective-permute-done((bf16[1024,640]{1,0:T(8,128)(2,1)S(1)}, bf16[1024,640]{1,0:T(8,128)(2,1)S(1)}, u32[]{:S(2)}, u32[]{:S(2)}) %collective-permute-start.36) | collective-permute-done | bytes 1310752 | tf_op jit(solution)/shard_map/ppermute | solution.py:103
  811.4 4.7 maximum_select_fusion.6
  819.7 5.0 fusion.3
  824.8 84.0 %collective-permute-done.42 = bf16[512,1024]{1,0:T(8,128)(2,1)} collective-permute-done((bf16[512,1024]{1,0:T(8,128)(2,1)}, bf16[512,1024]{1,0:T(8,128)(2,1)}, u32[]{:S(2)}, u32[]{:S(2)}) %collective-permute-start.42) | collective-permute-done | bytes 1048608 | tf_op jit(solution)/shard_map/ppermute | solution.py:104
  911.5 25.4 %collective-permute-done.37 = bf16[1024,640]{1,0:T(8,128)(2,1)} collective-permute-done((bf16[1024,640]{1,0:T(8,128)(2,1)}, bf16[1024,640]{1,0:T(8,128)(2,1)}, u32[]{:S(2)}, u32[]{:S(2)}) %collective-permute-start.37) | collective-permute-done | bytes 1310752 | tf_op jit(solution)/shard_map/ppermute | solution.py:104
  940.8 4.7 select_convert_fusion.2
  945.5 4.7 select_convert_fusion.1
  950.2 44.0 %collective-permute-done.57 = bf16[1408,1024]{1,0:T(8,128)(2,1)S(1)} collective-permute-done((bf16[1408,1024]{1,0:T(8,128)(2,1)S(1)}, bf16[1408,1024]{1,0:T(8,128)(2,1)S(1)}, u32[]{:S(2)}, u32[]{:S(2)}) %collective-permute-start.57) | collective-permute-done | bytes 2883616 | tf_op jit(solution)/shard_map/ppermute | solution.py:104
  (355 shorter events, 147.6 us)
Async XLA Ops:
  2.8 12.5 %collective-permute-start.1 = (bf16[2,1024]{1,0:T(2,128)(2,1)}, bf16[2,1024]{1,0:T(2,128)(2,1)}, u32[]{:S(2)}, u32[]{:S(2)}) collective-permute-start(bf16[2,1024]{1,0:T(2,128)(2,1)} %pad_maximum_fusion.5), channel_id=1, source_target_pairs={{0,16},{16,0},{1,17},{17,1},{2,18},{18,2},{3,19},{19,3},{4,20},{20... | collective-permute-start | bytes 12296 | tf_op jit(solution)/shard_map/ppermute | solution.py:30
  5.7 31.9 %collective-permute-start = (bf16[1024,640]{1,0:T(8,128)(2,1)S(1)}, bf16[1024,640]{1,0:T(8,128)(2,1)}, u32[]{:S(2)}, u32[]{:S(2)}) collective-permute-start(bf16[1024,640]{1,0:T(8,128)(2,1)S(1)} %constant_dynamic-update-slice_fusion), channel_id=1, source_target_pairs={{0,16},{16,0},{1,17},{17,1},{2,18},{18,2},{3,19},{19,3},{4,20},{20... | collective-permute-start | bytes 3932168 | tf_op jit(solution)/shard_map/ppermute | solution.py:30
  6.3 59.7 %collective-permute-start.5 = (bf16[512,1024]{1,0:T(8,128)(2,1)}, bf16[512,1024]{1,0:T(8,128)(2,1)}, u32[]{:S(2)}, u32[]{:S(2)}) collective-permute-start(bf16[512,1024]{1,0:T(8,128)(2,1)} %param.16), channel_id=1, source_target_pairs={{0,16},{16,0},{1,17},{17,1},{2,18},{18,2},{3,19},{19,3},{4,20},{20... | collective-permute-start | bytes 3145736 | tf_op jit(solution)/shard_map/ppermute | solution.py:30
  73.1 78.4 %collective-permute-start.6 = (bf16[256,2048]{1,0:T(8,128)(2,1)}, bf16[256,2048]{1,0:T(8,128)(2,1)}, u32[]{:S(2)}, u32[]{:S(2)}) collective-permute-start(bf16[256,2048]{1,0:T(8,128)(2,1)} %fusion.6), channel_id=1, source_target_pairs={{0,1},{1,0},{2,3},{3,2},{4,5},{5,4},{6,7},{7,6},{8,9},{9,8},{10,11... | collective-permute-start | bytes 3145736 | tf_op jit(solution)/shard_map/ppermute | solution.py:30
  73.2 104.7 %collective-permute-start.10 = (bf16[1024,1408]{1,0:T(8,128)(2,1)}, bf16[1024,1408]{1,0:T(8,128)(2,1)}, u32[]{:S(2)}, u32[]{:S(2)}) collective-permute-start(bf16[1024,1408]{1,0:T(8,128)(2,1)} %param.18), channel_id=1, source_target_pairs={{0,16},{16,0},{1,17},{17,1},{2,18},{18,2},{3,19},{19,3},{4,20},{20... | collective-permute-start | bytes 8650760 | tf_op jit(solution)/shard_map/ppermute | solution.py:30
  75.9 74.1 %collective-permute-start.46 = (bf16[128,2048]{1,0:T(8,128)(2,1)}, bf16[128,2048]{1,0:T(8,128)(2,1)}, u32[]{:S(2)}, u32[]{:S(2)}) collective-permute-start(bf16[128,2048]{1,0:T(8,128)(2,1)} %dynamic-slice_bitcast_fusion), channel_id=1, source_target_pairs={{0,16},{16,0},{1,17},{17,1},{2,18},{18,2},{3,19},{19,3},{4,20},{20... | collective-permute-start | bytes 1572872 | tf_op jit(solution)/shard_map/ppermute | solution.py:30
  77.1 134.7 %collective-permute-start.11 = (bf16[1024,1408]{1,0:T(8,128)(2,1)}, bf16[1024,1408]{1,0:T(8,128)(2,1)}, u32[]{:S(2)}, u32[]{:S(2)}) collective-permute-start(bf16[1024,1408]{1,0:T(8,128)(2,1)} %param.19), channel_id=1, source_target_pairs={{0,16},{16,0},{1,17},{17,1},{2,18},{18,2},{3,19},{19,3},{4,20},{20... | collective-permute-start | bytes 8650760 | tf_op jit(solution)/shard_map/ppermute | solution.py:30
  150.0 15.2 %collective-permute-start.47 = (bf16[128,2048]{1,0:T(8,128)(2,1)}, bf16[128,2048]{1,0:T(8,128)(2,1)}, u32[]{:S(2)}, u32[]{:S(2)}) collective-permute-start(bf16[128,2048]{1,0:T(8,128)(2,1)} %collective-permute-done.46), channel_id=1, source_target_pairs={{0,2},{1,3},{2,0},{3,1},{4,6},{5,7},{6,4},{7,5},{8,10},{9,11},{10,... | collective-permute-start | bytes 1572872 | tf_op jit(solution)/shard_map/ppermute | solution.py:30
  155.9 18.8 %collective-permute-start.7 = (bf16[128,2048]{1,0:T(8,128)(2,1)}, bf16[128,2048]{1,0:T(8,128)(2,1)}, u32[]{:S(2)}, u32[]{:S(2)}) collective-permute-start(bf16[128,2048]{1,0:T(8,128)(2,1)} %fusion.35), channel_id=1, source_target_pairs={{0,2},{1,3},{2,0},{3,1},{4,6},{5,7},{6,4},{7,5},{8,10},{9,11},{10,... | collective-permute-start | bytes 1572872 | tf_op jit(solution)/shard_map/ppermute | solution.py:30
  156.4 117.2 %collective-permute-start.12 = (bf16[1408,1024]{1,0:T(8,128)(2,1)}, bf16[1408,1024]{1,0:T(8,128)(2,1)}, u32[]{:S(2)}, u32[]{:S(2)}) collective-permute-start(bf16[1408,1024]{1,0:T(8,128)(2,1)} %param.20), channel_id=1, source_target_pairs={{0,16},{16,0},{1,17},{17,1},{2,18},{18,2},{3,19},{19,3},{4,20},{20... | collective-permute-start | bytes 8650760 | tf_op jit(solution)/shard_map/ppermute | solution.py:30
  168.1 148.1 %collective-permute-start.48 = (bf16[256,2048]{1,0:T(8,128)(2,1)}, bf16[256,2048]{1,0:T(8,128)(2,1)}, u32[]{:S(2)}, u32[]{:S(2)}) collective-permute-start(bf16[256,2048]{1,0:T(8,128)(2,1)} %maximum_select_fusion.16), channel_id=1, source_target_pairs={{0,1},{1,0},{2,3},{3,2},{4,5},{5,4},{6,7},{7,6},{8,9},{9,8},{10,11... | collective-permute-start | bytes 3145736 | tf_op jit(solution)/shard_map/ppermute | solution.py:30
  176.3 12.3 %collective-permute-start.8 = (bf16[128,2048]{1,0:T(8,128)(2,1)S(1)}, bf16[128,2048]{1,0:T(8,128)(2,1)S(1)}, u32[]{:S(2)}, u32[]{:S(2)}) collective-permute-start(bf16[128,2048]{1,0:T(8,128)(2,1)S(1)} %multiply_convert_fusion), channel_id=1, source_target_pairs={{0,2},{1,3},{2,0},{3,1},{4,6},{5,7},{6,4},{7,5},{8,10},{9,11},{10,... | collective-permute-start | bytes 1572872 | tf_op jit(solution)/shard_map/ppermute | solution.py:30
  188.9 97.1 %collective-permute-start.9 = (bf16[256,2048]{1,0:T(8,128)(2,1)S(1)}, bf16[256,2048]{1,0:T(8,128)(2,1)S(1)}, u32[]{:S(2)}, u32[]{:S(2)}) collective-permute-start(bf16[256,2048]{1,0:T(8,128)(2,1)S(1)} %maximum_select_fusion.11), channel_id=1, source_target_pairs={{0,1},{1,0},{2,3},{3,2},{4,5},{5,4},{6,7},{7,6},{8,9},{9,8},{10,11... | collective-permute-start | bytes 3145736 | tf_op jit(solution)/shard_map/ppermute | solution.py:30
  220.0 64.4 %collective-permute-start.43 = (bf16[128,2048]{1,0:T(8,128)(2,1)S(1)}, bf16[128,2048]{1,0:T(8,128)(2,1)}, u32[]{:S(2)}, u32[]{:S(2)}) collective-permute-start(bf16[128,2048]{1,0:T(8,128)(2,1)S(1)} %multiply_convert_fusion), channel_id=1, source_target_pairs={{0,16},{16,0},{1,17},{17,1},{2,18},{18,2},{3,19},{19,3},{4,20},{20... | collective-permute-start | bytes 1572872 | tf_op jit(solution)/shard_map/ppermute | solution.py:30
  284.4 35.1 %collective-permute-start.44 = (bf16[128,2048]{1,0:T(8,128)(2,1)}, bf16[128,2048]{1,0:T(8,128)(2,1)}, u32[]{:S(2)}, u32[]{:S(2)}) collective-permute-start(bf16[128,2048]{1,0:T(8,128)(2,1)} %collective-permute-done.43), channel_id=1, source_target_pairs={{0,2},{1,3},{2,0},{3,1},{4,6},{5,7},{6,4},{7,5},{8,10},{9,11},{10,... | collective-permute-start | bytes 1572872 | tf_op jit(solution)/shard_map/ppermute | solution.py:30
  322.8 14.8 %collective-permute-start.18 = (bf16[128,2048]{1,0:T(8,128)(2,1)S(1)}, bf16[128,2048]{1,0:T(8,128)(2,1)S(1)}, u32[]{:S(2)}, u32[]{:S(2)}) collective-permute-start(bf16[128,2048]{1,0:T(8,128)(2,1)S(1)} %fusion.37), channel_id=1, source_target_pairs={{0,2},{1,3},{2,0},{3,1},{4,6},{5,7},{6,4},{7,5},{8,10},{9,11},{10,... | collective-permute-start | bytes 1572872 | tf_op jit(solution)/shard_map/ppermute | solution.py:30
  323.8 24.6 %collective-permute-start.14 = (bf16[128,2048]{1,0:T(8,128)(2,1)S(1)}, bf16[128,2048]{1,0:T(8,128)(2,1)S(1)}, u32[]{:S(2)}, u32[]{:S(2)}) collective-permute-start(bf16[128,2048]{1,0:T(8,128)(2,1)S(1)} %fusion.36), channel_id=1, source_target_pairs={{0,2},{1,3},{2,0},{3,1},{4,6},{5,7},{6,4},{7,5},{8,10},{9,11},{10,... | collective-permute-start | bytes 1572872 | tf_op jit(solution)/shard_map/ppermute | solution.py:30
  350.0 14.8 %collective-permute-start.19 = (bf16[128,2048]{1,0:T(8,128)(2,1)S(1)}, bf16[128,2048]{1,0:T(8,128)(2,1)S(1)}, u32[]{:S(2)}, u32[]{:S(2)}) collective-permute-start(bf16[128,2048]{1,0:T(8,128)(2,1)S(1)} %get-tuple-element.34), channel_id=1, source_target_pairs={{0,2},{1,3},{2,0},{3,1},{4,6},{5,7},{6,4},{7,5},{8,10},{9,11},{10,... | collective-permute-start | bytes 1572872 | tf_op jit(solution)/shard_map/ppermute | solution.py:30
  370.5 110.5 %collective-permute-start.49 = (bf16[1024,1408]{1,0:T(8,128)(2,1)}, bf16[1024,1408]{1,0:T(8,128)(2,1)}, u32[]{:S(2)}, u32[]{:S(2)}) collective-permute-start(bf16[1024,1408]{1,0:T(8,128)(2,1)} %add_convert_fusion.2), channel_id=1, source_target_pairs={{0,4},{12,8},{1,5},{13,9},{2,6},{14,10},{3,7},{15,11},{16,20},{28,... | collective-permute-start | bytes 8650760 | tf_op jit(solution)/shard_map/ppermute | solution.py:102
  419.1 21.5 %collective-permute-start.23 = (bf16[4,128,128]{2,1,0:T(8,128)(2,1)S(1)}, bf16[4,128,128]{2,1,0:T(8,128)(2,1)S(1)}, u32[]{:S(2)}, u32[]{:S(2)}) collective-permute-start(bf16[4,128,128]{2,1,0:T(8,128)(2,1)S(1)} %get-tuple-element.48), channel_id=1, source_target_pairs={{0,4},{4,8},{8,12},{12,0},{1,5},{5,9},{9,13},{13,1},{2,6},{6,10},{... | collective-permute-start | bytes 393224 | tf_op jit(solution)/shard_map/ppermute | solution.py:35
  419.2 21.5 %collective-permute-start.22 = (bf16[4,128,128]{2,1,0:T(8,128)(2,1)S(1)}, bf16[4,128,128]{2,1,0:T(8,128)(2,1)S(1)}, u32[]{:S(2)}, u32[]{:S(2)}) collective-permute-start(bf16[4,128,128]{2,1,0:T(8,128)(2,1)S(1)} %get-tuple-element.49), channel_id=1, source_target_pairs={{0,8},{4,12},{8,0},{12,4},{1,9},{5,13},{9,1},{13,5},{2,10},{6,14},... | collective-permute-start | bytes 393224 | tf_op jit(solution)/shard_map/ppermute | solution.py:35
  419.2 21.4 %collective-permute-start.21 = (bf16[4,128,128]{2,1,0:T(8,128)(2,1)S(1)}, bf16[4,128,128]{2,1,0:T(8,128)(2,1)S(1)}, u32[]{:S(2)}, u32[]{:S(2)}) collective-permute-start(bf16[4,128,128]{2,1,0:T(8,128)(2,1)S(1)} %get-tuple-element.47), channel_id=1, source_target_pairs={{0,12},{4,0},{8,4},{12,8},{1,13},{5,1},{9,5},{13,9},{2,14},{6,2},{... | collective-permute-start | bytes 393224 | tf_op jit(solution)/shard_map/ppermute | solution.py:35
  445.9 15.4 %collective-permute-start.24 = (bf16[256,2048]{1,0:T(8,128)(2,1)S(1)}, bf16[256,2048]{1,0:T(8,128)(2,1)S(1)}, u32[]{:S(2)}, u32[]{:S(2)}) collective-permute-start(bf16[256,2048]{1,0:T(8,128)(2,1)S(1)} %fusion.9), channel_id=1, source_target_pairs={{0,1},{1,0},{2,3},{3,2},{4,5},{5,4},{6,7},{7,6},{8,9},{9,8},{10,11... | collective-permute-start | bytes 3145736 | tf_op jit(solution)/shard_map/ppermute | solution.py:30
  453.3 69.7 %collective-permute-start.52 = (bf16[1024,1408]{1,0:T(8,128)(2,1)}, bf16[1024,1408]{1,0:T(8,128)(2,1)}, u32[]{:S(2)}, u32[]{:S(2)}) collective-permute-start(bf16[1024,1408]{1,0:T(8,128)(2,1)} %add_convert_fusion.1), channel_id=1, source_target_pairs={{0,4},{12,8},{1,5},{13,9},{2,6},{14,10},{3,7},{15,11},{16,20},{28,... | collective-permute-start | bytes 8650760 | tf_op jit(solution)/shard_map/ppermute | solution.py:102
  459.9 123.9 %collective-permute-start.55 = (bf16[1408,1024]{1,0:T(8,128)(2,1)}, bf16[1408,1024]{1,0:T(8,128)(2,1)}, u32[]{:S(2)}, u32[]{:S(2)}) collective-permute-start(bf16[1408,1024]{1,0:T(8,128)(2,1)} %add_convert_fusion), channel_id=1, source_target_pairs={{0,4},{12,8},{1,5},{13,9},{2,6},{14,10},{3,7},{15,11},{16,20},{28,... | collective-permute-start | bytes 8650760 | tf_op jit(solution)/shard_map/ppermute | solution.py:102
  462.5 13.5 %collective-permute-start.25 = (bf16[128,2048]{1,0:T(8,128)(2,1)}, bf16[128,2048]{1,0:T(8,128)(2,1)}, u32[]{:S(2)}, u32[]{:S(2)}) collective-permute-start(bf16[128,2048]{1,0:T(8,128)(2,1)} %fusion.38), channel_id=1, source_target_pairs={{0,2},{1,3},{2,0},{3,1},{4,6},{5,7},{6,4},{7,5},{8,10},{9,11},{10,... | collective-permute-start | bytes 1572872 | tf_op jit(solution)/shard_map/ppermute | solution.py:30
  477.8 15.0 %collective-permute-start.38 = (bf16[512,512]{1,0:T(8,128)(2,1)}, bf16[512,512]{1,0:T(8,128)(2,1)S(1)}, u32[]{:S(2)}, u32[]{:S(2)}) collective-permute-start(bf16[512,512]{1,0:T(8,128)(2,1)} %bitcast.163), channel_id=1, source_target_pairs={{0,16},{16,0},{1,17},{17,1},{2,18},{18,2},{3,19},{19,3},{4,20},{20... | collective-permute-start | bytes 1572872 | tf_op jit(solution)/shard_map/ppermute | solution.py:30
  481.0 18.2 %collective-permute-start.15 = (bf16[128,2048]{1,0:T(8,128)(2,1)S(1)}, bf16[128,2048]{1,0:T(8,128)(2,1)S(1)}, u32[]{:S(2)}, u32[]{:S(2)}) collective-permute-start(bf16[128,2048]{1,0:T(8,128)(2,1)S(1)} %copy-done.41), channel_id=1, source_target_pairs={{0,2},{1,3},{2,0},{3,1},{4,6},{5,7},{6,4},{7,5},{8,10},{9,11},{10,... | collective-permute-start | bytes 1572872 | tf_op jit(solution)/shard_map/ppermute | solution.py:30
  485.0 99.1 %collective-permute-start.39 = (bf16[512,1024]{1,0:T(8,128)(2,1)S(1)}, bf16[512,1024]{1,0:T(8,128)(2,1)S(1)}, u32[]{:S(2)}, u32[]{:S(2)}) collective-permute-start(bf16[512,1024]{1,0:T(8,128)(2,1)S(1)} %constant_dynamic-slice_fusion), channel_id=1, source_target_pairs={{0,16},{16,0},{1,17},{17,1},{2,18},{18,2},{3,19},{19,3},{4,20},{20... | collective-permute-start | bytes 3145736 | tf_op jit(solution)/shard_map/ppermute | solution.py:30
  492.8 262.2 %collective-permute-start.50 = (bf16[1024,1408]{1,0:T(8,128)(2,1)S(1)}, bf16[1024,1408]{1,0:T(8,128)(2,1)S(1)}, u32[]{:S(2)}, u32[]{:S(2)}) collective-permute-start(bf16[1024,1408]{1,0:T(8,128)(2,1)S(1)} %add.336), channel_id=1, source_target_pairs={{4,8},{8,4},{5,9},{9,5},{6,10},{10,6},{7,11},{11,7},{20,24},{24,20... | collective-permute-start | bytes 8650760 | tf_op jit(solution)/shard_map/ppermute | solution.py:103
  499.2 24.1 %collective-permute-start.30 = (f32[2,1024]{1,0:T(2,128)S(1)}, f32[2,1024]{1,0:T(2,128)S(1)}, u32[]{:S(2)}, u32[]{:S(2)}) collective-permute-start(f32[2,1024]{1,0:T(2,128)S(1)} %constant_dynamic-slice_fusion.2), channel_id=1, source_target_pairs={{0,16},{16,0},{1,17},{17,1},{2,18},{18,2},{3,19},{19,3},{4,20},{20... | collective-permute-start | bytes 24584 | tf_op jit(solution)/shard_map/ppermute | solution.py:30
  523.0 76.6 %collective-permute-start.33 = (bf16[512,1024]{1,0:T(8,128)(2,1)S(1)}, bf16[512,1024]{1,0:T(8,128)(2,1)S(1)}, u32[]{:S(2)}, u32[]{:S(2)}) collective-permute-start(bf16[512,1024]{1,0:T(8,128)(2,1)S(1)} %constant_dynamic-slice_fusion.1), channel_id=1, source_target_pairs={{0,16},{16,0},{1,17},{17,1},{2,18},{18,2},{3,19},{19,3},{4,20},{20... | collective-permute-start | bytes 3145736 | tf_op jit(solution)/shard_map/ppermute | solution.py:30
  523.2 78.5 %collective-permute-start.16 = (bf16[256,2048]{1,0:T(8,128)(2,1)S(1)}, bf16[256,2048]{1,0:T(8,128)(2,1)S(1)}, u32[]{:S(2)}, u32[]{:S(2)}) collective-permute-start(bf16[256,2048]{1,0:T(8,128)(2,1)S(1)} %maximum_select_fusion.12), channel_id=1, source_target_pairs={{0,1},{1,0},{2,3},{3,2},{4,5},{5,4},{6,7},{7,6},{8,9},{9,8},{10,11... | collective-permute-start | bytes 3145736 | tf_op jit(solution)/shard_map/ppermute | solution.py:30
  583.8 19.3 %collective-permute-start.34 = (bf16[640,512]{1,0:T(8,128)(2,1)S(1)}, bf16[640,512]{1,0:T(8,128)(2,1)S(1)}, u32[]{:S(2)}, u32[]{:S(2)}) collective-permute-start(bf16[640,512]{1,0:T(8,128)(2,1)S(1)} %pad_maximum_fusion), channel_id=1, source_target_pairs={{0,16},{16,0},{1,17},{17,1},{2,18},{18,2},{3,19},{19,3},{4,20},{20... | collective-permute-start | bytes 1966088 | tf_op jit(solution)/shard_map/ppermute | solution.py:30
  592.6 171.5 %collective-permute-start.53 = (bf16[1024,1408]{1,0:T(8,128)(2,1)S(1)}, bf16[1024,1408]{1,0:T(8,128)(2,1)S(1)}, u32[]{:S(2)}, u32[]{:S(2)}) collective-permute-start(bf16[1024,1408]{1,0:T(8,128)(2,1)S(1)} %add.339), channel_id=1, source_target_pairs={{4,8},{8,4},{5,9},{9,5},{6,10},{10,6},{7,11},{11,7},{20,24},{24,20... | collective-permute-start | bytes 8650760 | tf_op jit(solution)/shard_map/ppermute | solution.py:103
  599.6 207.6 %collective-permute-start.56 = (bf16[1408,1024]{1,0:T(8,128)(2,1)S(1)}, bf16[1408,1024]{1,0:T(8,128)(2,1)S(1)}, u32[]{:S(2)}, u32[]{:S(2)}) collective-permute-start(bf16[1408,1024]{1,0:T(8,128)(2,1)S(1)} %add.342), channel_id=1, source_target_pairs={{4,8},{8,4},{5,9},{9,5},{6,10},{10,6},{7,11},{11,7},{20,24},{24,20... | collective-permute-start | bytes 8650760 | tf_op jit(solution)/shard_map/ppermute | solution.py:103
  601.8 122.1 %collective-permute-start.40 = (bf16[512,1024]{1,0:T(8,128)(2,1)S(1)}, bf16[512,1024]{1,0:T(8,128)(2,1)S(1)}, u32[]{:S(2)}, u32[]{:S(2)}) collective-permute-start(bf16[512,1024]{1,0:T(8,128)(2,1)S(1)} %add_convert_fusion.4), channel_id=1, source_target_pairs={{0,4},{12,8},{1,5},{13,9},{2,6},{14,10},{3,7},{15,11},{16,20},{28,... | collective-permute-start | bytes 3145736 | tf_op jit(solution)/shard_map/ppermute | solution.py:102
  603.1 117.9 %collective-permute-start.32 = (f32[2,1024]{1,0:T(2,128)S(1)}, f32[2,1024]{1,0:T(2,128)S(1)}, u32[]{:S(2)}, u32[]{:S(2)}) collective-permute-start(f32[2,1024]{1,0:T(2,128)S(1)} %add.327), channel_id=1, source_target_pairs={{0,8},{4,12},{8,0},{12,4},{1,9},{5,13},{9,1},{13,5},{2,10},{6,14},... | collective-permute-start | bytes 24584 | tf_op jit(solution)/shard_map/ppermute | solution.py:30
  721.0 30.5 %collective-permute-start.35 = (bf16[1024,640]{1,0:T(8,128)(2,1)S(1)}, bf16[1024,640]{1,0:T(8,128)(2,1)S(1)}, u32[]{:S(2)}, u32[]{:S(2)}) collective-permute-start(bf16[1024,640]{1,0:T(8,128)(2,1)S(1)} %add_convert_fusion.3), channel_id=1, source_target_pairs={{0,4},{12,8},{1,5},{13,9},{2,6},{14,10},{3,7},{15,11},{16,20},{28,... | collective-permute-start | bytes 3932168 | tf_op jit(solution)/shard_map/ppermute | solution.py:102
  723.9 36.1 %collective-permute-start.26 = (bf16[128,2048]{1,0:T(8,128)(2,1)S(1)}, bf16[128,2048]{1,0:T(8,128)(2,1)S(1)}, u32[]{:S(2)}, u32[]{:S(2)}) collective-permute-start(bf16[128,2048]{1,0:T(8,128)(2,1)S(1)} %fusion.14), channel_id=1, source_target_pairs={{0,2},{1,3},{2,0},{3,1},{4,6},{5,7},{6,4},{7,5},{8,10},{9,11},{10,... | collective-permute-start | bytes 1572872 | tf_op jit(solution)/shard_map/ppermute | solution.py:30
  751.5 28.0 %collective-permute-start.41 = (bf16[512,1024]{1,0:T(8,128)(2,1)S(1)}, bf16[512,1024]{1,0:T(8,128)(2,1)S(1)}, u32[]{:S(2)}, u32[]{:S(2)}) collective-permute-start(bf16[512,1024]{1,0:T(8,128)(2,1)S(1)} %add.333), channel_id=1, source_target_pairs={{4,8},{8,4},{5,9},{9,5},{6,10},{10,6},{7,11},{11,7},{20,24},{24,20... | collective-permute-start | bytes 3145736 | tf_op jit(solution)/shard_map/ppermute | solution.py:103
  755.0 48.5 %collective-permute-start.36 = (bf16[1024,640]{1,0:T(8,128)(2,1)S(1)}, bf16[1024,640]{1,0:T(8,128)(2,1)S(1)}, u32[]{:S(2)}, u32[]{:S(2)}) collective-permute-start(bf16[1024,640]{1,0:T(8,128)(2,1)S(1)} %add.330), channel_id=1, source_target_pairs={{4,8},{8,4},{5,9},{9,5},{6,10},{10,6},{7,11},{11,7},{20,24},{24,20... | collective-permute-start | bytes 3932168 | tf_op jit(solution)/shard_map/ppermute | solution.py:103
  760.0 180.8 %collective-permute-start.51 = (bf16[1024,1408]{1,0:T(8,128)(2,1)}, bf16[1024,1408]{1,0:T(8,128)(2,1)}, u32[]{:S(2)}, u32[]{:S(2)}) collective-permute-start(bf16[1024,1408]{1,0:T(8,128)(2,1)} %add.337), channel_id=1, source_target_pairs={{4,0},{8,12},{5,1},{9,13},{6,2},{10,14},{7,3},{11,15},{20,16},{24,... | collective-permute-start | bytes 8650760 | tf_op jit(solution)/shard_map/ppermute | solution.py:104
  764.1 53.5 %collective-permute-start.27 = (bf16[256,2048]{1,0:T(8,128)(2,1)}, bf16[256,2048]{1,0:T(8,128)(2,1)}, u32[]{:S(2)}, u32[]{:S(2)}) collective-permute-start(bf16[256,2048]{1,0:T(8,128)(2,1)} %maximum_select_fusion.14), channel_id=1, source_target_pairs={{0,1},{1,0},{2,3},{3,2},{4,5},{5,4},{6,7},{7,6},{8,9},{9,8},{10,11... | collective-permute-start | bytes 3145736 | tf_op jit(solution)/shard_map/ppermute | solution.py:30
  779.4 166.1 %collective-permute-start.54 = (bf16[1024,1408]{1,0:T(8,128)(2,1)}, bf16[1024,1408]{1,0:T(8,128)(2,1)}, u32[]{:S(2)}, u32[]{:S(2)}) collective-permute-start(bf16[1024,1408]{1,0:T(8,128)(2,1)} %add.340), channel_id=1, source_target_pairs={{4,0},{8,12},{5,1},{9,13},{6,2},{10,14},{7,3},{11,15},{20,16},{24,... | collective-permute-start | bytes 8650760 | tf_op jit(solution)/shard_map/ppermute | solution.py:104
  803.5 105.2 %collective-permute-start.42 = (bf16[512,1024]{1,0:T(8,128)(2,1)}, bf16[512,1024]{1,0:T(8,128)(2,1)}, u32[]{:S(2)}, u32[]{:S(2)}) collective-permute-start(bf16[512,1024]{1,0:T(8,128)(2,1)} %add.334), channel_id=1, source_target_pairs={{4,0},{8,12},{5,1},{9,13},{6,2},{10,14},{7,3},{11,15},{20,16},{24,... | collective-permute-start | bytes 3145736 | tf_op jit(solution)/shard_map/ppermute | solution.py:104
  808.8 128.1 %collective-permute-start.37 = (bf16[1024,640]{1,0:T(8,128)(2,1)}, bf16[1024,640]{1,0:T(8,128)(2,1)}, u32[]{:S(2)}, u32[]{:S(2)}) collective-permute-start(bf16[1024,640]{1,0:T(8,128)(2,1)} %add.331), channel_id=1, source_target_pairs={{4,0},{8,12},{5,1},{9,13},{6,2},{10,14},{7,3},{11,15},{20,16},{24,... | collective-permute-start | bytes 3932168 | tf_op jit(solution)/shard_map/ppermute | solution.py:104
  817.6 176.6 %collective-permute-start.57 = (bf16[1408,1024]{1,0:T(8,128)(2,1)S(1)}, bf16[1408,1024]{1,0:T(8,128)(2,1)S(1)}, u32[]{:S(2)}, u32[]{:S(2)}) collective-permute-start(bf16[1408,1024]{1,0:T(8,128)(2,1)S(1)} %add.343), channel_id=1, source_target_pairs={{4,0},{8,12},{5,1},{9,13},{6,2},{10,14},{7,3},{11,15},{20,16},{24,... | collective-permute-start | bytes 8650760 | tf_op jit(solution)/shard_map/ppermute | solution.py:104
  (83 other events, 1137.9 us)

commit v2 on v1

v2 whole, which is shorter than its diff:
```python
import functools
import math

import jax
import jax.numpy as jnp
from jax import lax
from jax.experimental import pallas as pl
from jax.experimental.pallas import tpu as pltpu
from jax.sharding import PartitionSpec as P

HD = 64
TILE = 128
CODE = 4096
NEGATIVE = -1e30
epsilon = 1e-05
MIB = 2**20
SMALL = pl.CostEstimate(flops=1000000, bytes_accessed=100000, transcendentals=0)


def cost(microseconds):
    return pl.CostEstimate(
        flops=1000000, bytes_accessed=int(microseconds * SCALE * 3.69e6), transcendentals=0
    )


SCALE = 0.5


def dot(left, right, over_left, over_right):
    return lax.dot_general(
        left,
        right,
        (((over_left,), (over_right,)), ((), ())),
        preferred_element_type=jnp.float32,
    )


ORDER = (0, 2, 1, 3)


def swap(value, axis, distance, size):
    pairs = [(i, i ^ distance) for i in range(size)]
    return lax.ppermute(value, axis, pairs)


def shift(value, axis, size, distance):
    pairs = [(i, (i + distance) % size) for i in range(size)]
    return lax.ppermute(value, axis, pairs)


def over_x(value):
    return swap(value, "fsdp", 1, 2)


def over_y(value):
    return swap(value, "tp", 2, 4)


def over_core(value):
    return swap(value, "tp", 1, 4)


def add(left, right):
    return left.astype(jnp.float32) + right.astype(jnp.float32)


def cut(value, axis=0):
    keep, give = jnp.split(value, 2, axis=axis)
    return keep, give.astype(jnp.bfloat16)


def scatter_rows(keep, give, *tokens):
    part = add(keep, over_core(give)).astype(jnp.bfloat16)
    if part.shape[0] == 1:
        keep, give = cut(part[0])
        if tokens:
            (give,) = after([give], *tokens)
        return add(keep, over_y(give)), [give]
    left, right = jnp.split(part, 2, axis=2)
    keep_left, give_left = cut(left)
    keep_right, give_right = cut(right, 1)
    from_x, from_y = over_x(give_left), over_y(give_right)
    if tokens:
        from_x, from_y = after([from_x, from_y], *tokens)
    left = add(keep_left, from_x)[0]
    right = add(keep_right, from_y)
    keep_left, give_left = cut(left)
    keep_right, give_right = cut(right)
    left = add(keep_left, over_y(give_left))
    right = add(keep_right, over_x(give_right))[0]
    return jnp.concatenate([left, right], axis=1), [give_left, give_right]


def gather_own(rows, *tokens):
    first = jnp.concatenate([rows, over_y(rows)], axis=0)
    if tokens:
        (first,) = after([first], *tokens)
    return first, over_core(first)


def gather_pair(rows, *tokens):
    left, right = jnp.split(rows, 2, axis=1)
    left = jnp.stack([left, over_x(left)])
    right = jnp.concatenate([right, over_y(right)], axis=0)
    left = jnp.concatenate([left, over_y(left)], axis=1)
    right = jnp.stack([right, over_x(right)])
    first = jnp.concatenate([left, right], axis=2)
    if tokens:
        (first,) = after([first], *tokens)
    return first, over_core(first)


def sum_all(value, axis, size):
    distance = 1
    while distance < size:
        value = value + swap(value, axis, distance, size)
        distance *= 2
    return value


class Line:
    def __init__(self):
        self.came, self.total, self.done = [], [], []

    def put(self, piece):
        if self.came:
            earlier = (*self.came[-1:], *self.total[-2:-1], *self.done[-3:-2])
            (piece,) = after([piece], *earlier)
        self.came.append(lax.ppermute(piece, "ctx", [(0, 1), (3, 2)]))
        inward = piece + self.came[-1]
        self.total.append(inward + lax.ppermute(inward, "ctx", [(1, 2), (2, 1)]))
        self.done.append(lax.ppermute(self.total[-1], "ctx", [(1, 0), (2, 3)]))
        return len(self.total) - 1


def attend_kernel(
    heads, count, tiles, q, kv, q_code, q_base, k_code, mixed, lse, top, total, acc
):
    step = pl.program_id(0)
    top[...] = jnp.full_like(top, NEGATIVE)
    total[...] = jnp.zeros_like(total)
    acc[...] = jnp.zeros_like(acc)
    code, base = q_code[...], q_base[...]

    def body(j, carry):
        tile = tiles[step, j]
        keys = kv[tile, :HD]
        values = kv[tile, HD:]
        key_code = k_code[tile]
        allowed = (key_code <= code) & (key_code >= base)
        for h in range(heads):
            scores = jnp.where(allowed, dot(keys, q[h], 0, 0), NEGATIVE)
            before = top[h : h + 1]
            highest = jnp.maximum(before, jnp.max(scores, axis=0, keepdims=True))
            probs = jnp.exp(scores - highest)
            fade = jnp.exp(before - highest)
            top[h : h + 1] = highest
            total[h : h + 1] = total[h : h + 1] * fade + jnp.sum(probs, axis=0, keepdims=True)
            acc[h] = acc[h] * fade + dot(values, probs.astype(jnp.bfloat16), 1, 0)
        return carry

    lax.fori_loop(0, count[step], body, 0)
    sums = total[...]
    lse[...] = top[...] + jnp.log(sums)
    inverse = 1.0 / sums
    for h in range(heads):
        mixed[h] = acc[h] * inverse[h : h + 1]


def attend(count, tiles, q, kv, q_code, q_base, k_code):
    heads, _, rows = q.shape
    stack = pl.BlockSpec(kv.shape, lambda i, *_: (0, 0, 0))
    codes = pl.BlockSpec(k_code.shape, lambda i, *_: (0, 0, 0))
    line = pl.BlockSpec((1, TILE), lambda i, *_: (0, i))
    block = pl.BlockSpec((heads, HD, TILE), lambda i, *_: (0, 0, i))
    return pl.pallas_call(
        functools.partial(attend_kernel, heads),
        grid_spec=pltpu.PrefetchScalarGridSpec(
            num_scalar_prefetch=2,
            grid=(rows // TILE,),
            in_specs=[block, stack, line, line, codes],
            out_specs=[block, pl.BlockSpec((heads, TILE), lambda i, *_: (0, i))],
            scratch_shapes=[
                pltpu.VMEM((heads, TILE), jnp.float32),
                pltpu.VMEM((heads, TILE), jnp.float32),
                pltpu.VMEM((heads, HD, TILE), jnp.float32),
            ],
        ),
        out_shape=[
            jax.ShapeDtypeStruct((heads, HD, rows), jnp.float32),
            jax.ShapeDtypeStruct((heads, rows), jnp.float32),
        ],
        compiler_params=pltpu.CompilerParams(vmem_limit_bytes=60 * MIB),
        cost_estimate=SMALL,
    )(count, tiles, q, kv, q_code, q_base, k_code)


def attend_back_kernel(
    heads, count, tiles, q, kv, q_code, q_base, k_code, mixed, lse, upstream, dq, dkv, centre
):
    step = pl.program_id(0)

    @pl.when(step == 0)
    def _():
        dkv[...] = jnp.zeros_like(dkv)

    dq[...] = jnp.zeros_like(dq)
    code, base = q_code[...], q_base[...]
    for h in range(heads):
        centre[h : h + 1] = jnp.sum(
            mixed[h] * upstream[h].astype(jnp.float32), axis=0, keepdims=True
        )

    def body(j, carry):
        tile = tiles[step, j]
        keys = kv[tile, :HD]
        values = kv[tile, HD:]
        key_code = k_code[tile]
        allowed = (key_code <= code) & (key_code >= base)
        key_term = dkv[tile, :HD]
        value_term = dkv[tile, HD:]
        for h in range(heads):
            scores = dot(keys, q[h], 0, 0) - lse[h : h + 1]
            probs = jnp.exp(jnp.where(allowed, scores, NEGATIVE))
            grad_probs = dot(values, upstream[h], 0, 0)
            grad_scores = (probs * (grad_probs - centre[h : h + 1])).astype(jnp.bfloat16)
            value_term = value_term + dot(upstream[h], probs.astype(jnp.bfloat16), 1, 1)
            key_term = key_term + dot(q[h], grad_scores, 1, 1)
            dq[h] += dot(keys, grad_scores, 1, 0)
        dkv[tile, :HD] = key_term
        dkv[tile, HD:] = value_term
        return carry

    lax.fori_loop(0, count[step], body, 0)


def attend_back(count, tiles, q, kv, q_code, q_base, k_code, mixed, lse, upstream):
    heads, _, rows = q.shape
    stack = pl.BlockSpec(kv.shape, lambda i, *_: (0, 0, 0))
    codes = pl.BlockSpec(k_code.shape, lambda i, *_: (0, 0, 0))
    line = pl.BlockSpec((1, TILE), lambda i, *_: (0, i))
    block = pl.BlockSpec((heads, HD, TILE), lambda i, *_: (0, 0, i))
    return pl.pallas_call(
        functools.partial(attend_back_kernel, heads),
        grid_spec=pltpu.PrefetchScalarGridSpec(
            num_scalar_prefetch=2,
            grid=(rows // TILE,),
            in_specs=[
                block,
                stack,
                line,
                line,
                codes,
                block,
                pl.BlockSpec((heads, TILE), lambda i, *_: (0, i)),
                block,
            ],
            out_specs=[block, stack],
            scratch_shapes=[pltpu.VMEM((heads, TILE), jnp.float32)],
        ),
        out_shape=[
            jax.ShapeDtypeStruct((heads, HD, rows), jnp.float32),
            jax.ShapeDtypeStruct(kv.shape, jnp.float32),
        ],
        compiler_params=pltpu.CompilerParams(vmem_limit_bytes=60 * MIB),
        cost_estimate=cost(24),
    )(count, tiles, q, kv, q_code, q_base, k_code, mixed, lse, upstream)


def plan_tiles(q_code, q_base, k_code):
    rows, keys = q_code.shape[0], k_code.shape[0]
    allowed = (k_code[None, :] <= q_code[:, None]) & (k_code[None, :] >= q_base[:, None])
    used = jnp.any(allowed.reshape(rows // TILE, TILE, keys // TILE, TILE), axis=(1, 3))
    place = jnp.cumsum(used.astype(jnp.int32), axis=1) - 1
    ladder = jnp.arange(keys // TILE)
    hit = used[:, :, None] & (place[:, :, None] == ladder[None, None, :])
    tiles = jnp.sum(jnp.where(hit, ladder[None, :, None], 0), axis=1).astype(jnp.int32)
    return jnp.sum(used.astype(jnp.int32), axis=1), tiles


def nothing(*refs):
    pass


def after(values, *tokens):
    anywhere = pl.BlockSpec(memory_space=pl.ANY)
    return pl.pallas_call(
        nothing,
        in_specs=[anywhere] * (len(values) + len(tokens)),
        out_specs=[anywhere] * len(values),
        out_shape=[jax.ShapeDtypeStruct(v.shape, v.dtype) for v in values],
        input_output_aliases={i: i for i in range(len(values))},
    )(*values, *tokens)


def outer_kernel(parts, places, upstream, *refs):
    pieces, out = refs[:parts], refs[parts]
    total = 0.0
    for i in range(parts):
        columns = pl.ds(pl.multiple_of(places[i], TILE), pieces[i].shape[1])
        total = total + dot(upstream[:, columns], pieces[i][...], 1, 1)
    out[...] = total


def outer(places, upstream, down_w):
    count, width = upstream.shape
    units = down_w[0].shape[0]
    block = 256
    flat = [pl.BlockSpec((block, w.shape[1]), lambda i, *_: (i, 0)) for w in down_w]
    return pl.pallas_call(
        functools.partial(outer_kernel, len(down_w)),
        grid_spec=pltpu.PrefetchScalarGridSpec(
            num_scalar_prefetch=1,
            grid=(pl.cdiv(units, block),),
            in_specs=[pl.BlockSpec((count, width), lambda i, *_: (0, 0)), *flat],
            out_specs=pl.BlockSpec((count, block), lambda i, *_: (0, i)),
        ),
        out_shape=jax.ShapeDtypeStruct((count, units), jnp.float32),
        compiler_params=pltpu.CompilerParams(vmem_limit_bytes=60 * MIB),
        cost_estimate=SMALL,
    )(places, upstream, *down_w)


def middle_kernel(parts, places, rows, grads, *refs):
    pieces, (hidden, dgate, dupper) = refs[: 2 * parts], refs[2 * parts :]
    gate = upper = 0.0
    for i in range(parts):
        columns = pl.ds(pl.multiple_of(places[i], TILE), pieces[i].shape[0])
        left = rows[:, columns]
        gate = gate + dot(left, pieces[i][...], 1, 0)
        upper = upper + dot(left, pieces[parts + i][...], 1, 0)
    grad = grads[...]
    sigma = 1.0 / (1.0 + jnp.exp(-gate))
    swish = gate * sigma
    hidden[...] = (swish * upper).astype(jnp.bfloat16)
    dgate[...] = (grad * upper * sigma * (1.0 + gate * (1.0 - sigma))).astype(jnp.bfloat16)
    dupper[...] = (grad * swish).astype(jnp.bfloat16)


def middle(places, rows, grads, gate_w, upper_w):
    parts = len(gate_w)
    count, width = rows.shape
    units = gate_w[0].shape[1]
    block = 256
    out = pl.BlockSpec((count, block), lambda i, *_: (0, i))
    tall = [pl.BlockSpec((w.shape[0], block), lambda i, *_: (0, i)) for w in gate_w]
    return pl.pallas_call(
        functools.partial(middle_kernel, parts),
        grid_spec=pltpu.PrefetchScalarGridSpec(
            num_scalar_prefetch=1,
            grid=(pl.cdiv(units, block),),
            in_specs=[pl.BlockSpec((count, width), lambda i, *_: (0, 0)), out, *tall, *tall],
            out_specs=[out, out, out],
        ),
        out_shape=[jax.ShapeDtypeStruct((count, units), jnp.bfloat16)] * 3,
        compiler_params=pltpu.CompilerParams(vmem_limit_bytes=60 * MIB),
        cost_estimate=cost(9),
    )(places, rows, grads, *gate_w, *upper_w)


def project_kernel(parts, factors, steps, over_left, over_right, skip, places, *refs):
    lefts, pieces, out = refs[:factors], refs[factors:-1], refs[-1]
    step = pl.program_id(0)

    def one(i, start):
        total = 0.0
        for f in range(factors):
            left, right = lefts[f], pieces[f * parts + i]
            left = left[:, start:] if over_left else left[start:]
            right = right[:, start:] if over_right else right[start:]
            total = total + dot(left, right, over_left, over_right)
        out[...] = total.astype(out.dtype)

    for i in range(parts):
        here = (step >= i * steps) & (step < (i + 1) * steps)
        if skip:
            pl.when(here & (places[parts] == 0))(functools.partial(one, i, 0))
            pl.when(here & (places[parts] != 0))(functools.partial(one, i, skip))
        else:
            pl.when(here)(functools.partial(one, i, 0))


def project(places, lefts, weights, over_left, over_right, skip=0):
    parts, factors = len(weights[0]), len(lefts)
    axis = 1 - over_right
    size = weights[0][0].shape[axis]
    block = min(512, size)
    steps = size // block
    depth = weights[0][0].shape[over_right]
    count = lefts[0].shape[1 - over_left]

    def spec(i):
        at = lambda s: jnp.clip(s - i * steps, 0, steps - 1)
        if axis == 0:
            return pl.BlockSpec((block, depth), lambda s, *_: (at(s), 0))
        return pl.BlockSpec((depth, block), lambda s, *_: (0, at(s)))

    return pl.pallas_call(
        functools.partial(
            project_kernel, parts, factors, steps, over_left, over_right, skip
        ),
        grid_spec=pltpu.PrefetchScalarGridSpec(
            num_scalar_prefetch=1,
            grid=(parts * steps,),
            in_specs=[pl.BlockSpec(v.shape, lambda s, *_: (0, 0)) for v in lefts]
            + [spec(i) for _ in range(factors) for i in range(parts)],
            out_specs=pl.BlockSpec(
                (count, block), lambda s, p: (0, p[s // steps] // block + s % steps)
            ),
        ),
        out_shape=jax.ShapeDtypeStruct((count, parts * size), jnp.bfloat16),
        compiler_params=pltpu.CompilerParams(vmem_limit_bytes=60 * MIB),
        cost_estimate=cost(3 * len(lefts)),
    )(places, *lefts, *[w for weight in weights for w in weight])


def collect_kernel(parts, sets, places, *refs):
    rows, pieces, out = refs[:sets], refs[sets:-1], refs[-1]
    at = 0
    for block in rows:
        total = 0.0
        for i in range(parts):
            columns = pl.ds(pl.multiple_of(places[i], TILE), pieces[i].shape[1])
            total = total + dot(pieces[i][...], block[:, columns], 1, 1)
        out[:, at : at + block.shape[0]] = total.astype(out.dtype)
        at += block.shape[0]


def collect(places, rows, pieces):
    parts, count = len(pieces), sum(v.shape[0] for v in rows)
    units = pieces[0].shape[0]
    block = 256
    specs = [pl.BlockSpec((block, w.shape[1]), lambda i, *_: (i, 0)) for w in pieces]
    return pl.pallas_call(
        functools.partial(collect_kernel, parts, len(rows)),
        grid_spec=pltpu.PrefetchScalarGridSpec(
            num_scalar_prefetch=1,
            grid=(units // block,),
            in_specs=[pl.BlockSpec(v.shape, lambda i, *_: (0, 0)) for v in rows] + specs,
            out_specs=pl.BlockSpec((block, count), lambda i, *_: (i, 0)),
        ),
        out_shape=jax.ShapeDtypeStruct((units, count), jnp.bfloat16),
        compiler_params=pltpu.CompilerParams(vmem_limit_bytes=60 * MIB),
        cost_estimate=cost(5),
    )(places, *rows, *pieces)


def weigh_kernel(parts, at_left, at_right, wide, places, *refs):
    lefts, rights, out = refs[:parts], refs[parts:-1], refs[-1]
    columns = pl.ds(pl.multiple_of(places[at_right], TILE), wide)
    total = 0.0
    for left, right in zip(lefts, rights):
        total = total + dot(left[...], right[:, columns], 0, 0)
    out[...] = total.astype(out.dtype)


def weigh(places, lefts, at_left, tall, rights, at_right, wide):
    parts = len(lefts)
    count = lefts[0].shape[0]
    block = TILE if tall % 256 or lefts[0].shape[1] % 256 else 256
    return pl.pallas_call(
        functools.partial(weigh_kernel, parts, at_left, at_right, wide),
        grid_spec=pltpu.PrefetchScalarGridSpec(
            num_scalar_prefetch=1,
            grid=(tall // block,),
            in_specs=[
                pl.BlockSpec((count, block), lambda i, p: (0, p[at_left] // block + i))
                for _ in lefts
            ]
            + [pl.BlockSpec(v.shape, lambda i, p: (0, 0)) for v in rights],
            out_specs=pl.BlockSpec((block, wide), lambda i, p: (i, 0)),
        ),
        out_shape=jax.ShapeDtypeStruct((tall, wide), jnp.bfloat16),
        compiler_params=pltpu.CompilerParams(vmem_limit_bytes=60 * MIB),
        cost_estimate=cost(6),
    )(places, *lefts, *rights)


def plus_kernel(left, right, out):
    out[...] = (left[...].astype(jnp.float32) + right[...].astype(jnp.float32)).astype(out.dtype)


def plus(left, right):
    rows, width = left.shape
    block = rows // 4 if rows % 64 == 0 else rows
    spec = pl.BlockSpec((block, width), lambda i: (i, 0))
    return pl.pallas_call(
        plus_kernel,
        grid=(rows // block,),
        in_specs=[spec, spec],
        out_specs=spec,
        out_shape=jax.ShapeDtypeStruct(left.shape, left.dtype),
        compiler_params=pltpu.CompilerParams(vmem_limit_bytes=60 * MIB),
        cost_estimate=SMALL,
    )(left, right)


def entry_kernel(parts, query_steps, places, rows, cosine, sine, *refs):
    pieces, (q, kv) = refs[:parts], refs[parts:]
    step = pl.program_id(0)
    total = 0.0
    for i in range(parts):
        columns = pl.ds(pl.multiple_of(places[i], TILE), pieces[i].shape[0])
        total = total + dot(pieces[i][...], rows[:, columns], 0, 1)
    half = HD // 2

    def turned(start):
        former, latter = total[start : start + half], total[start + half : start + HD]
        return jnp.concatenate(
            [
                former * cosine[...] - latter * sine[...],
                latter * cosine[...] + former * sine[...],
            ],
            axis=0,
        ).astype(jnp.bfloat16)

    @pl.when(step < query_steps)
    def _():
        for start in (0, HD):
            q[start : start + HD] = turned(start) * 0.125

    @pl.when(step == query_steps)
    def _():
        keys = turned(0)
        values = total[HD:].astype(jnp.bfloat16)
        for j in range(kv.shape[0]):
            columns = slice(j * TILE, (j + 1) * TILE)
            kv[j, :HD] = keys[:, columns]
            kv[j, HD:] = values[:, columns]


def entry(places, rows, cosine, sine, pieces):
    parts = len(pieces)
    count, width = rows.shape
    steps = pieces[0].shape[1] // TILE - 1
    table = pl.BlockSpec(cosine.shape, lambda i, *_: (0, 0))
    return pl.pallas_call(
        functools.partial(entry_kernel, parts, steps),
        grid_spec=pltpu.PrefetchScalarGridSpec(
            num_scalar_prefetch=1,
            grid=(steps + 1,),
            in_specs=[pl.BlockSpec((count, width), lambda i, *_: (0, 0)), table, table]
            + [pl.BlockSpec((w.shape[0], TILE), lambda i, *_: (0, i)) for w in pieces],
            out_specs=[
                pl.BlockSpec((TILE, count), lambda i, *_: (jnp.minimum(i, steps - 1), 0)),
                pl.BlockSpec((count // TILE, TILE, TILE), lambda i, *_: (0, 0, 0)),
            ],
        ),
        out_shape=[
            jax.ShapeDtypeStruct((steps * TILE, count), jnp.bfloat16),
            jax.ShapeDtypeStruct((count // TILE, TILE, TILE), jnp.bfloat16),
        ],
        compiler_params=pltpu.CompilerParams(vmem_limit_bytes=60 * MIB),
        cost_estimate=SMALL,
    )(places, rows, cosine, sine, *pieces)


def place_kernel(order, first, second, out):
    step = pl.program_id(0)

    @pl.when(step < 2)
    def _():
        out[...] = first[...].astype(out.dtype)

    @pl.when(step >= 2)
    def _():
        out[...] = second[...].astype(out.dtype)


def place(order, halves, dtype):
    size, width = halves[0].shape[0] // 2, halves[0].shape[1]
    return pl.pallas_call(
        place_kernel,
        grid_spec=pltpu.PrefetchScalarGridSpec(
            num_scalar_prefetch=1,
            grid=(4,),
            in_specs=[
                pl.BlockSpec((size, width), lambda i, *_: (jnp.minimum(i, 1), 0)),
                pl.BlockSpec((size, width), lambda i, *_: (jnp.maximum(i - 2, 0), 0)),
            ],
            out_specs=pl.BlockSpec((size, width), lambda i, o: (o[i], 0)),
        ),
        out_shape=jax.ShapeDtypeStruct((4 * size, width), dtype),
        compiler_params=pltpu.CompilerParams(vmem_limit_bytes=60 * MIB),
        cost_estimate=cost(5),
    )(order, *halves)


def finish_kernel(axis, where, *refs):
    pieces, out = refs[:-1], refs[-1]
    for i in range(len(pieces) // 2):
        total = jnp.where(where[0] != 0, pieces[2 * i][...], pieces[2 * i + 1][...])
        total = total.astype(jnp.float32)
        at = pl.ds(pl.multiple_of(where[1 + i], TILE), total.shape[axis])
        if len(pieces) == 2:
            out[...] = total
        elif axis == 0:
            out[at] = total
        else:
            out[:, at] = total


def finish(where, axis, kept, *came):
    shape = list(kept.shape)
    shape[axis] += came[1].shape[axis] if len(came) > 1 else 0
    block = 256 if shape[1 - axis] % 256 == 0 else shape[1 - axis]

    def spec(size):
        if axis == 0:
            return pl.BlockSpec((size, block), lambda s, *_: (0, s))
        return pl.BlockSpec((block, size), lambda s, *_: (s, 0))

    return pl.pallas_call(
        functools.partial(finish_kernel, axis),
        grid_spec=pltpu.PrefetchScalarGridSpec(
            num_scalar_prefetch=1,
            grid=(shape[1 - axis] // block,),
            in_specs=[spec(p.shape[axis]) for p in (kept, *came)],
            out_specs=spec(shape[axis]),
        ),
        out_shape=jax.ShapeDtypeStruct(shape, jnp.float32),
        compiler_params=pltpu.CompilerParams(vmem_limit_bytes=60 * MIB),
        cost_estimate=cost(6),
    )(where, kept, *came)


def rms_scale(values):
    return lax.rsqrt(jnp.mean(values * values, axis=-1, keepdims=True) + epsilon)


def norm_back(values, scale, gain, upstream):
    weighted = upstream * gain
    return scale * weighted - values * scale**3 * jnp.mean(
        values * weighted, axis=-1, keepdims=True
    )


def turn(values, cosine, sine):
    half = HD // 2
    former, latter = values[:, :half], values[:, half:]
    return jnp.concatenate(
        [former * cosine - latter * sine, latter * cosine + former * sine], axis=1
    )


def per_device(
    sizes,
    tokens,
    first_gain,
    query_weight,
    keyval_weight,
    output_weight,
    second_gain,
    gate_weight,
    up_weight,
    down_weight,
    segment_ids,
    positions,
    cotangent,
):
    nx, nz, nt = sizes
    low, high = jnp.bfloat16, jnp.float32
    rows, width = tokens.shape
    block = rows // nt
    half = width // nx
    here_x, here_z, here_t = (lax.axis_index(a) for a in ("fsdp", "ctx", "tp"))
    paired = nx == 2
    assert nt == 4 and block % TILE == 0 and keyval_weight.shape[1] == 2 * HD
    order = jnp.stack([here_t ^ k for k in ORDER]).astype(jnp.int32)

    def arranged(whole, axis=0):
        return jnp.concatenate(
            [
                lax.dynamic_slice_in_dim(whole, (here_t ^ k) * block, block, axis)
                for k in ORDER
            ],
            axis=axis,
        )

    def part(whole, start, size, axis):
        return lax.dynamic_slice_in_dim(whole, start, size, axis)

    def mine(whole):
        return part(whole, here_x * half, half, 1)

    def theirs(whole):
        return part(whole, (1 - here_x) * half, half, 1)

    units = gate_weight.shape[1]
    query_width = query_weight.shape[1]
    heads = query_width // HD
    qkv_shard = jnp.concatenate([query_weight, keyval_weight], axis=1)
    gain_shards = jnp.stack([first_gain, second_gain])
    if paired:
        big = (units // TILE + 1) // 2 * TILE
        small = units - big
        spare = big - small
        places = jnp.stack(
            [here_x * half, (1 - here_x) * half, here_x, 0 * here_x, here_x * spare]
        ).astype(jnp.int32)
        at, at_theirs = here_x * small, (1 - here_x) * small
        gains_there = over_x(gain_shards)
        gains = jnp.where(
            here_x == 0,
            jnp.concatenate([gain_shards, gains_there], axis=1),
            jnp.concatenate([gains_there, gain_shards], axis=1),
        )
        qkv_w = (qkv_shard, over_x(qkv_shard))
        output_w = (output_weight, over_x(output_weight))
        fourth = half // nz

        def around(received):
            return lax.all_gather(received, "ctx", axis=0, tiled=True)

        def columns(weight):
            start = (here_z * fourth, at_theirs)
            return over_x(lax.dynamic_slice(weight, start, (fourth, big)))

        gate_fourth, upper_fourth = columns(gate_weight), columns(up_weight)
        gate_own, upper_own = part(gate_weight, at, big, 1), part(up_weight, at, big, 1)
        down_w = (part(down_weight, at, big, 0), over_x(part(down_weight, at_theirs, big, 0)))
    else:
        spare = 0
        places = jnp.zeros((2,), jnp.int32)
        whole = lambda shard, dim: lax.all_gather(shard, "fsdp", axis=dim, tiled=True)
        gains = whole(gain_shards, 1)
        qkv_w, output_w = (whole(qkv_shard, 0),), (whole(output_weight, 1),)
        gate_w, upper_w = (whole(gate_weight, 0),), (whole(up_weight, 0),)
        down_w = (whole(down_weight, 1),)
    gains = gains.astype(high)
    gain_one, gain_two = gains[0], gains[1]

    codes = arranged((segment_ids * CODE + positions).reshape(nz, rows), 1)
    bases = arranged((segment_ids * CODE).reshape(nz, rows), 1)
    q_code = lax.dynamic_index_in_dim(codes, here_z, 0, False)
    q_base = lax.dynamic_index_in_dim(bases, here_z, 0, False)
    k_code = jnp.concatenate(
        [
            lax.dynamic_index_in_dim(codes, (here_z + nz - d) % nz, 0, False)
            for d in range(nz)
        ]
    )
    count, tiles = plan_tiles(q_code, q_base, k_code)
    k_wide = jnp.broadcast_to(k_code.reshape(-1, TILE, 1), (nz * rows // TILE, TILE, TILE))
    masks = (q_code[None], q_base[None], k_wide)
    spots = (q_code - q_base).astype(high)
    freqs = jnp.exp(jnp.arange(HD // 2).astype(high) * (-2.0 * math.log(10000.0) / HD))
    angles = freqs[:, None] * spots[None, :]
    cosine, sine = jnp.cos(angles), jnp.sin(angles)

    tokens = arranged(tokens)
    cotangent = arranged(cotangent)
    inputs = tokens.astype(high)
    scale_one = rms_scale(inputs)
    normed_one = (inputs * scale_one * gain_one).astype(low)
    q, kv = entry(places, normed_one, cosine, sine, qkv_w)
    q = q.reshape(heads, HD, rows)
    kv = jnp.concatenate([kv] + [shift(kv, "ctx", nz, d) for d in range(1, nz)], axis=0)
    if paired:
        gate_fourth, upper_fourth = after([gate_fourth, upper_fourth], kv)
        gate_w = (gate_own, around(gate_fourth))
        upper_w = (upper_own, around(upper_fourth))

    mixed, lse = attend(count, tiles, q, kv, *masks)
    mixed_low = mixed.reshape(query_width, rows).astype(low)
    attn = project(places, [mixed_low], [output_w], 0, 0)
    keep, give = cut(attn[None], 1)
    attn_own, _ = scatter_rows(keep, give)
    one_own = inputs[:block] + attn_own
    scale_two = rms_scale(one_own)
    normed_own = (one_own * scale_two * gain_two).astype(low)

    if paired:
        there = over_x(cotangent[:block])
        there = jnp.concatenate([there, over_y(there)], axis=0)
        upstream = [
            jnp.concatenate([c, t], axis=0)
            for c, t in zip(jnp.split(cotangent, 2), (there, over_core(there)))
        ]
        (normed_own,) = after([normed_own], *upstream, down_w[1], gate_w[1])
        normed_two = gather_pair(normed_own, upper_w[1])
    else:
        normed_two = gather_own(normed_own)
        upstream = jnp.split(cotangent, 2)
    normed_two = [v.reshape(-1, width) for v in normed_two]
    sets = 2 if paired else 1

    def spread(value, dim):
        return lax.psum_scatter(value, "fsdp", scatter_dimension=dim, tiled=True)

    grads = [outer(places, u, down_w) for u in upstream]

    def forward(i):
        return middle(places, normed_two[i], grads[i], gate_w, upper_w)

    def back(i):
        made = project(places, [dgate[i], dupper[i]], [gate_w, upper_w], 1, 1, spare)
        return made.reshape(sets, -1, width)

    def ffn(i):
        return project(places, [hidden[i]], [down_w], 1, 0, spare).reshape(sets, -1, width)

    line = Line()
    hidden, dgate, dupper = [None, None], [None, None], [None, None]
    if paired:
        mixed_there, one_there = after([mixed_low, theirs(normed_one)], grads[0])
        mixed_there, one_there = over_x(mixed_there), over_x(one_there)
    for i in range(2):
        hidden[i], dgate[i], dupper[i] = forward(i)
    if paired:
        line.put(weigh(places, hidden, 3, big, upstream, 0, half))
        line.put(weigh(places, normed_two, 0, half, dgate, 3, big))
        line.put(weigh(places, normed_two, 0, half, dupper, 3, big))
    else:
        weight_grad = lambda lefts, rights: sum(
            dot(left, right, 0, 0) for left, right in zip(lefts, rights)
        ).astype(low)
        line.put(spread(weight_grad(hidden, upstream), 1))
        line.put(spread(weight_grad(normed_two, dgate), 0))
        line.put(spread(weight_grad(normed_two, dupper), 0))
    given = back(1)
    if paired:
        (places,) = after([places], given, mixed_there, one_there)
    grad_own, sent = scatter_rows(back(0), given)
    grad_one = cotangent[:block].astype(high) + norm_back(
        one_own, scale_two, gain_two, grad_own
    )
    grad_one_low = grad_one.astype(low)
    gain_two_sum = jnp.sum(grad_own * one_own * scale_two, axis=0)
    grad_attn = gather_own(grad_one_low)
    if paired:
        given = weigh(places, hidden, 4, small, upstream, 1, half)
        (given,) = after([given], *sent)
        came_down = over_x(given)
        line.put(came_down)
        given = weigh(places, normed_two, 1, half, dgate, 4, small)
        (given,) = after([given], came_down)
        came_gate = over_x(given)
        line.put(came_gate)
        given = weigh(places, normed_two, 1, half, dupper, 4, small)
        (given,) = after([given], came_gate)
        came_upper = over_x(given)
        line.put(came_upper)
    grad_mixed = collect(places, grad_attn, output_w).reshape(heads, HD, rows)
    grad_attn = jnp.concatenate(grad_attn, axis=0)

    dq, dkv = attend_back(count, tiles, q, kv, *masks, mixed, lse, grad_mixed)
    per = rows // TILE
    dkv_own = dkv[:per]
    moved = [dkv[d * per : (d + 1) * per].astype(low) for d in range(1, nz)]
    received = [shift(m, "ctx", nz, nz - 1 - d) for d, m in enumerate(moved)]
    if paired:
        (attn_there,) = after([theirs(grad_attn)], came_upper)
        output_grad = dot(mixed_low, mine(grad_attn), 1, 0) + dot(
            mixed_there, over_x(attn_there), 1, 0
        )
        line.put(output_grad.astype(low))
    else:
        line.put(spread(dot(mixed_low, grad_attn, 1, 0).astype(low), 1))
    for m in received:
        dkv_own = dkv_own + m.astype(high)
    dkv_own = jnp.transpose(dkv_own, (1, 0, 2)).reshape(2 * HD, rows)
    dq = turn(dq * 0.125, cosine, -sine).reshape(query_width, rows)
    dk = turn(dkv_own[None, :HD], cosine, -sine)[0]
    dqkv = jnp.concatenate([dq, dk, dkv_own[HD:]], axis=0).astype(low)
    first = project(places, [dqkv], [qkv_w], 0, 1)
    keep, give = cut(first[None], 1)
    first_own, _ = scatter_rows(keep, give)
    if paired:
        qkv_grad = (
            dot(mine(normed_one), dqkv, 0, 1) + dot(one_there, over_x(dqkv), 0, 1)
        ).astype(low)
    else:
        qkv_grad = spread(dot(normed_one, dqkv, 0, 1).astype(low), 0)
    scale_own = scale_one[:block]
    inputs_own = inputs[:block]
    gain_one_sum = jnp.sum(first_own * inputs_own * scale_own, axis=0)
    input_own = grad_one + norm_back(inputs_own, scale_own, gain_one, first_own)
    input_grad = place(order, gather_own(input_own.astype(low)), high)
    ffn_own, _ = scatter_rows(ffn(0), ffn(1))
    activations = place(order, gather_own((one_own + ffn_own).astype(low)), low)

    gain_sums = sum_all(jnp.stack([gain_one_sum, gain_two_sum]), "tp", nt)
    if paired:
        gain_sums = mine(gain_sums) + over_x(theirs(gain_sums))
    else:
        gain_sums = lax.psum_scatter(gain_sums, "fsdp", scatter_dimension=1, tiled=True)
    upper_half, lower_half = jnp.split(qkv_grad, 2)
    line.put(upper_half)
    long = lower_half.shape[1]
    extra = -(-gain_sums.size // (16 * long)) * 16
    gain_sums = jnp.pad(gain_sums.reshape(-1), (0, extra * long - gain_sums.size))
    gain_sums = gain_sums.reshape(extra, long).astype(low)
    line.put(jnp.concatenate([lower_half, gain_sums], axis=0))
    assert nz == 4
    inner = ((here_z == 1) | (here_z == 2)).astype(jnp.int32)
    if paired:
        where = jnp.stack([inner, here_x * small, (1 - here_x) * big]).astype(jnp.int32)
    else:
        where = jnp.stack([inner, 0, 0]).astype(jnp.int32)
    def whole(i):
        return jnp.where(inner != 0, line.total[i], line.done[i])

    down_grad, gate_grad, upper_grad = (
        finish(where, axis, *(v for k in ((i, i + 3) if paired else (i,)) for v in (line.total[k], line.done[k])))
        for i, axis in ((0, 0), (1, 1), (2, 1))
    )
    output_grad = whole(-3).astype(high)
    qkv_grad = jnp.concatenate([whole(-2), whole(-1)[:-extra]], axis=0).astype(high)
    gain_sums = whole(-1)[-extra:].astype(high).reshape(-1)[: 2 * half].reshape(2, half)
    return (
        activations,
        input_grad,
        gain_sums[0],
        qkv_grad[:, :query_width],
        qkv_grad[:, query_width:],
        output_grad,
        gain_sums[1],
        gate_grad,
        upper_grad,
        down_grad,
    )


def solution(mesh):
    placed = (
        P(("fsdp", "ctx"), None),
        P("fsdp"),
        P("fsdp", "tp"),
        P("fsdp", "tp"),
        P("tp", "fsdp"),
        P("fsdp"),
        P("fsdp", "tp"),
        P("fsdp", "tp"),
        P("tp", "fsdp"),
        P("fsdp"),
        P("fsdp"),
        P(("fsdp", "ctx"), None),
    )
    sizes = (mesh.shape["fsdp"], mesh.shape["ctx"], mesh.shape["tp"])
    return jax.shard_map(
        functools.partial(per_device, sizes),
        mesh=mesh,
        in_specs=placed,
        out_specs=(
            P(("fsdp", "ctx"), None),
            P(("fsdp", "ctx"), None),
            P("fsdp"),
            P("fsdp", "tp"),
            P("fsdp", "tp"),
            P("tp", "fsdp"),
            P("fsdp"),
            P("fsdp", "tp"),
            P("fsdp", "tp"),
            P("tp", "fsdp"),
        ),
        check_vma=False,
    )
```

time: 1010 us -> 732 us (0.72)
  waiting for transfers between devices: 661 us -> 224 us
  Pallas kernels: 78.1 us -> 199 us
  starting transfers between devices: 74 us -> 134 us
  matrix products: 52.6 us -> 8.27 us
  local copies, waits for them, and re-layouts: 23.1 us -> 45.7 us
  between operations: 2.56 us -> 16 us
    ppermute x37 -> x44, waiting for transfers between devices: 342 us -> 119 us  [swap(): return lax.ppermute(value, axis, pairs)]
    ppermute x15 -> x27, waiting for transfers between devices: 295 us -> 72.4 us  [the longest x9 32.1 us: put(): self.total.append(inward + lax.ppermute(inward, 'ctx', [(1, 2), (2, 1)]))]
    pallas_call x2 -> x40, Pallas kernels: 28.5 us -> 153 us  [the longest x6 42.1 us: project(): pl.pallas_call(functools.partial(project_kernel, parts, factors, steps, o...]
    dot_general x17 -> x4, matrix products: 52.6 us -> 8.27 us  [dot(): lax.dot_general(left, right, (((over_left,), (over_right,)), ((), ())), p...]
    select_n x14 -> x2, other arithmetic: 42.7 us -> 2.34 us  [whole(): return jnp.where(inner != 0, line.total[i], line.done[i])]
    ppermute x15 -> x27, starting transfers between devices: 38.5 us -> 72.4 us  [the longest x9 35 us: put(): self.done.append(lax.ppermute(self.total[-1], 'ctx', [(1, 0), (2, 3)]))]
    dynamic_slice x5 -> x11, local copies, waits for them, and re-layouts: 0.36 us -> 18.4 us  [the longest x6 11.6 us: part(): return lax.dynamic_slice_in_dim(whole, start, size, axis)]
    add x19 -> x26, other arithmetic: 23.7 us -> 40.9 us  [the longest x9 20.7 us: put(): inward = piece + self.came[-1]]
  transfers between devices with their start and end apart: 58 -> 79, of which waited for: 24 -> 34; matrix products, arithmetic and copies ran while one was open for 16% -> 19% of each run, Pallas kernels for 8% -> 27%
where the time goes in v2:
time: 732 us; the launch traced here: 726 us
  waiting for transfers between devices  224 us (31%)
  Pallas kernels  199 us (27%)
  starting transfers between devices  134 us (18%)
  other arithmetic  100 us (14%)
  local copies, waits for them, and re-layouts  45.7 us (6%)
  between operations  16 us (2%)
  matrix products  8.27 us (1%)
    ppermute x44, waiting for transfers between devices, swap(): return lax.ppermute(value, axis, pairs)  119 us
    pallas_call x6, Pallas kernels, project(): pl.pallas_call(functools.partial(project_kernel, parts, factors, steps, o...  42.1 us
    pallas_call x6, Pallas kernels, weigh(): pl.pallas_call(functools.partial(weigh_kernel, parts, at_left, at_right,...  38.2 us
    ppermute x44, starting transfers between devices, swap(): return lax.ppermute(value, axis, pairs)  37.5 us
    ppermute x9, starting transfers between devices, put(): self.done.append(lax.ppermute(self.total[-1], 'ctx', [(1, 0), (2, 3)]))  35 us
    pallas_call x1, Pallas kernels, attend_back(): pl.pallas_call(functools.partial(attend_back_kernel, heads), grid_spec=pl...  33.8 us
    ppermute x6, waiting for transfers between devices, shift(): return lax.ppermute(value, axis, pairs)  32.2 us
    ppermute x9, waiting for transfers between devices, put(): self.total.append(inward + lax.ppermute(inward, 'ctx', [(1, 2), (2, 1)]))  32.1 us
  transfers between devices with their start and end apart: 79, of which 34 were waited for; matrix products, arithmetic and copies ran while one was open for 19% of the time, Pallas kernels for 27%

profile of v2, /device:TPU:8, one launch (start us, length us, event | category | flops | bytes accessed | tf_op | source)
XLA Modules:
  0.0 726.1 jit_solution(18088216628349792494)
XLA Ops:
  32.1 11.4 %collective-permute-done.1.refs_1_.refs_2_ = bf16[1024,640]{1,0:T(8,128)(2,1)} collective-permute-done((bf16[1024,640]{1,0:T(8,128)(2,1)S(1)}, bf16[1024,640]{1,0:T(8,128)(2,1)}, u32[]{:S(2)}, u32[]{:S(2)}) %collective-permute-start.1) | collective-permute-done | bytes 1310752 | tf_op jit(solution)/shard_map/ppermute | solution.py:43
  43.5 8.2 %shard_map.195 = (bf16[512,512]{1,0:T(8,128)(2,1)}, bf16[4,128,128]{2,1,0:T(8,128)(2,1)}) custom-call(s32[5]{0:T(128)} %stack.87.places.refs_0_, bf16[512,2048]{1,0:T(8,128)(2,1)} %multiply_convert_fusion.rows, f32[32,512]{1,0:T(8,128)} %get-tuple-element.98.cosine, f32[32,512]{1,0:T(8,128)} %get-tuple-element.97.sine, bf16[1024,640]{1,0:T(8,128)(2,1)} %copy-done.11, ...), custom_call_target="tpu_custom_call" | custom-call | flops 1000000 | bytes 100000 | tf_op jit(solution)/shard_map/pallas_call | solution.py:537
  63.8 10.5 %collective-permute-done.12.refs_0_ = bf16[256,768]{1,0:T(8,128)(2,1)S(1)} collective-permute-done((bf16[256,768]{1,0:T(8,128)(2,1)}, bf16[256,768]{1,0:T(8,128)(2,1)S(1)}, u32[]{:S(2)}, u32[]{:S(2)}) %collective-permute-start.12) | collective-permute-done | bytes 393248 | tf_op jit(solution)/shard_map/ppermute | solution.py:43
  74.3 8.5 %collective-permute-done.13.refs_1_ = bf16[256,768]{1,0:T(8,128)(2,1)} collective-permute-done((bf16[256,768]{1,0:T(8,128)(2,1)}, bf16[256,768]{1,0:T(8,128)(2,1)}, u32[]{:S(2)}, u32[]{:S(2)}) %collective-permute-start.13) | collective-permute-done | bytes 393248 | tf_op jit(solution)/shard_map/ppermute | solution.py:43
  85.3 11.8 %shard_map.196 = (f32[8,64,512]{2,1,0:T(8,128)}, f32[8,512]{1,0:T(8,128)}) custom-call(s32[4]{0:T(128)} %convert_reduce_fusion.count, s32[4,16]{1,0:T(4,128)} %select_reduce_fusion.tiles, bf16[8,64,512]{2,1,0:T(8,128)(2,1)} %bitcast.131, bf16[16,128,128]{2,1,0:T(8,128)(2,1)} %copy-done.34, s32[1,512]{1,0:T(1,128)} %copy-done.66, s32[1,512]{1,0:T(1,128)} %copy-done.67, ...), custom_call_target="tpu_custom_call" | custom-call | flops 1000000 | bytes 100000 | tf_op jit(solution)/shard_map/pallas_call | solution.py:176
  99.2 5.7 shard_map.197
  116.8 5.0 collective-permute-done.9
  134.5 7.4 %collective-permute-done.7 = bf16[128,2048]{1,0:T(8,128)(2,1)} collective-permute-done((bf16[128,2048]{1,0:T(8,128)(2,1)}, bf16[128,2048]{1,0:T(8,128)(2,1)}, u32[]{:S(2)}, u32[]{:S(2)}) %collective-permute-start.7) | collective-permute-done | bytes 524320 | tf_op jit(solution)/shard_map/ppermute | solution.py:43
  153.8 5.6 collective-permute-done.16
  161.8 10.3 %collective-permute-done.17 = bf16[256,1024]{1,0:T(8,128)(2,1)S(1)} collective-permute-done((bf16[256,1024]{1,0:T(8,128)(2,1)S(1)}, bf16[256,1024]{1,0:T(8,128)(2,1)S(1)}, u32[]{:S(2)}, u32[]{:S(2)}) %collective-permute-start.17) | collective-permute-done | bytes 524320 | tf_op jit(solution)/shard_map/ppermute | solution.py:43
  178.1 6.3 shard_map.204.refs_2_.grads
  189.1 6.3 shard_map.201.grads
  196.8 9.2 %shard_map.202 = (bf16[512,768]{1,0:T(8,128)(2,1)}, bf16[512,768]{1,0:T(8,128)(2,1)}, bf16[512,768]{1,0:T(8,128)(2,1)}) custom-call(s32[5]{0:T(128)} %stack.87.places.refs_0_, bf16[512,2048]{1,0:T(8,128)(2,1)} %bitcast.111, f32[512,768]{1,0:T(8,128)} %shard_map.201.grads, bf16[1024,768]{1,0:T(8,128)(2,1)} %constant_dynamic-slice_fusion.7.refs_0_.refs_2_, ...), custom_call_target="tpu_custom_call" | custom-call | flops 1000000 | bytes 16605000 | tf_op jit(solution)/shard_map/pallas_call | solution.py:347
  206.0 8.7 %shard_map.203 = bf16[512,2048]{1,0:T(8,128)(2,1)} custom-call(s32[5]{0:T(128)} %stack.87.places.refs_0_, bf16[512,768]{1,0:T(8,128)(2,1)} %get-tuple-element.31.refs_0_.refs_3_, bf16[512,768]{1,0:T(8,128)(2,1)} %get-tuple-element.32.refs_1_.refs_3_, bf16[1024,768]{1,0:T(8,128)(2,1)} %constant_dynamic-slice_fusion.7.refs_0_.refs_2_, ...), custom_call_target="tpu_custom_call" | custom-call | flops 1000000 | bytes 11070000 | tf_op jit(solution)/shard_map/pallas_call | solution.py:398
  216.2 9.2 %shard_map.207 = (bf16[512,768]{1,0:T(8,128)(2,1)}, bf16[512,768]{1,0:T(8,128)(2,1)}, bf16[512,768]{1,0:T(8,128)(2,1)}) custom-call(s32[5]{0:T(128)} %stack.87.places.refs_0_, bf16[512,2048]{1,0:T(8,128)(2,1)} %bitcast.106, f32[512,768]{1,0:T(8,128)} %shard_map.204.refs_2_.grads, bf16[1024,768]{1,0:T(8,128)(2,1)} %constant_dynamic-slice_fusion.7.refs_0_.refs_2_, ...), custom_call_target="tpu_custom_call" | custom-call | flops 1000000 | bytes 16605000 | tf_op jit(solution)/shard_map/pallas_call | solution.py:347
  225.4 6.6 shard_map.225
  233.5 6.1 shard_map.224.refs_0_
  239.6 6.1 shard_map.223.refs_0_
  246.4 6.4 shard_map.209
  252.8 8.7 %shard_map.211 = bf16[512,2048]{1,0:T(8,128)(2,1)} custom-call(s32[5]{0:T(128)} %shard_map.206.places, bf16[512,768]{1,0:T(8,128)(2,1)} %get-tuple-element.37.refs_0_.refs_2_, bf16[512,768]{1,0:T(8,128)(2,1)} %get-tuple-element.38.refs_1_.refs_2_, bf16[1024,768]{1,0:T(8,128)(2,1)} %constant_dynamic-slice_fusion.7.refs_0_.refs_2_, ...), custom_call_target="tpu_custom_call" | custom-call | flops 1000000 | bytes 11070000 | tf_op jit(solution)/shard_map/pallas_call | solution.py:398
  261.5 6.4 shard_map.208
  275.6 6.1 collective-permute-start.52
  289.9 9.2 %collective-permute-done.31 = bf16[2,128,1024]{2,1,0:T(8,128)(2,1)S(1)} collective-permute-done((bf16[2,128,1024]{2,1,0:T(8,128)(2,1)S(1)}, bf16[2,128,1024]{2,1,0:T(8,128)(2,1)S(1)}, u32[]{:S(2)}, u32[]{:S(2)}) %collective-permute-start.31) | collective-permute-done | bytes 524320 | tf_op jit(solution)/shard_map/ppermute | solution.py:43
  301.7 6.6 collective-permute-done.24
  320.3 4.9 collective-permute-done.23
  332.8 7.4 %shard_map.218.refs_0_ = bf16[640,1024]{1,0:T(8,128)(2,1)} custom-call(s32[5]{0:T(128)} %shard_map.206.places, bf16[512,768]{1,0:T(8,128)(2,1)} %get-tuple-element.35.refs_0_, bf16[512,768]{1,0:T(8,128)(2,1)} %get-tuple-element.36.refs_0_.refs_1_, bf16[512,2048]{1,0:T(8,128)(2,1)} %pad_maximum_fusion.refs_1_.upstream.refs_2_, ...), custom_call_target="tpu_custom_call" | custom-call | flops 1000000 | bytes 11070000 | tf_op jit(solution)/shard_map/pallas_call | solution.py:461
  342.2 6.9 collective-permute-start.55
  355.3 6.0 shard_map.217.refs_0_
  367.9 33.8 %shard_map.213 = (f32[8,64,512]{2,1,0:T(8,128)}, f32[16,128,128]{2,1,0:T(8,128)}) custom-call(s32[4]{0:T(128)} %convert_reduce_fusion.count, s32[4,16]{1,0:T(4,128)} %select_reduce_fusion.tiles, bf16[8,64,512]{2,1,0:T(8,128)(2,1)} %bitcast.132, bf16[16,128,128]{2,1,0:T(8,128)(2,1)} %copy-done.34, s32[1,512]{1,0:T(1,128)} %copy-done.66, s32[1,512]{1,0:T(1,128)} %copy-done.67, ...), custom_call_target="tpu_custom_call" | custom-call | flops 1000000 | bytes 44280000 | tf_op jit(solution)/shard_map/pallas_call | solution.py:243
  403.9 7.2 collective-permute-start.37
  411.1 9.6 %collective-permute-start.36 = (bf16[4,128,128]{2,1,0:T(8,128)(2,1)}, bf16[4,128,128]{2,1,0:T(8,128)(2,1)S(1)}, u32[]{:S(2)}, u32[]{:S(2)}) collective-permute-start(bf16[4,128,128]{2,1,0:T(8,128)(2,1)} %get-tuple-element.70), channel_id=1, source_target_pairs={{0,8},{4,12},{8,0},{12,4},{1,9},{5,13},{9,1},{13,5},{2,10},{6,14},... | collective-permute-start | bytes 393224 | tf_op jit(solution)/shard_map/ppermute | solution.py:48
  434.8 26.9 %collective-permute-done.35 = bf16[4,128,128]{2,1,0:T(8,128)(2,1)} collective-permute-done((bf16[4,128,128]{2,1,0:T(8,128)(2,1)}, bf16[4,128,128]{2,1,0:T(8,128)(2,1)}, u32[]{:S(2)}, u32[]{:S(2)}) %collective-permute-start.35) | collective-permute-done | bytes 131104 | tf_op jit(solution)/shard_map/ppermute | solution.py:48
  464.2 6.2 shard_map.214
  477.6 6.0 shard_map.216.refs_0_
  497.9 17.7 %collective-permute-done.48.refs_1_.refs_0_ = bf16[1024,640]{1,0:T(8,128)(2,1)} collective-permute-done((bf16[1024,640]{1,0:T(8,128)(2,1)}, bf16[1024,640]{1,0:T(8,128)(2,1)}, u32[]{:S(2)}, u32[]{:S(2)}) %collective-permute-start.48) | collective-permute-done | bytes 1310752 | tf_op jit(solution)/shard_map/ppermute | solution.py:43
  527.4 5.7 collective-permute-start.64
  545.2 6.5 collective-permute-done.49
  563.8 5.0 collective-permute-done.63
  579.0 14.7 %collective-permute-done.65.refs_1_ = bf16[512,1024]{1,0:T(8,128)(2,1)S(1)} collective-permute-done((bf16[512,1024]{1,0:T(8,128)(2,1)}, bf16[512,1024]{1,0:T(8,128)(2,1)S(1)}, u32[]{:S(2)}, u32[]{:S(2)}) %collective-permute-start.65) | collective-permute-done | bytes 1048608 | tf_op jit(solution)/shard_map/ppermute | solution.py:129
  625.0 8.2 %collective-permute-done.70.refs_3_ = bf16[1024,640]{1,0:T(8,128)(2,1)} collective-permute-done((bf16[1024,640]{1,0:T(8,128)(2,1)S(1)}, bf16[1024,640]{1,0:T(8,128)(2,1)}, u32[]{:S(2)}, u32[]{:S(2)}) %collective-permute-start.70) | collective-permute-done | bytes 1310752 | tf_op jit(solution)/shard_map/ppermute | solution.py:132
  637.9 5.6 collective-permute-start.76
  647.0 5.4 collective-permute-done.71
  655.7 8.5 %collective-permute-done.74 = bf16[512,640]{1,0:T(8,128)(2,1)S(1)} collective-permute-done((bf16[512,640]{1,0:T(8,128)(2,1)S(1)}, bf16[512,640]{1,0:T(8,128)(2,1)S(1)}, u32[]{:S(2)}, u32[]{:S(2)}) %collective-permute-start.74) | collective-permute-done | bytes 655392 | tf_op jit(solution)/shard_map/ppermute | solution.py:131
  667.9 10.1 %collective-permute-done.72 = bf16[528,640]{1,0:T(8,128)(2,1)} collective-permute-done((bf16[528,640]{1,0:T(8,128)(2,1)}, bf16[528,640]{1,0:T(8,128)(2,1)}, u32[]{:S(2)}, u32[]{:S(2)}) %collective-permute-start.72) | collective-permute-done | bytes 675872 | tf_op jit(solution)/shard_map/ppermute | solution.py:131
  687.9 5.2 shard_map.215
  693.0 6.2 shard_map.236
  699.3 6.2 shard_map.234
  705.5 6.2 shard_map.235
  (449 shorter events, 297.6 us)
Async XLA Ops:
  7.2 142.3 %all-gather.3.cloned.1.call-start = ((), (), s32[]{:S(2)}) async-start(), calls=%async_computation | async-start | bytes 1966080 | tf_op jit(solution)/shard_map/all_gather | solution.py:713
  11.6 31.9 %collective-permute-start.1 = (bf16[1024,640]{1,0:T(8,128)(2,1)S(1)}, bf16[1024,640]{1,0:T(8,128)(2,1)}, u32[]{:S(2)}, u32[]{:S(2)}) collective-permute-start(bf16[1024,640]{1,0:T(8,128)(2,1)S(1)} %constant_dynamic-update-slice_fusion.refs_0_.refs_1_), channel_id=1, source_target_pairs={{0,16},{16,0},{1,17},{17,1},{2,18},{18,2},{3,19},{19,3},{4,20},{20... | collective-permute-start | bytes 3932168 | tf_op jit(solution)/shard_map/ppermute | solution.py:43
  12.2 87.0 %collective-permute-start.5 = (bf16[512,1024]{1,0:T(8,128)(2,1)}, bf16[512,1024]{1,0:T(8,128)(2,1)}, u32[]{:S(2)}, u32[]{:S(2)}) collective-permute-start(bf16[512,1024]{1,0:T(8,128)(2,1)} %refs_2_.1), channel_id=1, source_target_pairs={{0,16},{16,0},{1,17},{17,1},{2,18},{18,2},{3,19},{19,3},{4,20},{20... | collective-permute-start | bytes 3145736 | tf_op jit(solution)/shard_map/ppermute | solution.py:43
  15.5 58.8 %collective-permute-start.12 = (bf16[256,768]{1,0:T(8,128)(2,1)}, bf16[256,768]{1,0:T(8,128)(2,1)S(1)}, u32[]{:S(2)}, u32[]{:S(2)}) collective-permute-start(bf16[256,768]{1,0:T(8,128)(2,1)} %dynamic_slice.126), channel_id=1, source_target_pairs={{0,16},{16,0},{1,17},{17,1},{2,18},{18,2},{3,19},{19,3},{4,20},{20... | collective-permute-start | bytes 1179656 | tf_op jit(solution)/shard_map/ppermute | solution.py:43
  17.8 65.0 %collective-permute-start.13 = (bf16[256,768]{1,0:T(8,128)(2,1)}, bf16[256,768]{1,0:T(8,128)(2,1)}, u32[]{:S(2)}, u32[]{:S(2)}) collective-permute-start(bf16[256,768]{1,0:T(8,128)(2,1)} %dynamic_slice.127), channel_id=1, source_target_pairs={{0,16},{16,0},{1,17},{17,1},{2,18},{18,2},{3,19},{19,3},{4,20},{20... | collective-permute-start | bytes 1179656 | tf_op jit(solution)/shard_map/ppermute | solution.py:43
  60.7 46.5 %collective-permute-start.8 = (bf16[128,2048]{1,0:T(8,128)(2,1)S(1)}, bf16[128,2048]{1,0:T(8,128)(2,1)}, u32[]{:S(2)}, u32[]{:S(2)}) collective-permute-start(bf16[128,2048]{1,0:T(8,128)(2,1)S(1)} %copy-done.40), channel_id=1, source_target_pairs={{0,16},{16,0},{1,17},{17,1},{2,18},{18,2},{3,19},{19,3},{4,20},{20... | collective-permute-start | bytes 1572872 | tf_op jit(solution)/shard_map/ppermute | solution.py:43
  82.9 92.1 %all-gather.5.cloned.1.call-start = ((), (), s32[]{:S(2)}) async-start(), calls=%async_computation.1 | async-start | bytes 1966080 | tf_op jit(solution)/shard_map/all_gather | solution.py:713
  112.7 36.7 %collective-permute-start.11 = (bf16[768,1024]{1,0:T(8,128)(2,1)}, bf16[768,1024]{1,0:T(8,128)(2,1)S(1)}, u32[]{:S(2)}, u32[]{:S(2)}) collective-permute-start(bf16[768,1024]{1,0:T(8,128)(2,1)} %get-tuple-element.54), channel_id=1, source_target_pairs={{0,16},{16,0},{1,17},{17,1},{2,18},{18,2},{3,19},{19,3},{4,20},{20... | collective-permute-start | bytes 4718600 | tf_op jit(solution)/shard_map/ppermute | solution.py:43
  184.4 61.2 %collective-permute-start.20 = (bf16[512,1024]{1,0:T(8,128)(2,1)}, bf16[512,1024]{1,0:T(8,128)(2,1)}, u32[]{:S(2)}, u32[]{:S(2)}) collective-permute-start(bf16[512,1024]{1,0:T(8,128)(2,1)} %get-tuple-element.34), channel_id=1, source_target_pairs={{0,16},{16,0},{1,17},{17,1},{2,18},{18,2},{3,19},{19,3},{4,20},{20... | collective-permute-start | bytes 3145736 | tf_op jit(solution)/shard_map/ppermute | solution.py:43
  214.7 66.9 %collective-permute-start.28 = (bf16[2,256,2048]{2,1,0:T(8,128)(2,1)}, bf16[2,256,2048]{2,1,0:T(8,128)(2,1)}, u32[]{:S(2)}, u32[]{:S(2)}) collective-permute-start(bf16[2,256,2048]{2,1,0:T(8,128)(2,1)} %bitcast.121), channel_id=1, source_target_pairs={{0,1},{1,0},{2,3},{3,2},{4,5},{5,4},{6,7},{7,6},{8,9},{9,8},{10,11... | collective-permute-start | bytes 6291464 | tf_op jit(solution)/shard_map/ppermute | solution.py:43
  214.8 30.8 %collective-permute-start.19 = (bf16[512,512]{1,0:T(8,128)(2,1)S(1)}, bf16[512,512]{1,0:T(8,128)(2,1)S(1)}, u32[]{:S(2)}, u32[]{:S(2)}) collective-permute-start(bf16[512,512]{1,0:T(8,128)(2,1)S(1)} %copy-done.52), channel_id=1, source_target_pairs={{0,16},{16,0},{1,17},{17,1},{2,18},{18,2},{3,19},{19,3},{4,20},{20... | collective-permute-start | bytes 1572872 | tf_op jit(solution)/shard_map/ppermute | solution.py:43
  232.0 38.4 %collective-permute-start.50 = (bf16[768,1024]{1,0:T(8,128)(2,1)}, bf16[768,1024]{1,0:T(8,128)(2,1)S(1)}, u32[]{:S(2)}, u32[]{:S(2)}) collective-permute-start(bf16[768,1024]{1,0:T(8,128)(2,1)} %shard_map.225), channel_id=1, source_target_pairs={{0,4},{12,8},{1,5},{13,9},{2,6},{14,10},{3,7},{15,11},{16,20},{28,... | collective-permute-start | bytes 4718600 | tf_op jit(solution)/shard_map/ppermute | solution.py:129
  252.8 33.0 %collective-permute-start.21 = (bf16[2,256,2048]{2,1,0:T(8,128)(2,1)}, bf16[2,256,2048]{2,1,0:T(8,128)(2,1)}, u32[]{:S(2)}, u32[]{:S(2)}) collective-permute-start(bf16[2,256,2048]{2,1,0:T(8,128)(2,1)} %bitcast.129), channel_id=1, source_target_pairs={{0,1},{1,0},{2,3},{3,2},{4,5},{5,4},{6,7},{7,6},{8,9},{9,8},{10,11... | collective-permute-start | bytes 6291464 | tf_op jit(solution)/shard_map/ppermute | solution.py:43
  271.6 58.6 %collective-permute-start.51 = (bf16[1024,768]{1,0:T(8,128)(2,1)}, bf16[1024,768]{1,0:T(8,128)(2,1)S(1)}, u32[]{:S(2)}, u32[]{:S(2)}) collective-permute-start(bf16[1024,768]{1,0:T(8,128)(2,1)} %shard_map.226), channel_id=1, source_target_pairs={{0,4},{12,8},{1,5},{13,9},{2,6},{14,10},{3,7},{15,11},{16,20},{28,... | collective-permute-start | bytes 4718600 | tf_op jit(solution)/shard_map/ppermute | solution.py:129
  275.6 52.8 %collective-permute-start.52 = (bf16[768,1024]{1,0:T(8,128)(2,1)S(1)}, bf16[768,1024]{1,0:T(8,128)(2,1)S(1)}, u32[]{:S(2)}, u32[]{:S(2)}) collective-permute-start(bf16[768,1024]{1,0:T(8,128)(2,1)S(1)} %add.320), channel_id=1, source_target_pairs={{4,8},{8,4},{5,9},{9,5},{6,10},{10,6},{7,11},{11,7},{20,24},{24,20... | collective-permute-start | bytes 4718600 | tf_op jit(solution)/shard_map/ppermute | solution.py:131
  327.0 26.9 %collective-permute-start.33 = (bf16[128,2048]{1,0:T(8,128)(2,1)}, bf16[128,2048]{1,0:T(8,128)(2,1)}, u32[]{:S(2)}, u32[]{:S(2)}) collective-permute-start(bf16[128,2048]{1,0:T(8,128)(2,1)} %get-tuple-element.46), channel_id=1, source_target_pairs={{0,2},{1,3},{2,0},{3,1},{4,6},{5,7},{6,4},{7,5},{8,10},{9,11},{10,... | collective-permute-start | bytes 1572872 | tf_op jit(solution)/shard_map/ppermute | solution.py:43
  331.3 89.3 %collective-permute-start.53 = (bf16[1024,768]{1,0:T(8,128)(2,1)}, bf16[1024,768]{1,0:T(8,128)(2,1)}, u32[]{:S(2)}, u32[]{:S(2)}) collective-permute-start(bf16[1024,768]{1,0:T(8,128)(2,1)} %shard_map.227), channel_id=1, source_target_pairs={{0,4},{12,8},{1,5},{13,9},{2,6},{14,10},{3,7},{15,11},{16,20},{28,... | collective-permute-start | bytes 4718600 | tf_op jit(solution)/shard_map/ppermute | solution.py:129
  340.3 22.8 %collective-permute-start.46 = (bf16[640,1024]{1,0:T(8,128)(2,1)}, bf16[640,1024]{1,0:T(8,128)(2,1)}, u32[]{:S(2)}, u32[]{:S(2)}) collective-permute-start(bf16[640,1024]{1,0:T(8,128)(2,1)} %shard_map.219), channel_id=1, source_target_pairs={{0,16},{16,0},{1,17},{17,1},{2,18},{18,2},{3,19},{19,3},{4,20},{20... | collective-permute-start | bytes 3932168 | tf_op jit(solution)/shard_map/ppermute | solution.py:43
  342.2 87.8 %collective-permute-start.55 = (bf16[768,1024]{1,0:T(8,128)(2,1)S(1)}, bf16[768,1024]{1,0:T(8,128)(2,1)}, u32[]{:S(2)}, u32[]{:S(2)}) collective-permute-start(bf16[768,1024]{1,0:T(8,128)(2,1)S(1)} %copy-done.5), channel_id=1, source_target_pairs={{4,0},{8,12},{5,1},{9,13},{6,2},{10,14},{7,3},{11,15},{20,16},{24,... | collective-permute-start | bytes 4718600 | tf_op jit(solution)/shard_map/ppermute | solution.py:132
  352.0 74.4 %collective-permute-start.54 = (bf16[1024,768]{1,0:T(8,128)(2,1)}, bf16[1024,768]{1,0:T(8,128)(2,1)}, u32[]{:S(2)}, u32[]{:S(2)}) collective-permute-start(bf16[1024,768]{1,0:T(8,128)(2,1)} %add.322), channel_id=1, source_target_pairs={{4,8},{8,4},{5,9},{9,5},{6,10},{10,6},{7,11},{11,7},{20,24},{24,20... | collective-permute-start | bytes 4718600 | tf_op jit(solution)/shard_map/ppermute | solution.py:131
  403.9 29.5 %collective-permute-start.37 = (bf16[4,128,128]{2,1,0:T(8,128)(2,1)}, bf16[4,128,128]{2,1,0:T(8,128)(2,1)S(1)}, u32[]{:S(2)}, u32[]{:S(2)}) collective-permute-start(bf16[4,128,128]{2,1,0:T(8,128)(2,1)} %get-tuple-element.69), channel_id=1, source_target_pairs={{0,4},{4,8},{8,12},{12,0},{1,5},{5,9},{9,13},{13,1},{2,6},{6,10},{... | collective-permute-start | bytes 393224 | tf_op jit(solution)/shard_map/ppermute | solution.py:48
  423.7 49.2 %collective-permute-start.57 = (bf16[1024,768]{1,0:T(8,128)(2,1)}, bf16[1024,768]{1,0:T(8,128)(2,1)}, u32[]{:S(2)}, u32[]{:S(2)}) collective-permute-start(bf16[1024,768]{1,0:T(8,128)(2,1)} %add.324), channel_id=1, source_target_pairs={{4,8},{8,4},{5,9},{9,5},{6,10},{10,6},{7,11},{11,7},{20,24},{24,20... | collective-permute-start | bytes 4718600 | tf_op jit(solution)/shard_map/ppermute | solution.py:131
  426.4 35.3 %collective-permute-start.35 = (bf16[4,128,128]{2,1,0:T(8,128)(2,1)}, bf16[4,128,128]{2,1,0:T(8,128)(2,1)}, u32[]{:S(2)}, u32[]{:S(2)}) collective-permute-start(bf16[4,128,128]{2,1,0:T(8,128)(2,1)} %get-tuple-element.68), channel_id=1, source_target_pairs={{0,12},{4,0},{8,4},{12,8},{1,13},{5,1},{9,5},{13,9},{2,14},{6,2},{... | collective-permute-start | bytes 393224 | tf_op jit(solution)/shard_map/ppermute | solution.py:48
  430.0 59.0 %collective-permute-start.58 = (bf16[1024,768]{1,0:T(8,128)(2,1)S(1)}, bf16[1024,768]{1,0:T(8,128)(2,1)}, u32[]{:S(2)}, u32[]{:S(2)}) collective-permute-start(bf16[1024,768]{1,0:T(8,128)(2,1)S(1)} %add.323.refs_2_.refs_0_), channel_id=1, source_target_pairs={{4,0},{8,12},{5,1},{9,13},{6,2},{10,14},{7,3},{11,15},{20,16},{24,... | collective-permute-start | bytes 4718600 | tf_op jit(solution)/shard_map/ppermute | solution.py:132
  433.3 50.2 %collective-permute-start.47 = (bf16[1024,640]{1,0:T(8,128)(2,1)}, bf16[1024,640]{1,0:T(8,128)(2,1)}, u32[]{:S(2)}, u32[]{:S(2)}) collective-permute-start(bf16[1024,640]{1,0:T(8,128)(2,1)} %shard_map.220), channel_id=1, source_target_pairs={{0,16},{16,0},{1,17},{17,1},{2,18},{18,2},{3,19},{19,3},{4,20},{20... | collective-permute-start | bytes 3932168 | tf_op jit(solution)/shard_map/ppermute | solution.py:43
  433.4 50.3 %collective-permute-start.56 = (bf16[640,1024]{1,0:T(8,128)(2,1)}, bf16[640,1024]{1,0:T(8,128)(2,1)}, u32[]{:S(2)}, u32[]{:S(2)}) collective-permute-start(bf16[640,1024]{1,0:T(8,128)(2,1)} %shard_map.228), channel_id=1, source_target_pairs={{0,4},{12,8},{1,5},{13,9},{2,6},{14,10},{3,7},{15,11},{16,20},{28,... | collective-permute-start | bytes 3932168 | tf_op jit(solution)/shard_map/ppermute | solution.py:129
  475.1 48.7 %collective-permute-start.61 = (bf16[1024,768]{1,0:T(8,128)(2,1)S(1)}, bf16[1024,768]{1,0:T(8,128)(2,1)}, u32[]{:S(2)}, u32[]{:S(2)}) collective-permute-start(bf16[1024,768]{1,0:T(8,128)(2,1)S(1)} %add.325.refs_2_.refs_0_), channel_id=1, source_target_pairs={{4,0},{8,12},{5,1},{9,13},{6,2},{10,14},{7,3},{11,15},{20,16},{24,... | collective-permute-start | bytes 4718600 | tf_op jit(solution)/shard_map/ppermute | solution.py:132
  483.6 32.0 %collective-permute-start.48 = (bf16[1024,640]{1,0:T(8,128)(2,1)}, bf16[1024,640]{1,0:T(8,128)(2,1)}, u32[]{:S(2)}, u32[]{:S(2)}) collective-permute-start(bf16[1024,640]{1,0:T(8,128)(2,1)} %shard_map.221), channel_id=1, source_target_pairs={{0,16},{16,0},{1,17},{17,1},{2,18},{18,2},{3,19},{19,3},{4,20},{20... | collective-permute-start | bytes 3932168 | tf_op jit(solution)/shard_map/ppermute | solution.py:43
  487.0 33.5 %collective-permute-start.60 = (bf16[640,1024]{1,0:T(8,128)(2,1)}, bf16[640,1024]{1,0:T(8,128)(2,1)}, u32[]{:S(2)}, u32[]{:S(2)}) collective-permute-start(bf16[640,1024]{1,0:T(8,128)(2,1)} %add.326), channel_id=1, source_target_pairs={{4,8},{8,4},{5,9},{9,5},{6,10},{10,6},{7,11},{11,7},{20,24},{24,20... | collective-permute-start | bytes 3932168 | tf_op jit(solution)/shard_map/ppermute | solution.py:131
  489.1 34.8 %collective-permute-start.59 = (bf16[1024,640]{1,0:T(8,128)(2,1)}, bf16[1024,640]{1,0:T(8,128)(2,1)}, u32[]{:S(2)}, u32[]{:S(2)}) collective-permute-start(bf16[1024,640]{1,0:T(8,128)(2,1)} %shard_map.229), channel_id=1, source_target_pairs={{0,4},{12,8},{1,5},{13,9},{2,6},{14,10},{3,7},{15,11},{16,20},{28,... | collective-permute-start | bytes 3932168 | tf_op jit(solution)/shard_map/ppermute | solution.py:129
  493.2 41.9 %collective-permute-start.42 = (bf16[640,512]{1,0:T(8,128)(2,1)}, bf16[640,512]{1,0:T(8,128)(2,1)}, u32[]{:S(2)}, u32[]{:S(2)}) collective-permute-start(bf16[640,512]{1,0:T(8,128)(2,1)} %pad_maximum_fusion.9.refs_0_), channel_id=1, source_target_pairs={{0,16},{16,0},{1,17},{17,1},{2,18},{18,2},{3,19},{19,3},{4,20},{20... | collective-permute-start | bytes 1966088 | tf_op jit(solution)/shard_map/ppermute | solution.py:43
  515.5 36.1 %collective-permute-start.49 = (bf16[512,1024]{1,0:T(8,128)(2,1)}, bf16[512,1024]{1,0:T(8,128)(2,1)}, u32[]{:S(2)}, u32[]{:S(2)}) collective-permute-start(bf16[512,1024]{1,0:T(8,128)(2,1)} %shard_map.222), channel_id=1, source_target_pairs={{0,16},{16,0},{1,17},{17,1},{2,18},{18,2},{3,19},{19,3},{4,20},{20... | collective-permute-start | bytes 3145736 | tf_op jit(solution)/shard_map/ppermute | solution.py:43
  523.8 32.6 %collective-permute-start.62 = (bf16[1024,640]{1,0:T(8,128)(2,1)}, bf16[1024,640]{1,0:T(8,128)(2,1)S(1)}, u32[]{:S(2)}, u32[]{:S(2)}) collective-permute-start(bf16[1024,640]{1,0:T(8,128)(2,1)} %shard_map.230), channel_id=1, source_target_pairs={{0,4},{12,8},{1,5},{13,9},{2,6},{14,10},{3,7},{15,11},{16,20},{28,... | collective-permute-start | bytes 3932168 | tf_op jit(solution)/shard_map/ppermute | solution.py:129
  527.4 42.8 %collective-permute-start.64 = (bf16[640,1024]{1,0:T(8,128)(2,1)S(1)}, bf16[640,1024]{1,0:T(8,128)(2,1)}, u32[]{:S(2)}, u32[]{:S(2)}) collective-permute-start(bf16[640,1024]{1,0:T(8,128)(2,1)S(1)} %copy-done.8), channel_id=1, source_target_pairs={{4,0},{8,12},{5,1},{9,13},{6,2},{10,14},{7,3},{11,15},{20,16},{24,... | collective-permute-start | bytes 3932168 | tf_op jit(solution)/shard_map/ppermute | solution.py:132
  535.1 33.6 %collective-permute-start.63 = (bf16[1024,640]{1,0:T(8,128)(2,1)S(1)}, bf16[1024,640]{1,0:T(8,128)(2,1)S(1)}, u32[]{:S(2)}, u32[]{:S(2)}) collective-permute-start(bf16[1024,640]{1,0:T(8,128)(2,1)S(1)} %add.328), channel_id=1, source_target_pairs={{4,8},{8,4},{5,9},{9,5},{6,10},{10,6},{7,11},{11,7},{20,24},{24,20... | collective-permute-start | bytes 3932168 | tf_op jit(solution)/shard_map/ppermute | solution.py:131
  542.3 92.3 %collective-permute-start.26 = (bf16[128,2048]{1,0:T(8,128)(2,1)}, bf16[128,2048]{1,0:T(8,128)(2,1)}, u32[]{:S(2)}, u32[]{:S(2)}) collective-permute-start(bf16[128,2048]{1,0:T(8,128)(2,1)} %get-tuple-element.67), channel_id=1, source_target_pairs={{0,2},{1,3},{2,0},{3,1},{4,6},{5,7},{6,4},{7,5},{8,10},{9,11},{10,... | collective-permute-start | bytes 1572872 | tf_op jit(solution)/shard_map/ppermute | solution.py:43
  559.7 38.0 %collective-permute-start.66 = (bf16[1024,640]{1,0:T(8,128)(2,1)}, bf16[1024,640]{1,0:T(8,128)(2,1)}, u32[]{:S(2)}, u32[]{:S(2)}) collective-permute-start(bf16[1024,640]{1,0:T(8,128)(2,1)} %add.330), channel_id=1, source_target_pairs={{4,8},{8,4},{5,9},{9,5},{6,10},{10,6},{7,11},{11,7},{20,24},{24,20... | collective-permute-start | bytes 3932168 | tf_op jit(solution)/shard_map/ppermute | solution.py:131
  570.2 23.5 %collective-permute-start.65 = (bf16[512,1024]{1,0:T(8,128)(2,1)}, bf16[512,1024]{1,0:T(8,128)(2,1)S(1)}, u32[]{:S(2)}, u32[]{:S(2)}) collective-permute-start(bf16[512,1024]{1,0:T(8,128)(2,1)} %shard_map.231), channel_id=1, source_target_pairs={{0,4},{12,8},{1,5},{13,9},{2,6},{14,10},{3,7},{15,11},{16,20},{28,... | collective-permute-start | bytes 3145736 | tf_op jit(solution)/shard_map/ppermute | solution.py:129
  571.9 33.7 %collective-permute-start.67 = (bf16[1024,640]{1,0:T(8,128)(2,1)S(1)}, bf16[1024,640]{1,0:T(8,128)(2,1)S(1)}, u32[]{:S(2)}, u32[]{:S(2)}) collective-permute-start(bf16[1024,640]{1,0:T(8,128)(2,1)S(1)} %copy-done.9), channel_id=1, source_target_pairs={{4,0},{8,12},{5,1},{9,13},{6,2},{10,14},{7,3},{11,15},{20,16},{24,... | collective-permute-start | bytes 3932168 | tf_op jit(solution)/shard_map/ppermute | solution.py:132
  577.8 24.3 %collective-permute-start.44 = (f32[2,2048]{1,0:T(2,128)S(1)}, f32[2,2048]{1,0:T(2,128)S(1)}, u32[]{:S(2)}, u32[]{:S(2)}) collective-permute-start(f32[2,2048]{1,0:T(2,128)S(1)} %fusion.37), channel_id=1, source_target_pairs={{0,2},{1,3},{2,0},{3,1},{4,6},{5,7},{6,4},{7,5},{8,10},{9,11},{10,... | collective-permute-start | bytes 49160 | tf_op jit(solution)/shard_map/ppermute | solution.py:43
  599.7 33.5 %collective-permute-start.70 = (bf16[1024,640]{1,0:T(8,128)(2,1)S(1)}, bf16[1024,640]{1,0:T(8,128)(2,1)}, u32[]{:S(2)}, u32[]{:S(2)}) collective-permute-start(bf16[1024,640]{1,0:T(8,128)(2,1)S(1)} %add.331.refs_2_), channel_id=1, source_target_pairs={{4,0},{8,12},{5,1},{9,13},{6,2},{10,14},{7,3},{11,15},{20,16},{24,... | collective-permute-start | bytes 3932168 | tf_op jit(solution)/shard_map/ppermute | solution.py:132
  610.8 25.3 %collective-permute-start.40 = (bf16[128,2048]{1,0:T(8,128)(2,1)}, bf16[128,2048]{1,0:T(8,128)(2,1)}, u32[]{:S(2)}, u32[]{:S(2)}) collective-permute-start(bf16[128,2048]{1,0:T(8,128)(2,1)} %add_convert_fusion.4), channel_id=1, source_target_pairs={{0,2},{1,3},{2,0},{3,1},{4,6},{5,7},{6,4},{7,5},{8,10},{9,11},{10,... | collective-permute-start | bytes 1572872 | tf_op jit(solution)/shard_map/ppermute | solution.py:43
  636.0 47.1 %collective-permute-start.27 = (bf16[256,2048]{1,0:T(8,128)(2,1)S(1)}, bf16[256,2048]{1,0:T(8,128)(2,1)}, u32[]{:S(2)}, u32[]{:S(2)}) collective-permute-start(bf16[256,2048]{1,0:T(8,128)(2,1)S(1)} %pad_maximum_fusion.4.first), channel_id=1, source_target_pairs={{0,1},{1,0},{2,3},{3,2},{4,5},{5,4},{6,7},{7,6},{8,9},{9,8},{10,11... | collective-permute-start | bytes 3145736 | tf_op jit(solution)/shard_map/ppermute | solution.py:43
  637.8 50.1 %collective-permute-start.41 = (bf16[256,2048]{1,0:T(8,128)(2,1)S(1)}, bf16[256,2048]{1,0:T(8,128)(2,1)}, u32[]{:S(2)}, u32[]{:S(2)}) collective-permute-start(bf16[256,2048]{1,0:T(8,128)(2,1)S(1)} %pad_maximum_fusion.7.first), channel_id=1, source_target_pairs={{0,1},{1,0},{2,3},{3,2},{4,5},{5,4},{6,7},{7,6},{8,9},{9,8},{10,11... | collective-permute-start | bytes 3145736 | tf_op jit(solution)/shard_map/ppermute | solution.py:43
  637.9 73.8 %collective-permute-start.76 = (bf16[512,1024]{1,0:T(8,128)(2,1)S(1)}, bf16[512,1024]{1,0:T(8,128)(2,1)}, u32[]{:S(2)}, u32[]{:S(2)}) collective-permute-start(bf16[512,1024]{1,0:T(8,128)(2,1)S(1)} %copy-done.12), channel_id=1, source_target_pairs={{4,0},{8,12},{5,1},{9,13},{6,2},{10,14},{7,3},{11,15},{20,16},{24,... | collective-permute-start | bytes 3145736 | tf_op jit(solution)/shard_map/ppermute | solution.py:132
  653.5 24.6 %collective-permute-start.72 = (bf16[528,640]{1,0:T(8,128)(2,1)}, bf16[528,640]{1,0:T(8,128)(2,1)}, u32[]{:S(2)}, u32[]{:S(2)}) collective-permute-start(bf16[528,640]{1,0:T(8,128)(2,1)} %add.334), channel_id=1, source_target_pairs={{4,8},{8,4},{5,9},{9,5},{6,10},{10,6},{7,11},{11,7},{20,24},{24,20... | collective-permute-start | bytes 2027528 | tf_op jit(solution)/shard_map/ppermute | solution.py:131
  665.2 47.9 %collective-permute-start.75 = (bf16[512,640]{1,0:T(8,128)(2,1)}, bf16[512,640]{1,0:T(8,128)(2,1)}, u32[]{:S(2)}, u32[]{:S(2)}) collective-permute-start(bf16[512,640]{1,0:T(8,128)(2,1)} %add.337), channel_id=1, source_target_pairs={{4,0},{8,12},{5,1},{9,13},{6,2},{10,14},{7,3},{11,15},{20,16},{24,... | collective-permute-start | bytes 1966088 | tf_op jit(solution)/shard_map/ppermute | solution.py:132
  680.4 34.0 %collective-permute-start.73 = (bf16[528,640]{1,0:T(8,128)(2,1)}, bf16[528,640]{1,0:T(8,128)(2,1)}, u32[]{:S(2)}, u32[]{:S(2)}) collective-permute-start(bf16[528,640]{1,0:T(8,128)(2,1)} %add.335), channel_id=1, source_target_pairs={{4,0},{8,12},{5,1},{9,13},{6,2},{10,14},{7,3},{11,15},{20,16},{24,... | collective-permute-start | bytes 2027528 | tf_op jit(solution)/shard_map/ppermute | solution.py:132
  (105 other events, 1029.8 us)
Sparse Core Ops, SparseCore 0:
  83.0 36.3 all-gather.2
  131.6 39.1 all-gather.4

commit v3 on v2

--- a/solution.py
+++ b/solution.py
@@ -69,19 +69,17 @@
     return keep, give.astype(jnp.bfloat16)
 
 
-def scatter_rows(keep, give, *tokens):
+def scatter_rows(keep, give, between=None):
     part = add(keep, over_core(give)).astype(jnp.bfloat16)
     if part.shape[0] == 1:
         keep, give = cut(part[0])
-        if tokens:
-            (give,) = after([give], *tokens)
         return add(keep, over_y(give)), [give]
     left, right = jnp.split(part, 2, axis=2)
     keep_left, give_left = cut(left)
     keep_right, give_right = cut(right, 1)
     from_x, from_y = over_x(give_left), over_y(give_right)
-    if tokens:
-        from_x, from_y = after([from_x, from_y], *tokens)
+    if between:
+        from_x, from_y = after([from_x, from_y], *between([give_left, give_right]))
     left = add(keep_left, from_x)[0]
     right = add(keep_right, from_y)
     keep_left, give_left = cut(left)
@@ -91,6 +89,11 @@
     return jnp.concatenate([left, right], axis=1), [give_left, give_right]
 
 
+def both_cores(rows):
+    first = over_x(rows[: rows.shape[0] // 2])
+    return jnp.concatenate([first, over_core(first)], axis=0)
+
+
 def gather_own(rows, *tokens):
     first = jnp.concatenate([rows, over_y(rows)], axis=0)
     if tokens:
@@ -98,15 +101,17 @@
     return first, over_core(first)
 
 
-def gather_pair(rows, *tokens):
+def gather_pair(rows, early=(), late=()):
     left, right = jnp.split(rows, 2, axis=1)
     left = jnp.stack([left, over_x(left)])
     right = jnp.concatenate([right, over_y(right)], axis=0)
+    if early:
+        left, right = after([left, right], *early)
     left = jnp.concatenate([left, over_y(left)], axis=1)
     right = jnp.stack([right, over_x(right)])
     first = jnp.concatenate([left, right], axis=2)
-    if tokens:
-        (first,) = after([first], *tokens)
+    if late:
+        (first,) = after([first], *late)
     return first, over_core(first)
 
 
@@ -120,12 +125,15 @@
 
 class Line:
     def __init__(self):
-        self.came, self.total, self.done = [], [], []
+        self.piece, self.came, self.total, self.done = [], [], [], []
 
     def put(self, piece):
-        if self.came:
-            earlier = (*self.came[-1:], *self.total[-2:-1], *self.done[-3:-2])
+        k = len(self.came)
+        far = k - 1
+        earlier = [v[i] for v, i in ((self.came, far), (self.total, far - 1), (self.done, far - 2)) if i >= 0]
+        if earlier:
             (piece,) = after([piece], *earlier)
+        self.piece.append(piece)
         self.came.append(lax.ppermute(piece, "ctx", [(0, 1), (3, 2)]))
         inward = piece + self.came[-1]
         self.total.append(inward + lax.ppermute(inward, "ctx", [(1, 2), (2, 1)]))
@@ -586,23 +594,23 @@
     )(order, *halves)
 
 
-def finish_kernel(axis, where, *refs):
-    pieces, out = refs[:-1], refs[-1]
-    for i in range(len(pieces) // 2):
-        total = jnp.where(where[0] != 0, pieces[2 * i][...], pieces[2 * i + 1][...])
-        total = total.astype(jnp.float32)
-        at = pl.ds(pl.multiple_of(where[1 + i], TILE), total.shape[axis])
-        if len(pieces) == 2:
-            out[...] = total
-        elif axis == 0:
-            out[at] = total
+def finish_kernel(axis, where, kept, *refs):
+    out = refs[-1]
+    if len(refs) == 1:
+        out[...] = kept[...].astype(jnp.float32)
+        return
+    came = jnp.where(where[0] != 0, refs[0][...], refs[1][...])
+    for i, piece in enumerate((kept[...], came)):
+        at = pl.ds(pl.multiple_of(where[1 + i], TILE), piece.shape[axis])
+        if axis == 0:
+            out[at] = piece.astype(jnp.float32)
         else:
-            out[:, at] = total
+            out[:, at] = piece.astype(jnp.float32)
 
 
 def finish(where, axis, kept, *came):
     shape = list(kept.shape)
-    shape[axis] += came[1].shape[axis] if len(came) > 1 else 0
+    shape[axis] += came[0].shape[axis] if came else 0
     block = 256 if shape[1 - axis] % 256 == 0 else shape[1 - axis]
 
     def spec(size):
@@ -706,7 +714,7 @@
             jnp.concatenate([gains_there, gain_shards], axis=1),
         )
         qkv_w = (qkv_shard, over_x(qkv_shard))
-        output_w = (output_weight, over_x(output_weight))
+        output_w = (output_weight, over_x(after([output_weight], gains_there)[0]))
         fourth = half // nz
 
         def around(received):
@@ -714,7 +722,8 @@
 
         def columns(weight):
             start = (here_z * fourth, at_theirs)
-            return over_x(lax.dynamic_slice(weight, start, (fourth, big)))
+            piece = lax.dynamic_slice(weight, start, (fourth, big))
+            return over_x(after([piece], gains_there)[0])
 
         gate_fourth, upper_fourth = columns(gate_weight), columns(up_weight)
         gate_own, upper_own = part(gate_weight, at, big, 1), part(up_weight, at, big, 1)
@@ -756,12 +765,12 @@
     q, kv = entry(places, normed_one, cosine, sine, qkv_w)
     q = q.reshape(heads, HD, rows)
     kv = jnp.concatenate([kv] + [shift(kv, "ctx", nz, d) for d in range(1, nz)], axis=0)
+    mixed, lse = attend(count, tiles, q, kv, *masks)
     if paired:
-        gate_fourth, upper_fourth = after([gate_fourth, upper_fourth], kv)
+        gate_fourth, upper_fourth = after([gate_fourth, upper_fourth], lse)
         gate_w = (gate_own, around(gate_fourth))
         upper_w = (upper_own, around(upper_fourth))
 
-    mixed, lse = attend(count, tiles, q, kv, *masks)
     mixed_low = mixed.reshape(query_width, rows).astype(low)
     attn = project(places, [mixed_low], [output_w], 0, 0)
     keep, give = cut(attn[None], 1)
@@ -778,17 +787,17 @@
             for c, t in zip(jnp.split(cotangent, 2), (there, over_core(there)))
         ]
         (normed_own,) = after([normed_own], *upstream, down_w[1], gate_w[1])
-        normed_two = gather_pair(normed_own, upper_w[1])
+        grads = [outer(places, u, down_w) for u in upstream]
+        normed_two = gather_pair(normed_own, [grads[0]], [grads[1], upper_w[1]])
     else:
         normed_two = gather_own(normed_own)
         upstream = jnp.split(cotangent, 2)
+        grads = [outer(places, u, down_w) for u in upstream]
     normed_two = [v.reshape(-1, width) for v in normed_two]
     sets = 2 if paired else 1
 
     def spread(value, dim):
         return lax.psum_scatter(value, "fsdp", scatter_dimension=dim, tiled=True)
-
-    grads = [outer(places, u, down_w) for u in upstream]
 
     def forward(i):
         return middle(places, normed_two[i], grads[i], gate_w, upper_w)
@@ -801,27 +810,53 @@
         return project(places, [hidden[i]], [down_w], 1, 0, spare).reshape(sets, -1, width)
 
     line = Line()
+    scattered, sums = {}, {}
+
+    def scatter(name, piece):
+        scattered[name] = lax.psum_scatter(piece, "ctx", scatter_dimension=0, tiled=True)
+
+    def gather(name, *tokens):
+        piece = scattered[name]
+        if tokens:
+            (piece,) = after([piece], *tokens)
+        sums[name] = lax.all_gather(piece, "ctx", axis=0, tiled=True)
+
     hidden, dgate, dupper = [None, None], [None, None], [None, None]
     if paired:
-        mixed_there, one_there = after([mixed_low, theirs(normed_one)], grads[0])
-        mixed_there, one_there = over_x(mixed_there), over_x(one_there)
-    for i in range(2):
-        hidden[i], dgate[i], dupper[i] = forward(i)
-    if paired:
-        line.put(weigh(places, hidden, 3, big, upstream, 0, half))
-        line.put(weigh(places, normed_two, 0, half, dgate, 3, big))
-        line.put(weigh(places, normed_two, 0, half, dupper, 3, big))
+        hidden[1], dgate[1], dupper[1] = forward(1)
+        (places,) = after([places], hidden[1])
+        grad_give = back(1)
+        (places,) = after([places], grad_give)
+        hidden[0], dgate[0], dupper[0] = forward(0)
+        (places,) = after([places], hidden[0])
+        kept_down = weigh(places, hidden, 3, big, upstream, 0, half)
+        scatter("down", kept_down)
+        (places,) = after([places], kept_down)
+        grad_keep = back(0)
+        kept = {}
+
+        def between(sent):
+            after_sent = after([places], grad_keep, *sent)[0]
+            kept["gate"] = weigh(after_sent, normed_two, 0, half, dgate, 3, big)
+            scatter("gate", kept["gate"])
+            return [kept["gate"], scattered["down"]]
+
+        grad_own, sent = scatter_rows(grad_keep, grad_give, between)
+        (places,) = after([places], kept["gate"], *sent)
+        kept_upper = weigh(places, normed_two, 0, half, dupper, 3, big)
+        scatter("upper", kept_upper)
+        (places,) = after([places], kept_upper)
+        (grad_own,) = after([grad_own], kept_upper)
     else:
+        for i in range(2):
+            hidden[i], dgate[i], dupper[i] = forward(i)
         weight_grad = lambda lefts, rights: sum(
             dot(left, right, 0, 0) for left, right in zip(lefts, rights)
         ).astype(low)
-        line.put(spread(weight_grad(hidden, upstream), 1))
-        line.put(spread(weight_grad(normed_two, dgate), 0))
-        line.put(spread(weight_grad(normed_two, dupper), 0))
-    given = back(1)
-    if paired:
-        (places,) = after([places], given, mixed_there, one_there)
-    grad_own, sent = scatter_rows(back(0), given)
+        scatter("down", spread(weight_grad(hidden, upstream), 1))
+        scatter("gate", spread(weight_grad(normed_two, dgate), 0))
+        scatter("upper", spread(weight_grad(normed_two, dupper), 0))
+        grad_own, _ = scatter_rows(back(0), back(1))
     grad_one = cotangent[:block].astype(high) + norm_back(
         one_own, scale_two, gain_two, grad_own
     )
@@ -829,32 +864,38 @@
     gain_two_sum = jnp.sum(grad_own * one_own * scale_two, axis=0)
     grad_attn = gather_own(grad_one_low)
     if paired:
-        given = weigh(places, hidden, 4, small, upstream, 1, half)
-        (given,) = after([given], *sent)
-        came_down = over_x(given)
-        line.put(came_down)
-        given = weigh(places, normed_two, 1, half, dgate, 4, small)
-        (given,) = after([given], came_down)
-        came_gate = over_x(given)
-        line.put(came_gate)
-        given = weigh(places, normed_two, 1, half, dupper, 4, small)
-        (given,) = after([given], came_gate)
-        came_upper = over_x(given)
-        line.put(came_upper)
+        (places,) = after([places], grad_one_low)
+        given_down = weigh(places, hidden, 4, small, upstream, 1, half)
+        (places,) = after([places], given_down)
+        given_gate = weigh(places, normed_two, 1, half, dgate, 4, small)
+        (places,) = after([places], given_gate)
+        line.put(over_x(given_down))
     grad_mixed = collect(places, grad_attn, output_w).reshape(heads, HD, rows)
     grad_attn = jnp.concatenate(grad_attn, axis=0)
 
+    if paired:
+        (grad_mixed,) = after([grad_mixed], line.piece[0], scattered["gate"])
     dq, dkv = attend_back(count, tiles, q, kv, *masks, mixed, lse, grad_mixed)
     per = rows // TILE
     dkv_own = dkv[:per]
     moved = [dkv[d * per : (d + 1) * per].astype(low) for d in range(1, nz)]
     received = [shift(m, "ctx", nz, nz - 1 - d) for d, m in enumerate(moved)]
     if paired:
-        (attn_there,) = after([theirs(grad_attn)], came_upper)
-        output_grad = dot(mixed_low, mine(grad_attn), 1, 0) + dot(
-            mixed_there, over_x(attn_there), 1, 0
+        (places,) = after([places], *moved)
+        given_upper = weigh(places, normed_two, 1, half, dupper, 4, small)
+        (places,) = after([places], given_upper)
+        came_gate = over_x(given_gate)
+        line.put(came_gate)
+        gather("down")
+        received = after(received, given_upper, line.piece[1], scattered["upper"], sums["down"])
+        gather("gate", scattered["upper"])
+        came_upper = over_x(given_upper)
+        line.put(came_upper)
+        attn_there, one_there, mixed_there = after(
+            [theirs(grad_attn), theirs(normed_one), mixed_low], came_upper
         )
-        line.put(output_grad.astype(low))
+        attn_there, one_there = both_cores(attn_there), both_cores(one_there)
+        mixed_there = over_x(mixed_there)
     else:
         line.put(spread(dot(mixed_low, grad_attn, 1, 0).astype(low), 1))
     for m in received:
@@ -864,19 +905,38 @@
     dk = turn(dkv_own[None, :HD], cosine, -sine)[0]
     dqkv = jnp.concatenate([dq, dk, dkv_own[HD:]], axis=0).astype(low)
     first = project(places, [dqkv], [qkv_w], 0, 1)
+    (places,) = after([places], first)
     keep, give = cut(first[None], 1)
-    first_own, _ = scatter_rows(keep, give)
+    first_own, sent = scatter_rows(keep, give)
     if paired:
-        qkv_grad = (
-            dot(mine(normed_one), dqkv, 0, 1) + dot(one_there, over_x(dqkv), 0, 1)
-        ).astype(low)
+        (first_own,) = after([first_own], line.piece[2], sums["gate"])
+        gather("upper", *sent)
+        (places,) = after([places], *sent)
     else:
         qkv_grad = spread(dot(normed_one, dqkv, 0, 1).astype(low), 0)
     scale_own = scale_one[:block]
     inputs_own = inputs[:block]
     gain_one_sum = jnp.sum(first_own * inputs_own * scale_own, axis=0)
     input_own = grad_one + norm_back(inputs_own, scale_own, gain_one, first_own)
-    input_grad = place(order, gather_own(input_own.astype(low)), high)
+    input_low = input_own.astype(low)
+    if paired:
+        attn_there, mixed_there, one_there = after(
+            [attn_there, mixed_there, one_there], input_low
+        )
+        output_grad = dot(mixed_low, mine(grad_attn), 1, 0) + dot(
+            mixed_there, attn_there, 1, 0
+        )
+        line.put(output_grad.astype(low))
+        (dqkv_there,) = after([over_x(dqkv)], input_low, line.piece[2])
+        qkv_grad = (
+            dot(mine(normed_one), dqkv, 0, 1) + dot(one_there, dqkv_there, 0, 1)
+        ).astype(low)
+    if not paired:
+        gather("down")
+        gather("gate")
+        gather("upper")
+    late = [sums["upper"]] if paired else []
+    input_grad = place(order, gather_own(input_low, *late), high)
     ffn_own, _ = scatter_rows(ffn(0), ffn(1))
     activations = place(order, gather_own((one_own + ffn_own).astype(low)), low)
 
@@ -902,8 +962,8 @@
         return jnp.where(inner != 0, line.total[i], line.done[i])
 
     down_grad, gate_grad, upper_grad = (
-        finish(where, axis, *(v for k in ((i, i + 3) if paired else (i,)) for v in (line.total[k], line.done[k])))
-        for i, axis in ((0, 0), (1, 1), (2, 1))
+        finish(where, axis, sums[name], *([line.total[i], line.done[i]] if paired else []))
+        for i, (name, axis) in enumerate((("down", 0), ("gate", 1), ("upper", 1)))
     )
     output_grad = whole(-3).astype(high)
     qkv_grad = jnp.concatenate([whole(-2), whole(-1)[:-extra]], axis=0).astype(high)

time: 732 us -> 705 us (0.963)
  starting transfers between devices: 134 us -> 109 us
  waiting for transfers between devices: 224 us -> 205 us
  local copies, waits for them, and re-layouts: 45.7 us -> 55.3 us
    ppermute x9 -> x6, waiting for transfers between devices: 32.1 us -> 78.1 us  [put(): self.total.append(inward + lax.ppermute(inward, 'ctx', [(1, 2), (2, 1)]))]
    ppermute x6, waiting for transfers between devices: 32.2 us -> 3.99 us  [shift(): return lax.ppermute(value, axis, pairs)]
    ppermute x9 -> x6, waiting for transfers between devices: 30 us -> 4.2 us  [put(): self.came.append(lax.ppermute(piece, 'ctx', [(0, 1), (3, 2)]))]
    ppermute x44 -> x46, waiting for transfers between devices: 119 us -> 99.8 us  [swap(): return lax.ppermute(value, axis, pairs)]
    ppermute x9 -> x6, starting transfers between devices: 35 us -> 18 us  [put(): self.done.append(lax.ppermute(self.total[-1], 'ctx', [(1, 0), (2, 3)]))]
    reduce_scatter x0 -> x3, waiting for transfers between devices: none -> 15.4 us  [scatter(): lax.psum_scatter(piece, 'ctx', scatter_dimension=0, tiled=True)]
    add x9 -> x6, other arithmetic: 20.7 us -> 11.9 us  [put(): inward = piece + self.came[-1]]
    ppermute x9 -> x6, starting transfers between devices: 24.6 us -> 16.9 us  [put(): self.total.append(inward + lax.ppermute(inward, 'ctx', [(1, 2), (2, 1)]))]
  transfers between devices with their start and end apart: 79 -> 78, of which waited for: 34 -> 29; matrix products, arithmetic and copies ran while one was open for 19% -> 22% of each run, Pallas kernels for 27% -> 24%
where the time goes in v3:
time: 705 us; the launch traced here: 695 us
  waiting for transfers between devices  205 us (29%)
  Pallas kernels  198 us (28%)
  starting transfers between devices  109 us (15%)
  other arithmetic  103 us (15%)
  local copies, waits for them, and re-layouts  55.3 us (8%)
  between operations  16 us (2%)
  matrix products  9.81 us (1%)
    ppermute x46, waiting for transfers between devices, swap(): return lax.ppermute(value, axis, pairs)  99.8 us
    ppermute x6, waiting for transfers between devices, put(): self.total.append(inward + lax.ppermute(inward, 'ctx', [(1, 2), (2, 1)]))  78.1 us
    pallas_call x6, Pallas kernels, project(): pl.pallas_call(functools.partial(project_kernel, parts, factors, steps, o...  41.9 us
    pallas_call x6, Pallas kernels, weigh(): pl.pallas_call(functools.partial(weigh_kernel, parts, at_left, at_right,...  38.7 us
    ppermute x46, starting transfers between devices, swap(): return lax.ppermute(value, axis, pairs)  38.4 us
    pallas_call x1, Pallas kernels, attend_back(): pl.pallas_call(functools.partial(attend_back_kernel, heads), grid_spec=pl...  33.8 us
    ppermute x6, starting transfers between devices, shift(): return lax.ppermute(value, axis, pairs)  26.4 us
    pallas_call x2, Pallas kernels, middle(): pl.pallas_call(functools.partial(middle_kernel, parts), grid_spec=pltpu.P...  18.5 us
  transfers between devices with their start and end apart: 78, of which 29 were waited for; matrix products, arithmetic and copies ran while one was open for 22% of the time, Pallas kernels for 24%

profile of v3, /device:TPU:8, one launch (start us, length us, event | category | flops | bytes accessed | tf_op | source)
XLA Modules:
  0.0 694.6 jit_solution(3925080538493155644)
XLA Ops:
  26.0 4.1 multiply_convert_fusion.rows
  30.1 13.4 %collective-permute-done.1.refs_1_.refs_2_ = bf16[1024,640]{1,0:T(8,128)(2,1)} collective-permute-done((bf16[1024,640]{1,0:T(8,128)(2,1)S(1)}, bf16[1024,640]{1,0:T(8,128)(2,1)}, u32[]{:S(2)}, u32[]{:S(2)}) %collective-permute-start.1) | collective-permute-done | bytes 1310752 | tf_op jit(solution)/shard_map/ppermute | solution.py:43
  43.5 8.0 %shard_map.195 = (bf16[512,512]{1,0:T(8,128)(2,1)}, bf16[4,128,128]{2,1,0:T(8,128)(2,1)}) custom-call(s32[5]{0:T(128)} %stack.87.places.refs_0_, bf16[512,2048]{1,0:T(8,128)(2,1)} %multiply_convert_fusion.rows, f32[32,512]{1,0:T(8,128)} %get-tuple-element.117.cosine, f32[32,512]{1,0:T(8,128)} %get-tuple-element.116.sine, bf16[1024,640]{1,0:T(8,128)(2,1)} %copy-done.10, ...), custom_call_target="tpu_custom_call" | custom-call | flops 1000000 | bytes 100000 | tf_op jit(solution)/shard_map/pallas_call | solution.py:545
  68.4 11.8 %shard_map.196 = (f32[8,64,512]{2,1,0:T(8,128)}, f32[8,512]{1,0:T(8,128)}) custom-call(s32[4]{0:T(128)} %convert_reduce_fusion.count, s32[4,16]{1,0:T(4,128)} %select_reduce_fusion.tiles, bf16[8,64,512]{2,1,0:T(8,128)(2,1)} %bitcast.127, bf16[16,128,128]{2,1,0:T(8,128)(2,1)} %copy-done.59, s32[1,512]{1,0:T(1,128)} %copy-done.85, s32[1,512]{1,0:T(1,128)} %copy-done.86, ...), custom_call_target="tpu_custom_call" | custom-call | flops 1000000 | bytes 100000 | tf_op jit(solution)/shard_map/pallas_call | solution.py:184
  85.6 5.7 shard_map.198
  95.2 4.0 constant_dynamic-slice_fusion.8
  102.2 5.9 collective-permute-done.9
  121.4 6.9 collective-permute-done.7
  131.0 4.9 collective-permute-done.11.refs_3_.refs_1_.refs_2_
  139.3 6.4 shard_map.203.refs_2_.grads
  150.3 6.3 shard_map.205.refs_1_.grads
  156.6 3.7 collective-permute-done.17
  168.7 9.3 %shard_map.207 = (bf16[512,768]{1,0:T(8,128)(2,1)}, bf16[512,768]{1,0:T(8,128)(2,1)}, bf16[512,768]{1,0:T(8,128)(2,1)}) custom-call(s32[5]{0:T(128)} %stack.87.places.refs_0_, bf16[512,2048]{1,0:T(8,128)(2,1)} %bitcast.105, f32[512,768]{1,0:T(8,128)} %shard_map.205.refs_1_.grads, bf16[1024,768]{1,0:T(8,128)(2,1)} %constant_dynamic-slice_fusion.7.refs_0_.refs_2_, ...), custom_call_target="tpu_custom_call" | custom-call | flops 1000000 | bytes 16605000 | tf_op jit(solution)/shard_map/pallas_call | solution.py:355
  178.0 8.6 %shard_map.209 = bf16[512,2048]{1,0:T(8,128)(2,1)} custom-call(s32[5]{0:T(128)} %shard_map.208.places.refs_0_, bf16[512,768]{1,0:T(8,128)(2,1)} %get-tuple-element.46.refs_0_.refs_3_, bf16[512,768]{1,0:T(8,128)(2,1)} %get-tuple-element.47.refs_1_.refs_3_, bf16[1024,768]{1,0:T(8,128)(2,1)} %constant_dynamic-slice_fusion.7.refs_0_.refs_2_, ...), custom_call_target="tpu_custom_call" | custom-call | flops 1000000 | bytes 11070000 | tf_op jit(solution)/shard_map/pallas_call | solution.py:406
  186.6 9.2 %shard_map.211 = (bf16[512,768]{1,0:T(8,128)(2,1)}, bf16[512,768]{1,0:T(8,128)(2,1)}, bf16[512,768]{1,0:T(8,128)(2,1)}) custom-call(s32[5]{0:T(128)} %shard_map.210.places.refs_0_, bf16[512,2048]{1,0:T(8,128)(2,1)} %bitcast.100, f32[512,768]{1,0:T(8,128)} %shard_map.203.refs_2_.grads, bf16[1024,768]{1,0:T(8,128)(2,1)} %constant_dynamic-slice_fusion.7.refs_0_.refs_2_, ...), custom_call_target="tpu_custom_call" | custom-call | flops 1000000 | bytes 16605000 | tf_op jit(solution)/shard_map/pallas_call | solution.py:355
  195.8 6.7 shard_map.213.refs_1_
  204.0 8.6 %shard_map.215 = bf16[512,2048]{1,0:T(8,128)(2,1)} custom-call(s32[5]{0:T(128)} %shard_map.214.places.refs_0_, bf16[512,768]{1,0:T(8,128)(2,1)} %get-tuple-element.49.refs_0_.refs_2_, bf16[512,768]{1,0:T(8,128)(2,1)} %get-tuple-element.50.refs_1_.refs_2_, bf16[1024,768]{1,0:T(8,128)(2,1)} %constant_dynamic-slice_fusion.7.refs_0_.refs_2_, ...), custom_call_target="tpu_custom_call" | custom-call | flops 1000000 | bytes 11070000 | tf_op jit(solution)/shard_map/pallas_call | solution.py:406
  217.3 6.1 shard_map.217.refs_2_.refs_1_
  223.4 15.4 %reduce-scatter.4.cloned.1.call-done.refs_3_ = bf16[192,1024]{1,0:T(8,128)(2,1)} async-done(((bf16[768,1024]{1,0:T(8,128)(2,1)}), bf16[192,1024]{1,0:T(8,128)(2,1)}) %reduce-scatter.4.cloned.1.call-update) | async-done | bytes 393232 | tf_op jit(solution)/shard_map/reduce_scatter | solution.py:816
  242.1 10.2 %collective-permute-done.20.refs_0_ = bf16[1,256,1024]{2,1,0:T(8,128)(2,1)} collective-permute-done((bf16[1,256,1024]{2,1,0:T(8,128)(2,1)}, bf16[1,256,1024]{2,1,0:T(8,128)(2,1)}, u32[]{:S(2)}, u32[]{:S(2)}) %collective-permute-start.20) | collective-permute-done | bytes 524320 | tf_op jit(solution)/shard_map/ppermute | solution.py:43
  259.2 6.2 shard_map.220.refs_1_
  273.2 7.6 %shard_map.224.refs_1_ = bf16[640,1024]{1,0:T(8,128)(2,1)} custom-call(s32[5]{0:T(128)} %shard_map.223.places.refs_0_, bf16[512,768]{1,0:T(8,128)(2,1)} %get-tuple-element.48.refs_1_.refs_0_, bf16[512,768]{1,0:T(8,128)(2,1)} %get-tuple-element.45.refs_1_.refs_0_, bf16[512,2048]{1,0:T(8,128)(2,1)} %pad_maximum_fusion.refs_1_.upstream.refs_2_, ...), custom_call_target="tpu_custom_call" | custom-call | flops 1000000 | bytes 11070000 | tf_op jit(solution)/shard_map/pallas_call | solution.py:469
  284.7 6.1 shard_map.226.refs_1_
  292.3 20.5 %collective-permute-done.26.refs_1_ = bf16[640,1024]{1,0:T(8,128)(2,1)S(1)} collective-permute-done((bf16[640,1024]{1,0:T(8,128)(2,1)}, bf16[640,1024]{1,0:T(8,128)(2,1)S(1)}, u32[]{:S(2)}, u32[]{:S(2)}) %collective-permute-start.26) | collective-permute-done | bytes 1310752 | tf_op jit(solution)/shard_map/ppermute | solution.py:43
  314.1 4.8 shard_map.228
  318.9 33.8 %shard_map.230 = (f32[8,64,512]{2,1,0:T(8,128)}, f32[16,128,128]{2,1,0:T(8,128)}) custom-call(s32[4]{0:T(128)} %convert_reduce_fusion.count, s32[4,16]{1,0:T(4,128)} %select_reduce_fusion.tiles, bf16[8,64,512]{2,1,0:T(8,128)(2,1)} %bitcast.128, bf16[16,128,128]{2,1,0:T(8,128)(2,1)} %copy-done.59, s32[1,512]{1,0:T(1,128)} %copy-done.85, s32[1,512]{1,0:T(1,128)} %copy-done.86, ...), custom_call_target="tpu_custom_call" | custom-call | flops 1000000 | bytes 44280000 | tf_op jit(solution)/shard_map/pallas_call | solution.py:251
  354.9 18.8 %collective-permute-start.28 = (bf16[4,128,128]{2,1,0:T(8,128)(2,1)}, bf16[4,128,128]{2,1,0:T(8,128)(2,1)}, u32[]{:S(2)}, u32[]{:S(2)}) collective-permute-start(bf16[4,128,128]{2,1,0:T(8,128)(2,1)} %get-tuple-element.90.refs_2_), channel_id=1, source_target_pairs={{0,8},{4,12},{8,0},{12,4},{1,9},{5,13},{9,1},{13,5},{2,10},{6,14},... | collective-permute-start | bytes 393224 | tf_op jit(solution)/shard_map/ppermute | solution.py:48
  376.9 6.0 shard_map.232.refs_1_.refs_3_
  386.5 6.2 shard_map.236.refs_1_
  401.0 8.4 %collective-permute-done.41.refs_0_.refs_3_ = bf16[1024,640]{1,0:T(8,128)(2,1)} collective-permute-done((bf16[1024,640]{1,0:T(8,128)(2,1)}, bf16[1024,640]{1,0:T(8,128)(2,1)}, u32[]{:S(2)}, u32[]{:S(2)}) %collective-permute-start.41) | collective-permute-done | bytes 1310752 | tf_op jit(solution)/shard_map/ppermute | solution.py:43
  420.8 3.6 collective-permute-done.46
  424.4 5.6 collective-permute-done.49
  438.8 20.3 %collective-permute-done.43 = bf16[640,1024]{1,0:T(8,128)(2,1)} collective-permute-done((bf16[640,1024]{1,0:T(8,128)(2,1)}, bf16[640,1024]{1,0:T(8,128)(2,1)}, u32[]{:S(2)}, u32[]{:S(2)}) %collective-permute-start.43) | collective-permute-done | bytes 1310752 | tf_op jit(solution)/shard_map/ppermute | solution.py:139
  467.7 6.4 shard_map.239
  474.0 6.5 shard_map.240
  510.9 18.2 %collective-permute-done.56 = bf16[1024,640]{1,0:T(8,128)(2,1)} collective-permute-done((bf16[1024,640]{1,0:T(8,128)(2,1)}, bf16[1024,640]{1,0:T(8,128)(2,1)}, u32[]{:S(2)}, u32[]{:S(2)}) %collective-permute-start.56) | collective-permute-done | bytes 1310752 | tf_op jit(solution)/shard_map/ppermute | solution.py:139
  545.5 10.1 %collective-permute-done.34 = bf16[1,256,1024]{2,1,0:T(8,128)(2,1)S(1)} collective-permute-done((bf16[1,256,1024]{2,1,0:T(8,128)(2,1)S(1)}, bf16[1,256,1024]{2,1,0:T(8,128)(2,1)S(1)}, u32[]{:S(2)}, u32[]{:S(2)}) %collective-permute-start.34) | collective-permute-done | bytes 524320 | tf_op jit(solution)/shard_map/ppermute | solution.py:43
  564.7 5.8 collective-permute-done.59
  586.3 13.0 %collective-permute-done.62 = bf16[512,1024]{1,0:T(8,128)(2,1)} collective-permute-done((bf16[512,1024]{1,0:T(8,128)(2,1)}, bf16[512,1024]{1,0:T(8,128)(2,1)}, u32[]{:S(2)}, u32[]{:S(2)}) %collective-permute-start.62) | collective-permute-done | bytes 1048608 | tf_op jit(solution)/shard_map/ppermute | solution.py:139
  610.4 6.4 collective-permute-start.69
  623.6 3.6 collective-permute-start.65
  627.2 10.3 %collective-permute-done.67 = bf16[512,640]{1,0:T(8,128)(2,1)S(1)} collective-permute-done((bf16[512,640]{1,0:T(8,128)(2,1)S(1)}, bf16[512,640]{1,0:T(8,128)(2,1)S(1)}, u32[]{:S(2)}, u32[]{:S(2)}) %collective-permute-start.67) | collective-permute-done | bytes 655392 | tf_op jit(solution)/shard_map/ppermute | solution.py:139
  640.5 10.5 %collective-permute-done.65 = bf16[528,640]{1,0:T(8,128)(2,1)} collective-permute-done((bf16[528,640]{1,0:T(8,128)(2,1)S(1)}, bf16[528,640]{1,0:T(8,128)(2,1)}, u32[]{:S(2)}, u32[]{:S(2)}) %collective-permute-start.65) | collective-permute-done | bytes 675872 | tf_op jit(solution)/shard_map/ppermute | solution.py:139
  655.2 5.8 shard_map.256
  661.0 5.8 shard_map.254
  666.8 5.2 shard_map.247
  672.0 5.8 shard_map.255
  677.8 4.8 shard_map.241
  (518 shorter events, 257.6 us)
Async XLA Ops:
  7.2 128.7 %all-gather.6.cloned.1.call-start = ((), (), s32[]{:S(2)}) async-start(), calls=%async_computation.3 | async-start | bytes 1966080 | tf_op jit(solution)/shard_map/all_gather | solution.py:721
  11.6 31.9 %collective-permute-start.1 = (bf16[1024,640]{1,0:T(8,128)(2,1)S(1)}, bf16[1024,640]{1,0:T(8,128)(2,1)}, u32[]{:S(2)}, u32[]{:S(2)}) collective-permute-start(bf16[1024,640]{1,0:T(8,128)(2,1)S(1)} %constant_dynamic-update-slice_fusion.refs_0_.refs_1_), channel_id=1, source_target_pairs={{0,16},{16,0},{1,17},{17,1},{2,18},{18,2},{3,19},{19,3},{4,20},{20... | collective-permute-start | bytes 3932168 | tf_op jit(solution)/shard_map/ppermute | solution.py:43
  23.6 62.0 %collective-permute-start.5 = (bf16[512,1024]{1,0:T(8,128)(2,1)}, bf16[512,1024]{1,0:T(8,128)(2,1)}, u32[]{:S(2)}, u32[]{:S(2)}) collective-permute-start(bf16[512,1024]{1,0:T(8,128)(2,1)} %shard_map.197), channel_id=1, source_target_pairs={{0,16},{16,0},{1,17},{17,1},{2,18},{18,2},{3,19},{19,3},{4,20},{20... | collective-permute-start | bytes 3145736 | tf_op jit(solution)/shard_map/ppermute | solution.py:43
  57.9 24.8 %collective-permute-start.13 = (bf16[256,768]{1,0:T(8,128)(2,1)}, bf16[256,768]{1,0:T(8,128)(2,1)S(1)}, u32[]{:S(2)}, u32[]{:S(2)}) collective-permute-start(bf16[256,768]{1,0:T(8,128)(2,1)} %shard_map.200), channel_id=1, source_target_pairs={{0,16},{16,0},{1,17},{17,1},{2,18},{18,2},{3,19},{19,3},{4,20},{20... | collective-permute-start | bytes 1179656 | tf_op jit(solution)/shard_map/ppermute | solution.py:43
  65.4 28.3 %collective-permute-start.8 = (bf16[128,2048]{1,0:T(8,128)(2,1)S(1)}, bf16[128,2048]{1,0:T(8,128)(2,1)S(1)}, u32[]{:S(2)}, u32[]{:S(2)}) collective-permute-start(bf16[128,2048]{1,0:T(8,128)(2,1)S(1)} %copy-done.43), channel_id=1, source_target_pairs={{0,16},{16,0},{1,17},{17,1},{2,18},{18,2},{3,19},{19,3},{4,20},{20... | collective-permute-start | bytes 1572872 | tf_op jit(solution)/shard_map/ppermute | solution.py:43
  83.5 79.5 %all-gather.8.cloned.1.call-start = ((), (), s32[]{:S(2)}) async-start(), calls=%async_computation.4 | async-start | bytes 1966080 | tf_op jit(solution)/shard_map/all_gather | solution.py:721
  99.2 36.7 %collective-permute-start.11 = (bf16[768,1024]{1,0:T(8,128)(2,1)}, bf16[768,1024]{1,0:T(8,128)(2,1)S(1)}, u32[]{:S(2)}, u32[]{:S(2)}) collective-permute-start(bf16[768,1024]{1,0:T(8,128)(2,1)} %get-tuple-element.76), channel_id=1, source_target_pairs={{0,16},{16,0},{1,17},{17,1},{2,18},{18,2},{3,19},{19,3},{4,20},{20... | collective-permute-start | bytes 4718600 | tf_op jit(solution)/shard_map/ppermute | solution.py:43
  117.9 120.9 %reduce-scatter.4.cloned.1.call-start = ((), (), s32[]{:S(2)}) async-start(), calls=%async_computation.5 | async-start | bytes 1966080 | tf_op jit(solution)/shard_map/reduce_scatter | solution.py:816
  202.5 116.3 %reduce-scatter.6.cloned.1.call-start = ((), (), s32[]{:S(2)}) async-start(), calls=%async_computation.6 | async-start | bytes 1966080 | tf_op jit(solution)/shard_map/reduce_scatter | solution.py:816
  223.4 159.8 %all-gather.10.cloned.1.call-start = ((), (), s32[]{:S(2)}) async-start(), calls=%async_computation.8 | async-start | bytes 1966080 | tf_op jit(solution)/shard_map/all_gather | solution.py:822
  238.8 144.4 %reduce-scatter.8.cloned.1.call-start = ((), (), s32[]{:S(2)}) async-start(), calls=%async_computation.7 | async-start | bytes 1966080 | tf_op jit(solution)/shard_map/reduce_scatter | solution.py:816
  280.8 31.9 %collective-permute-start.26 = (bf16[640,1024]{1,0:T(8,128)(2,1)}, bf16[640,1024]{1,0:T(8,128)(2,1)S(1)}, u32[]{:S(2)}, u32[]{:S(2)}) collective-permute-start(bf16[640,1024]{1,0:T(8,128)(2,1)} %shard_map.224.refs_1_), channel_id=1, source_target_pairs={{0,16},{16,0},{1,17},{17,1},{2,18},{18,2},{3,19},{19,3},{4,20},{20... | collective-permute-start | bytes 3932168 | tf_op jit(solution)/shard_map/ppermute | solution.py:43
  284.7 29.3 %collective-permute-start.25 = (bf16[256,2048]{1,0:T(8,128)(2,1)}, bf16[256,2048]{1,0:T(8,128)(2,1)}, u32[]{:S(2)}, u32[]{:S(2)}) collective-permute-start(bf16[256,2048]{1,0:T(8,128)(2,1)} %pad_maximum_fusion.5.refs_0_), channel_id=1, source_target_pairs={{0,1},{1,0},{2,3},{3,2},{4,5},{5,4},{6,7},{7,6},{8,9},{9,8},{10,11... | collective-permute-start | bytes 3145736 | tf_op jit(solution)/shard_map/ppermute | solution.py:43
  290.8 92.1 %collective-permute-start.30 = (bf16[1024,640]{1,0:T(8,128)(2,1)}, bf16[1024,640]{1,0:T(8,128)(2,1)}, u32[]{:S(2)}, u32[]{:S(2)}) collective-permute-start(bf16[1024,640]{1,0:T(8,128)(2,1)} %shard_map.226.refs_1_), channel_id=1, source_target_pairs={{0,16},{16,0},{1,17},{17,1},{2,18},{18,2},{3,19},{19,3},{4,20},{20... | collective-permute-start | bytes 3932168 | tf_op jit(solution)/shard_map/ppermute | solution.py:43
  312.7 70.3 %collective-permute-start.31 = (bf16[640,1024]{1,0:T(8,128)(2,1)S(1)}, bf16[640,1024]{1,0:T(8,128)(2,1)}, u32[]{:S(2)}, u32[]{:S(2)}) collective-permute-start(bf16[640,1024]{1,0:T(8,128)(2,1)S(1)} %collective-permute-done.26.refs_1_), channel_id=1, source_target_pairs={{0,4},{12,8},{1,5},{13,9},{2,6},{14,10},{3,7},{15,11},{16,20},{28,... | collective-permute-start | bytes 3932168 | tf_op jit(solution)/shard_map/ppermute | solution.py:137
  318.8 172.2 %all-gather.12.cloned.1.call-start = ((), (), s32[]{:S(2)}) async-start(), calls=%async_computation.9 | async-start | bytes 1966080 | tf_op jit(solution)/shard_map/all_gather | solution.py:822
  354.9 28.2 %collective-permute-start.27 = (bf16[4,128,128]{2,1,0:T(8,128)(2,1)}, bf16[4,128,128]{2,1,0:T(8,128)(2,1)S(1)}, u32[]{:S(2)}, u32[]{:S(2)}) collective-permute-start(bf16[4,128,128]{2,1,0:T(8,128)(2,1)} %get-tuple-element.91.refs_1_), channel_id=1, source_target_pairs={{0,12},{4,0},{8,4},{12,8},{1,13},{5,1},{9,5},{13,9},{2,14},{6,2},{... | collective-permute-start | bytes 393224 | tf_op jit(solution)/shard_map/ppermute | solution.py:48
  354.9 28.2 %collective-permute-start.28 = (bf16[4,128,128]{2,1,0:T(8,128)(2,1)}, bf16[4,128,128]{2,1,0:T(8,128)(2,1)}, u32[]{:S(2)}, u32[]{:S(2)}) collective-permute-start(bf16[4,128,128]{2,1,0:T(8,128)(2,1)} %get-tuple-element.90.refs_2_), channel_id=1, source_target_pairs={{0,8},{4,12},{8,0},{12,4},{1,9},{5,13},{9,1},{13,5},{2,10},{6,14},... | collective-permute-start | bytes 393224 | tf_op jit(solution)/shard_map/ppermute | solution.py:48
  383.0 26.4 %collective-permute-start.41 = (bf16[1024,640]{1,0:T(8,128)(2,1)}, bf16[1024,640]{1,0:T(8,128)(2,1)}, u32[]{:S(2)}, u32[]{:S(2)}) collective-permute-start(bf16[1024,640]{1,0:T(8,128)(2,1)} %shard_map.232.refs_1_.refs_3_), channel_id=1, source_target_pairs={{0,16},{16,0},{1,17},{17,1},{2,18},{18,2},{3,19},{19,3},{4,20},{20... | collective-permute-start | bytes 3932168 | tf_op jit(solution)/shard_map/ppermute | solution.py:43
  395.1 34.9 %collective-permute-start.32 = (bf16[1,256,2048]{2,1,0:T(8,128)(2,1)}, bf16[1,256,2048]{2,1,0:T(8,128)(2,1)}, u32[]{:S(2)}, u32[]{:S(2)}) collective-permute-start(bf16[1,256,2048]{2,1,0:T(8,128)(2,1)} %split.147), channel_id=1, source_target_pairs={{0,1},{1,0},{2,3},{3,2},{4,5},{5,4},{6,7},{7,6},{8,9},{9,8},{10,11... | collective-permute-start | bytes 3145736 | tf_op jit(solution)/shard_map/ppermute | solution.py:43
  395.2 213.3 %all-gather.14.cloned.1.call-start = ((), (), s32[]{:S(2)}) async-start(), calls=%async_computation.10 | async-start | bytes 1966080 | tf_op jit(solution)/shard_map/all_gather | solution.py:822
  413.7 50.3 %collective-permute-start.42 = (bf16[1024,640]{1,0:T(8,128)(2,1)}, bf16[1024,640]{1,0:T(8,128)(2,1)}, u32[]{:S(2)}, u32[]{:S(2)}) collective-permute-start(bf16[1024,640]{1,0:T(8,128)(2,1)} %shard_map.234.refs_4_), channel_id=1, source_target_pairs={{0,4},{12,8},{1,5},{13,9},{2,6},{14,10},{3,7},{15,11},{16,20},{28,... | collective-permute-start | bytes 3932168 | tf_op jit(solution)/shard_map/ppermute | solution.py:137
  417.9 41.2 %collective-permute-start.43 = (bf16[640,1024]{1,0:T(8,128)(2,1)}, bf16[640,1024]{1,0:T(8,128)(2,1)}, u32[]{:S(2)}, u32[]{:S(2)}) collective-permute-start(bf16[640,1024]{1,0:T(8,128)(2,1)} %add.300), channel_id=1, source_target_pairs={{4,8},{8,4},{5,9},{9,5},{6,10},{10,6},{7,11},{11,7},{20,24},{24,20... | collective-permute-start | bytes 3932168 | tf_op jit(solution)/shard_map/ppermute | solution.py:139
  424.4 56.1 %collective-permute-start.47 = (bf16[256,1024]{1,0:T(8,128)(2,1)}, bf16[256,1024]{1,0:T(8,128)(2,1)}, u32[]{:S(2)}, u32[]{:S(2)}) collective-permute-start(bf16[256,1024]{1,0:T(8,128)(2,1)} %collective-permute-done.46), channel_id=1, source_target_pairs={{0,1},{1,0},{2,3},{3,2},{4,5},{5,4},{6,7},{7,6},{8,9},{9,8},{10,11... | collective-permute-start | bytes 1572872 | tf_op jit(solution)/shard_map/ppermute | solution.py:43
  430.0 55.2 %collective-permute-start.50 = (bf16[256,1024]{1,0:T(8,128)(2,1)}, bf16[256,1024]{1,0:T(8,128)(2,1)}, u32[]{:S(2)}, u32[]{:S(2)}) collective-permute-start(bf16[256,1024]{1,0:T(8,128)(2,1)} %collective-permute-done.49), channel_id=1, source_target_pairs={{0,1},{1,0},{2,3},{3,2},{4,5},{5,4},{6,7},{7,6},{8,9},{9,8},{10,11... | collective-permute-start | bytes 1572872 | tf_op jit(solution)/shard_map/ppermute | solution.py:43
  433.5 54.0 %collective-permute-start.40 = (bf16[128,2048]{1,0:T(8,128)(2,1)}, bf16[128,2048]{1,0:T(8,128)(2,1)}, u32[]{:S(2)}, u32[]{:S(2)}) collective-permute-start(bf16[128,2048]{1,0:T(8,128)(2,1)} %slice_bitcast_fusion.2.refs_1_), channel_id=1, source_target_pairs={{0,2},{1,3},{2,0},{3,1},{4,6},{5,7},{6,4},{7,5},{8,10},{9,11},{10,... | collective-permute-start | bytes 1572872 | tf_op jit(solution)/shard_map/ppermute | solution.py:43
  459.1 36.5 %collective-permute-start.51 = (bf16[640,512]{1,0:T(8,128)(2,1)S(1)}, bf16[640,512]{1,0:T(8,128)(2,1)}, u32[]{:S(2)}, u32[]{:S(2)}) collective-permute-start(bf16[640,512]{1,0:T(8,128)(2,1)S(1)} %copy-done.60), channel_id=1, source_target_pairs={{0,16},{16,0},{1,17},{17,1},{2,18},{18,2},{3,19},{19,3},{4,20},{20... | collective-permute-start | bytes 1966088 | tf_op jit(solution)/shard_map/ppermute | solution.py:43
  464.0 33.8 %collective-permute-start.48 = (bf16[512,512]{1,0:T(8,128)(2,1)S(1)}, bf16[512,512]{1,0:T(8,128)(2,1)}, u32[]{:S(2)}, u32[]{:S(2)}) collective-permute-start(bf16[512,512]{1,0:T(8,128)(2,1)S(1)} %copy-done.61), channel_id=1, source_target_pairs={{0,16},{16,0},{1,17},{17,1},{2,18},{18,2},{3,19},{19,3},{4,20},{20... | collective-permute-start | bytes 1572872 | tf_op jit(solution)/shard_map/ppermute | solution.py:43
  480.5 54.1 %collective-permute-start.57 = (bf16[640,1024]{1,0:T(8,128)(2,1)S(1)}, bf16[640,1024]{1,0:T(8,128)(2,1)}, u32[]{:S(2)}, u32[]{:S(2)}) collective-permute-start(bf16[640,1024]{1,0:T(8,128)(2,1)S(1)} %copy-done.8), channel_id=1, source_target_pairs={{4,0},{8,12},{5,1},{9,13},{6,2},{10,14},{7,3},{11,15},{20,16},{24,... | collective-permute-start | bytes 3932168 | tf_op jit(solution)/shard_map/ppermute | solution.py:140
  487.5 47.1 %collective-permute-start.55 = (bf16[1024,640]{1,0:T(8,128)(2,1)}, bf16[1024,640]{1,0:T(8,128)(2,1)}, u32[]{:S(2)}, u32[]{:S(2)}) collective-permute-start(bf16[1024,640]{1,0:T(8,128)(2,1)} %shard_map.242.refs_1_.refs_2_), channel_id=1, source_target_pairs={{0,4},{12,8},{1,5},{13,9},{2,6},{14,10},{3,7},{15,11},{16,20},{28,... | collective-permute-start | bytes 3932168 | tf_op jit(solution)/shard_map/ppermute | solution.py:137
  495.6 33.5 %collective-permute-start.56 = (bf16[1024,640]{1,0:T(8,128)(2,1)}, bf16[1024,640]{1,0:T(8,128)(2,1)}, u32[]{:S(2)}, u32[]{:S(2)}) collective-permute-start(bf16[1024,640]{1,0:T(8,128)(2,1)} %add.310), channel_id=1, source_target_pairs={{4,8},{8,4},{5,9},{9,5},{6,10},{10,6},{7,11},{11,7},{20,24},{24,20... | collective-permute-start | bytes 3932168 | tf_op jit(solution)/shard_map/ppermute | solution.py:139
  505.4 35.2 %collective-permute-start.53 = (f32[2,2048]{1,0:T(2,128)}, f32[2,2048]{1,0:T(2,128)}, u32[]{:S(2)}, u32[]{:S(2)}) collective-permute-start(f32[2,2048]{1,0:T(2,128)} %fusion.35), channel_id=1, source_target_pairs={{0,2},{1,3},{2,0},{3,1},{4,6},{5,7},{6,4},{7,5},{8,10},{9,11},{10,... | collective-permute-start | bytes 49160 | tf_op jit(solution)/shard_map/ppermute | solution.py:43
  509.5 33.6 %collective-permute-start.36 = (bf16[2,128,1024]{2,1,0:T(8,128)(2,1)S(1)}, bf16[2,128,1024]{2,1,0:T(8,128)(2,1)}, u32[]{:S(2)}, u32[]{:S(2)}) collective-permute-start(bf16[2,128,1024]{2,1,0:T(8,128)(2,1)S(1)} %split.154), channel_id=1, source_target_pairs={{0,2},{1,3},{2,0},{3,1},{4,6},{5,7},{6,4},{7,5},{8,10},{9,11},{10,... | collective-permute-start | bytes 1572872 | tf_op jit(solution)/shard_map/ppermute | solution.py:43
  532.2 41.1 %collective-permute-start.60 = (bf16[1024,640]{1,0:T(8,128)(2,1)}, bf16[1024,640]{1,0:T(8,128)(2,1)}, u32[]{:S(2)}, u32[]{:S(2)}) collective-permute-start(bf16[1024,640]{1,0:T(8,128)(2,1)} %add.311.refs_2_.refs_0_), channel_id=1, source_target_pairs={{4,0},{8,12},{5,1},{9,13},{6,2},{10,14},{7,3},{11,15},{20,16},{24,... | collective-permute-start | bytes 3932168 | tf_op jit(solution)/shard_map/ppermute | solution.py:140
  534.7 27.0 %collective-permute-start.58 = (bf16[512,1024]{1,0:T(8,128)(2,1)}, bf16[512,1024]{1,0:T(8,128)(2,1)S(1)}, u32[]{:S(2)}, u32[]{:S(2)}) collective-permute-start(bf16[512,1024]{1,0:T(8,128)(2,1)} %shard_map.251), channel_id=1, source_target_pairs={{0,4},{12,8},{1,5},{13,9},{2,6},{14,10},{3,7},{15,11},{16,20},{28,... | collective-permute-start | bytes 3145736 | tf_op jit(solution)/shard_map/ppermute | solution.py:137
  538.2 32.3 %collective-permute-start.59 = (bf16[1024,640]{1,0:T(8,128)(2,1)S(1)}, bf16[1024,640]{1,0:T(8,128)(2,1)S(1)}, u32[]{:S(2)}, u32[]{:S(2)}) collective-permute-start(bf16[1024,640]{1,0:T(8,128)(2,1)S(1)} %add.312), channel_id=1, source_target_pairs={{4,8},{8,4},{5,9},{9,5},{6,10},{10,6},{7,11},{11,7},{20,24},{24,20... | collective-permute-start | bytes 3932168 | tf_op jit(solution)/shard_map/ppermute | solution.py:139
  545.0 30.6 %collective-permute-start.37 = (bf16[1,128,1024]{2,1,0:T(8,128)(2,1)}, bf16[1,128,1024]{2,1,0:T(8,128)(2,1)}, u32[]{:S(2)}, u32[]{:S(2)}) collective-permute-start(bf16[1,128,1024]{2,1,0:T(8,128)(2,1)} %split.195), channel_id=1, source_target_pairs={{0,16},{16,0},{1,17},{17,1},{2,18},{18,2},{3,19},{19,3},{4,20},{20... | collective-permute-start | bytes 786440 | tf_op jit(solution)/shard_map/ppermute | solution.py:43
  556.6 23.8 %collective-permute-start.35 = (bf16[128,1024]{1,0:T(8,128)(2,1)}, bf16[128,1024]{1,0:T(8,128)(2,1)}, u32[]{:S(2)}, u32[]{:S(2)}) collective-permute-start(bf16[128,1024]{1,0:T(8,128)(2,1)} %fusion.11), channel_id=1, source_target_pairs={{0,2},{1,3},{2,0},{3,1},{4,6},{5,7},{6,4},{7,5},{8,10},{9,11},{10,... | collective-permute-start | bytes 786440 | tf_op jit(solution)/shard_map/ppermute | solution.py:43
  561.7 44.6 %collective-permute-start.44 = (bf16[128,2048]{1,0:T(8,128)(2,1)S(1)}, bf16[128,2048]{1,0:T(8,128)(2,1)}, u32[]{:S(2)}, u32[]{:S(2)}) collective-permute-start(bf16[128,2048]{1,0:T(8,128)(2,1)S(1)} %copy-done.24), channel_id=1, source_target_pairs={{0,2},{1,3},{2,0},{3,1},{4,6},{5,7},{6,4},{7,5},{8,10},{9,11},{10,... | collective-permute-start | bytes 1572872 | tf_op jit(solution)/shard_map/ppermute | solution.py:43
  573.3 25.9 %collective-permute-start.62 = (bf16[512,1024]{1,0:T(8,128)(2,1)}, bf16[512,1024]{1,0:T(8,128)(2,1)}, u32[]{:S(2)}, u32[]{:S(2)}) collective-permute-start(bf16[512,1024]{1,0:T(8,128)(2,1)} %add.314), channel_id=1, source_target_pairs={{4,8},{8,4},{5,9},{9,5},{6,10},{10,6},{7,11},{11,7},{20,24},{24,20... | collective-permute-start | bytes 3145736 | tf_op jit(solution)/shard_map/ppermute | solution.py:139
  576.9 28.1 %collective-permute-start.63 = (bf16[1024,640]{1,0:T(8,128)(2,1)S(1)}, bf16[1024,640]{1,0:T(8,128)(2,1)}, u32[]{:S(2)}, u32[]{:S(2)}) collective-permute-start(bf16[1024,640]{1,0:T(8,128)(2,1)S(1)} %copy-done.9), channel_id=1, source_target_pairs={{4,0},{8,12},{5,1},{9,13},{6,2},{10,14},{7,3},{11,15},{20,16},{24,... | collective-permute-start | bytes 3932168 | tf_op jit(solution)/shard_map/ppermute | solution.py:140
  583.8 24.7 %collective-permute-start.38 = (bf16[128,2048]{1,0:T(8,128)(2,1)}, bf16[128,2048]{1,0:T(8,128)(2,1)}, u32[]{:S(2)}, u32[]{:S(2)}) collective-permute-start(bf16[128,2048]{1,0:T(8,128)(2,1)} %fusion.1), channel_id=1, source_target_pairs={{0,2},{1,3},{2,0},{3,1},{4,6},{5,7},{6,4},{7,5},{8,10},{9,11},{10,... | collective-permute-start | bytes 1572872 | tf_op jit(solution)/shard_map/ppermute | solution.py:43
  608.4 58.4 %collective-permute-start.45 = (bf16[256,2048]{1,0:T(8,128)(2,1)}, bf16[256,2048]{1,0:T(8,128)(2,1)}, u32[]{:S(2)}, u32[]{:S(2)}) collective-permute-start(bf16[256,2048]{1,0:T(8,128)(2,1)} %shard_map.246.first), channel_id=1, source_target_pairs={{0,1},{1,0},{2,3},{3,2},{4,5},{5,4},{6,7},{7,6},{8,9},{9,8},{10,11... | collective-permute-start | bytes 3145736 | tf_op jit(solution)/shard_map/ppermute | solution.py:43
  610.0 67.8 %collective-permute-start.39 = (bf16[256,2048]{1,0:T(8,128)(2,1)S(1)}, bf16[256,2048]{1,0:T(8,128)(2,1)}, u32[]{:S(2)}, u32[]{:S(2)}) collective-permute-start(bf16[256,2048]{1,0:T(8,128)(2,1)S(1)} %pad_maximum_fusion.6.first), channel_id=1, source_target_pairs={{0,1},{1,0},{2,3},{3,2},{4,5},{5,4},{6,7},{7,6},{8,9},{9,8},{10,11... | collective-permute-start | bytes 3145736 | tf_op jit(solution)/shard_map/ppermute | solution.py:43
  610.4 72.2 %collective-permute-start.69 = (bf16[512,1024]{1,0:T(8,128)(2,1)S(1)}, bf16[512,1024]{1,0:T(8,128)(2,1)}, u32[]{:S(2)}, u32[]{:S(2)}) collective-permute-start(bf16[512,1024]{1,0:T(8,128)(2,1)S(1)} %copy-done.12), channel_id=1, source_target_pairs={{4,0},{8,12},{5,1},{9,13},{6,2},{10,14},{7,3},{11,15},{20,16},{24,... | collective-permute-start | bytes 3145736 | tf_op jit(solution)/shard_map/ppermute | solution.py:140
  623.6 27.4 %collective-permute-start.65 = (bf16[528,640]{1,0:T(8,128)(2,1)S(1)}, bf16[528,640]{1,0:T(8,128)(2,1)}, u32[]{:S(2)}, u32[]{:S(2)}) collective-permute-start(bf16[528,640]{1,0:T(8,128)(2,1)S(1)} %add.316), channel_id=1, source_target_pairs={{4,8},{8,4},{5,9},{9,5},{6,10},{10,6},{7,11},{11,7},{20,24},{24,20... | collective-permute-start | bytes 2027528 | tf_op jit(solution)/shard_map/ppermute | solution.py:139
  637.7 46.3 %collective-permute-start.68 = (bf16[512,640]{1,0:T(8,128)(2,1)S(1)}, bf16[512,640]{1,0:T(8,128)(2,1)}, u32[]{:S(2)}, u32[]{:S(2)}) collective-permute-start(bf16[512,640]{1,0:T(8,128)(2,1)S(1)} %add.319), channel_id=1, source_target_pairs={{4,0},{8,12},{5,1},{9,13},{6,2},{10,14},{7,3},{11,15},{20,16},{24,... | collective-permute-start | bytes 1966088 | tf_op jit(solution)/shard_map/ppermute | solution.py:140
  652.5 31.6 %collective-permute-start.66 = (bf16[528,640]{1,0:T(8,128)(2,1)S(1)}, bf16[528,640]{1,0:T(8,128)(2,1)}, u32[]{:S(2)}, u32[]{:S(2)}) collective-permute-start(bf16[528,640]{1,0:T(8,128)(2,1)S(1)} %add.317), channel_id=1, source_target_pairs={{4,0},{8,12},{5,1},{9,13},{6,2},{10,14},{7,3},{11,15},{20,16},{24,... | collective-permute-start | bytes 2027528 | tf_op jit(solution)/shard_map/ppermute | solution.py:140
  (125 other events, 1022.6 us)
Sparse Core Ops, SparseCore 0:
  83.6 37.9 all-gather.5
  123.2 35.9 all-gather.7
  202.7 36.0 reduce-scatter.3
  241.5 34.2 reduce-scatter.5
  277.2 36.1 all-gather.9
  315.6 49.5 reduce-scatter.7
  395.3 53.6 all-gather.11
  450.6 38.2 all-gather.13

commit v4 on v3

--- a/solution.py
+++ b/solution.py
@@ -127,18 +127,27 @@
     def __init__(self):
         self.piece, self.came, self.total, self.done = [], [], [], []
 
-    def put(self, piece):
-        k = len(self.came)
-        far = k - 1
-        earlier = [v[i] for v, i in ((self.came, far), (self.total, far - 1), (self.done, far - 2)) if i >= 0]
+    def start(self, piece):
+        k = len(self.piece)
+        before = ((self.came, k - 1), (self.total, k - 2), (self.done, k - 3))
+        earlier = [v[i] for v, i in before if i >= 0]
         if earlier:
             (piece,) = after([piece], *earlier)
         self.piece.append(piece)
-        self.came.append(lax.ppermute(piece, "ctx", [(0, 1), (3, 2)]))
-        inward = piece + self.came[-1]
+
+    def land(self, *hold):
+        piece = self.piece[len(self.came)]
+        came = lax.ppermute(piece, "ctx", [(0, 1), (3, 2)])
+        if hold:
+            (came,) = after([came], *hold)
+        self.came.append(came)
+        inward = piece + came
         self.total.append(inward + lax.ppermute(inward, "ctx", [(1, 2), (2, 1)]))
         self.done.append(lax.ppermute(self.total[-1], "ctx", [(1, 0), (2, 3)]))
-        return len(self.total) - 1
+
+    def put(self, piece):
+        self.start(piece)
+        self.land()
 
 
 def attend_kernel(
@@ -839,14 +848,13 @@
             after_sent = after([places], grad_keep, *sent)[0]
             kept["gate"] = weigh(after_sent, normed_two, 0, half, dgate, 3, big)
             scatter("gate", kept["gate"])
-            return [kept["gate"], scattered["down"]]
+            return [kept["gate"]]
 
         grad_own, sent = scatter_rows(grad_keep, grad_give, between)
         (places,) = after([places], kept["gate"], *sent)
-        kept_upper = weigh(places, normed_two, 0, half, dupper, 3, big)
-        scatter("upper", kept_upper)
-        (places,) = after([places], kept_upper)
-        (grad_own,) = after([grad_own], kept_upper)
+        given_down = weigh(places, hidden, 4, small, upstream, 1, half)
+        (places,) = after([places], given_down)
+        (grad_own,) = after([grad_own], given_down)
     else:
         for i in range(2):
             hidden[i], dgate[i], dupper[i] = forward(i)
@@ -865,8 +873,9 @@
     grad_attn = gather_own(grad_one_low)
     if paired:
         (places,) = after([places], grad_one_low)
-        given_down = weigh(places, hidden, 4, small, upstream, 1, half)
-        (places,) = after([places], given_down)
+        kept_upper = weigh(places, normed_two, 0, half, dupper, 3, big)
+        scatter("upper", kept_upper)
+        (places,) = after([places], kept_upper)
         given_gate = weigh(places, normed_two, 1, half, dgate, 4, small)
         (places,) = after([places], given_gate)
         line.put(over_x(given_down))
@@ -885,17 +894,14 @@
         given_upper = weigh(places, normed_two, 1, half, dupper, 4, small)
         (places,) = after([places], given_upper)
         came_gate = over_x(given_gate)
-        line.put(came_gate)
+        line.start(came_gate)
         gather("down")
         received = after(received, given_upper, line.piece[1], scattered["upper"], sums["down"])
         gather("gate", scattered["upper"])
         came_upper = over_x(given_upper)
-        line.put(came_upper)
         attn_there, one_there, mixed_there = after(
             [theirs(grad_attn), theirs(normed_one), mixed_low], came_upper
         )
-        attn_there, one_there = both_cores(attn_there), both_cores(one_there)
-        mixed_there = over_x(mixed_there)
     else:
         line.put(spread(dot(mixed_low, grad_attn, 1, 0).astype(low), 1))
     for m in received:
@@ -909,7 +915,8 @@
     keep, give = cut(first[None], 1)
     first_own, sent = scatter_rows(keep, give)
     if paired:
-        (first_own,) = after([first_own], line.piece[2], sums["gate"])
+        line.land(first_own)
+        line.put(came_upper)
         gather("upper", *sent)
         (places,) = after([places], *sent)
     else:
@@ -923,11 +930,13 @@
         attn_there, mixed_there, one_there = after(
             [attn_there, mixed_there, one_there], input_low
         )
+        attn_there, one_there = both_cores(attn_there), both_cores(one_there)
+        mixed_there = over_x(mixed_there)
         output_grad = dot(mixed_low, mine(grad_attn), 1, 0) + dot(
             mixed_there, attn_there, 1, 0
         )
         line.put(output_grad.astype(low))
-        (dqkv_there,) = after([over_x(dqkv)], input_low, line.piece[2])
+        (dqkv_there,) = after([over_x(dqkv)], input_low)
         qkv_grad = (
             dot(mine(normed_one), dqkv, 0, 1) + dot(one_there, dqkv_there, 0, 1)
         ).astype(low)
@@ -935,9 +944,15 @@
         gather("down")
         gather("gate")
         gather("upper")
-    late = [sums["upper"]] if paired else []
+    late = [line.piece[2]] if paired else []
+    (places,) = after([places], input_low)
+    if paired:
+        (places,) = after([places], sums["gate"])
     input_grad = place(order, gather_own(input_low, *late), high)
-    ffn_own, _ = scatter_rows(ffn(0), ffn(1))
+    ffn_give = ffn(1)
+    if paired:
+        (places,) = after([places], ffn_give, sums["upper"])
+    ffn_own, _ = scatter_rows(ffn(0), ffn_give)
     activations = place(order, gather_own((one_own + ffn_own).astype(low)), low)
 
     gain_sums = sum_all(jnp.stack([gain_one_sum, gain_two_sum]), "tp", nt)
@@ -966,14 +981,16 @@
         for i, (name, axis) in enumerate((("down", 0), ("gate", 1), ("upper", 1)))
     )
     output_grad = whole(-3).astype(high)
-    qkv_grad = jnp.concatenate([whole(-2), whole(-1)[:-extra]], axis=0).astype(high)
+    halves = (whole(-2).astype(high), whole(-1)[:-extra].astype(high))
+    query_grad = jnp.concatenate([v[:, :query_width] for v in halves], axis=0)
+    keyval_grad = jnp.concatenate([v[:, query_width:] for v in halves], axis=0)
     gain_sums = whole(-1)[-extra:].astype(high).reshape(-1)[: 2 * half].reshape(2, half)
     return (
         activations,
         input_grad,
         gain_sums[0],
-        qkv_grad[:, :query_width],
-        qkv_grad[:, query_width:],
+        query_grad,
+        keyval_grad,
         output_grad,
         gain_sums[1],
         gate_grad,

time: 705 us -> 688 us (0.976)
  starting transfers between devices: 109 us -> 99.1 us
    all_gather x3, waiting for transfers between devices: 0.02 us -> 17.1 us  [gather(): sums[name] = lax.all_gather(piece, 'ctx', axis=0, tiled=True)]
    ppermute x6, waiting for transfers between devices: 3.99 us -> 17.7 us  [shift(): return lax.ppermute(value, axis, pairs)]
    ppermute x6, starting transfers between devices: 26.4 us -> 14.5 us  [shift(): return lax.ppermute(value, axis, pairs)]
    reduce_scatter x3, waiting for transfers between devices: 15.4 us -> 4.32 us  [scatter(): lax.psum_scatter(piece, 'ctx', scatter_dimension=0, tiled=True)]
    ppermute x46, waiting for transfers between devices: 99.8 us -> 89.5 us  [swap(): return lax.ppermute(value, axis, pairs)]
    ppermute x18, waiting for transfers between devices: 85.2 us -> 76.5 us  [the longest x6 66.1 us: land(): self.total.append(inward + lax.ppermute(inward, 'ctx', [(1, 2), (2, 1)]))]
    unnamed x198 -> x182, local copies, waits for them, and re-layouts: 16.4 us -> 16.8 us
  transfers between devices with their start and end apart: 78 -> 78, of which waited for: 29 -> 33; matrix products, arithmetic and copies ran while one was open for 22% -> 21% of each run, Pallas kernels for 24% -> 23%
where the time goes in v4:
time: 688 us; the launch traced here: 678 us
  waiting for transfers between devices  205 us (30%)
  Pallas kernels  193 us (28%)
  other arithmetic  102 us (15%)
  starting transfers between devices  99.1 us (14%)
  local copies, waits for them, and re-layouts  52.6 us (8%)
  between operations  15.9 us (2%)
  matrix products  9.47 us (1%)
    ppermute x46, waiting for transfers between devices, swap(): return lax.ppermute(value, axis, pairs)  89.5 us
    ppermute x6, waiting for transfers between devices, land(): self.total.append(inward + lax.ppermute(inward, 'ctx', [(1, 2), (2, 1)]))  66.1 us
    pallas_call x6, Pallas kernels, project(): pl.pallas_call(functools.partial(project_kernel, parts, factors, steps, o...  41.9 us
    ppermute x46, starting transfers between devices, swap(): return lax.ppermute(value, axis, pairs)  40.7 us
    pallas_call x6, Pallas kernels, weigh(): pl.pallas_call(functools.partial(weigh_kernel, parts, at_left, at_right,...  38.7 us
    pallas_call x1, Pallas kernels, attend_back(): pl.pallas_call(functools.partial(attend_back_kernel, heads), grid_spec=pl...  30.5 us
    ppermute x6, starting transfers between devices, land(): self.total.append(inward + lax.ppermute(inward, 'ctx', [(1, 2), (2, 1)]))  19.6 us
    pallas_call x2, Pallas kernels, middle(): pl.pallas_call(functools.partial(middle_kernel, parts), grid_spec=pltpu.P...  18.4 us
  transfers between devices with their start and end apart: 78, of which 33 were waited for; matrix products, arithmetic and copies ran while one was open for 21% of the time, Pallas kernels for 23%

profile of v4, /device:TPU:8, one launch (start us, length us, event | category | flops | bytes accessed | tf_op | source)
XLA Modules:
  0.0 677.7 jit_solution(510365687571834264)
XLA Ops:
  26.0 4.1 multiply_convert_fusion.rows
  30.1 13.4 %collective-permute-done.1.refs_1_.refs_2_ = bf16[1024,640]{1,0:T(8,128)(2,1)} collective-permute-done((bf16[1024,640]{1,0:T(8,128)(2,1)S(1)}, bf16[1024,640]{1,0:T(8,128)(2,1)}, u32[]{:S(2)}, u32[]{:S(2)}) %collective-permute-start.1) | collective-permute-done | bytes 1310752 | tf_op jit(solution)/shard_map/ppermute | solution.py:43
  43.5 8.0 %shard_map.195 = (bf16[512,512]{1,0:T(8,128)(2,1)}, bf16[4,128,128]{2,1,0:T(8,128)(2,1)}) custom-call(s32[5]{0:T(128)} %stack.87.places.refs_0_, bf16[512,2048]{1,0:T(8,128)(2,1)} %multiply_convert_fusion.rows, f32[32,512]{1,0:T(8,128)} %get-tuple-element.118.cosine, f32[32,512]{1,0:T(8,128)} %get-tuple-element.117.sine, bf16[1024,640]{1,0:T(8,128)(2,1)} %copy-done.13, ...), custom_call_target="tpu_custom_call" | custom-call | flops 1000000 | bytes 100000 | tf_op jit(solution)/shard_map/pallas_call | solution.py:554
  68.4 10.9 %shard_map.196 = (f32[8,64,512]{2,1,0:T(8,128)}, f32[8,512]{1,0:T(8,128)}) custom-call(s32[4]{0:T(128)} %convert_reduce_fusion.count, s32[4,16]{1,0:T(4,128)} %select_reduce_fusion.tiles, bf16[8,64,512]{2,1,0:T(8,128)(2,1)} %bitcast.132, bf16[16,128,128]{2,1,0:T(8,128)(2,1)} %copy-done.54, s32[1,512]{1,0:T(1,128)} %copy-done.79, s32[1,512]{1,0:T(1,128)} %copy-done.80, ...), custom_call_target="tpu_custom_call" | custom-call | flops 1000000 | bytes 100000 | tf_op jit(solution)/shard_map/pallas_call | solution.py:193
  85.7 5.7 shard_map.198
  95.2 3.9 constant_dynamic-slice_fusion.8
  102.2 6.1 collective-permute-done.9
  121.8 6.9 %collective-permute-done.7 = bf16[128,2048]{1,0:T(8,128)(2,1)} collective-permute-done((bf16[128,2048]{1,0:T(8,128)(2,1)}, bf16[128,2048]{1,0:T(8,128)(2,1)}, u32[]{:S(2)}, u32[]{:S(2)}) %collective-permute-start.7) | collective-permute-done | bytes 524320 | tf_op jit(solution)/shard_map/ppermute | solution.py:43
  131.5 4.3 collective-permute-done.11.refs_3_.refs_1_.refs_2_
  139.3 6.4 shard_map.203.refs_2_.grads
  150.4 6.3 shard_map.205.refs_1_.grads
  168.7 9.2 %shard_map.207 = (bf16[512,768]{1,0:T(8,128)(2,1)}, bf16[512,768]{1,0:T(8,128)(2,1)}, bf16[512,768]{1,0:T(8,128)(2,1)}) custom-call(s32[5]{0:T(128)} %stack.87.places.refs_0_, bf16[512,2048]{1,0:T(8,128)(2,1)} %bitcast.109, f32[512,768]{1,0:T(8,128)} %shard_map.205.refs_1_.grads, bf16[1024,768]{1,0:T(8,128)(2,1)} %constant_dynamic-slice_fusion.7.refs_0_.refs_2_, ...), custom_call_target="tpu_custom_call" | custom-call | flops 1000000 | bytes 16605000 | tf_op jit(solution)/shard_map/pallas_call | solution.py:364
  177.9 8.6 %shard_map.209 = bf16[512,2048]{1,0:T(8,128)(2,1)} custom-call(s32[5]{0:T(128)} %shard_map.208.places.refs_0_, bf16[512,768]{1,0:T(8,128)(2,1)} %get-tuple-element.46.refs_0_.refs_3_, bf16[512,768]{1,0:T(8,128)(2,1)} %get-tuple-element.47.refs_1_.refs_3_, bf16[1024,768]{1,0:T(8,128)(2,1)} %constant_dynamic-slice_fusion.7.refs_0_.refs_2_, ...), custom_call_target="tpu_custom_call" | custom-call | flops 1000000 | bytes 11070000 | tf_op jit(solution)/shard_map/pallas_call | solution.py:415
  186.5 9.2 %shard_map.211 = (bf16[512,768]{1,0:T(8,128)(2,1)}, bf16[512,768]{1,0:T(8,128)(2,1)}, bf16[512,768]{1,0:T(8,128)(2,1)}) custom-call(s32[5]{0:T(128)} %shard_map.210.places.refs_0_, bf16[512,2048]{1,0:T(8,128)(2,1)} %bitcast.104, f32[512,768]{1,0:T(8,128)} %shard_map.203.refs_2_.grads, bf16[1024,768]{1,0:T(8,128)(2,1)} %constant_dynamic-slice_fusion.7.refs_0_.refs_2_, ...), custom_call_target="tpu_custom_call" | custom-call | flops 1000000 | bytes 16605000 | tf_op jit(solution)/shard_map/pallas_call | solution.py:364
  195.7 6.7 shard_map.213.refs_1_
  203.9 8.6 %shard_map.215 = bf16[512,2048]{1,0:T(8,128)(2,1)} custom-call(s32[5]{0:T(128)} %shard_map.214.places.refs_0_, bf16[512,768]{1,0:T(8,128)(2,1)} %get-tuple-element.49.refs_0_.refs_2_, bf16[512,768]{1,0:T(8,128)(2,1)} %get-tuple-element.50.refs_1_.refs_2_, bf16[1024,768]{1,0:T(8,128)(2,1)} %constant_dynamic-slice_fusion.7.refs_0_.refs_2_, ...), custom_call_target="tpu_custom_call" | custom-call | flops 1000000 | bytes 11070000 | tf_op jit(solution)/shard_map/pallas_call | solution.py:415
  217.3 6.1 shard_map.217.refs_2_.refs_1_
  225.7 12.3 %collective-permute-done.20.refs_0_ = bf16[1,256,1024]{2,1,0:T(8,128)(2,1)} collective-permute-done((bf16[1,256,1024]{2,1,0:T(8,128)(2,1)}, bf16[1,256,1024]{2,1,0:T(8,128)(2,1)}, u32[]{:S(2)}, u32[]{:S(2)}) %collective-permute-start.20) | collective-permute-done | bytes 524320 | tf_op jit(solution)/shard_map/ppermute | solution.py:43
  245.5 7.6 %shard_map.220.refs_1_ = bf16[640,1024]{1,0:T(8,128)(2,1)} custom-call(s32[5]{0:T(128)} %shard_map.219.places.refs_0_, bf16[512,768]{1,0:T(8,128)(2,1)} %get-tuple-element.48.refs_1_.refs_0_, bf16[512,768]{1,0:T(8,128)(2,1)} %get-tuple-element.45.refs_1_.refs_0_, bf16[512,2048]{1,0:T(8,128)(2,1)} %pad_maximum_fusion.refs_1_.upstream.refs_2_, ...), custom_call_target="tpu_custom_call" | custom-call | flops 1000000 | bytes 11070000 | tf_op jit(solution)/shard_map/pallas_call | solution.py:478
  260.2 6.2 shard_map.224.refs_1_
  268.0 11.4 %collective-permute-done.24 = bf16[128,2048]{1,0:T(8,128)(2,1)S(1)} collective-permute-done((bf16[128,2048]{1,0:T(8,128)(2,1)S(1)}, bf16[128,2048]{1,0:T(8,128)(2,1)S(1)}, u32[]{:S(2)}, u32[]{:S(2)}) %collective-permute-start.24) | collective-permute-done | bytes 524320 | tf_op jit(solution)/shard_map/ppermute | solution.py:43
  281.3 6.1 shard_map.226.refs_1_
  289.1 9.3 %collective-permute-done.26.refs_1_ = bf16[640,1024]{1,0:T(8,128)(2,1)} collective-permute-done((bf16[640,1024]{1,0:T(8,128)(2,1)S(1)}, bf16[640,1024]{1,0:T(8,128)(2,1)}, u32[]{:S(2)}, u32[]{:S(2)}) %collective-permute-start.26) | collective-permute-done | bytes 1310752 | tf_op jit(solution)/shard_map/ppermute | solution.py:43
  299.7 4.8 shard_map.228
  304.5 30.5 %shard_map.230 = (f32[8,64,512]{2,1,0:T(8,128)}, f32[16,128,128]{2,1,0:T(8,128)}) custom-call(s32[4]{0:T(128)} %convert_reduce_fusion.count, s32[4,16]{1,0:T(4,128)} %select_reduce_fusion.tiles, bf16[8,64,512]{2,1,0:T(8,128)(2,1)} %bitcast.133, bf16[16,128,128]{2,1,0:T(8,128)(2,1)} %copy-done.54, s32[1,512]{1,0:T(1,128)} %copy-done.79, s32[1,512]{1,0:T(1,128)} %copy-done.80, ...), custom_call_target="tpu_custom_call" | custom-call | flops 1000000 | bytes 44280000 | tf_op jit(solution)/shard_map/pallas_call | solution.py:260
  337.2 9.8 %collective-permute-start.28 = (bf16[4,128,128]{2,1,0:T(8,128)(2,1)}, bf16[4,128,128]{2,1,0:T(8,128)(2,1)}, u32[]{:S(2)}, u32[]{:S(2)}) collective-permute-start(bf16[4,128,128]{2,1,0:T(8,128)(2,1)} %get-tuple-element.91.refs_2_), channel_id=1, source_target_pairs={{0,8},{4,12},{8,0},{12,4},{1,9},{5,13},{9,1},{13,5},{2,10},{6,14},... | collective-permute-start | bytes 393224 | tf_op jit(solution)/shard_map/ppermute | solution.py:48
  347.3 6.0 shard_map.232.refs_1_.refs_3_
  355.8 4.2 collective-permute-done.28.refs_1_
  360.0 8.2 %collective-permute-done.29.refs_2_ = bf16[4,128,128]{2,1,0:T(8,128)(2,1)} collective-permute-done((bf16[4,128,128]{2,1,0:T(8,128)(2,1)}, bf16[4,128,128]{2,1,0:T(8,128)(2,1)}, u32[]{:S(2)}, u32[]{:S(2)}) %collective-permute-start.29) | collective-permute-done | bytes 131104 | tf_op jit(solution)/shard_map/ppermute | solution.py:48
  368.2 4.3 reduce-scatter.6.cloned.1.call-done.refs_5_.refs_1_.refs_0_
  375.2 6.2 shard_map.236.refs_1_
  399.0 5.6 collective-permute-start.44
  406.1 9.6 %collective-permute-done.42.refs_0_.refs_3_ = bf16[1024,640]{1,0:T(8,128)(2,1)S(1)} collective-permute-done((bf16[1024,640]{1,0:T(8,128)(2,1)}, bf16[1024,640]{1,0:T(8,128)(2,1)S(1)}, u32[]{:S(2)}, u32[]{:S(2)}) %collective-permute-start.42) | collective-permute-done | bytes 1310752 | tf_op jit(solution)/shard_map/ppermute | solution.py:43
  424.6 17.1 %all-gather.12.cloned.1.call-done.refs_1_.kept = bf16[1024,768]{1,0:T(8,128)(2,1)} async-done(((bf16[256,768]{1,0:T(8,128)(2,1)}), bf16[1024,768]{1,0:T(8,128)(2,1)}) %all-gather.12.cloned.1.call-update) | async-done | bytes 1572880 | tf_op jit(solution)/shard_map/all_gather | solution.py:831
  441.7 6.5 shard_map.242
  454.5 4.2 collective-permute-start.56
  477.5 31.7 %collective-permute-done.56 = bf16[1024,640]{1,0:T(8,128)(2,1)} collective-permute-done((bf16[1024,640]{1,0:T(8,128)(2,1)}, bf16[1024,640]{1,0:T(8,128)(2,1)}, u32[]{:S(2)}, u32[]{:S(2)}) %collective-permute-start.56) | collective-permute-done | bytes 1310752 | tf_op jit(solution)/shard_map/ppermute | solution.py:145
  524.9 6.3 shard_map.245
  538.2 6.7 collective-permute-done.58.refs_1_
  550.6 5.2 collective-permute-done.59
  567.8 9.3 %collective-permute-done.62 = bf16[512,1024]{1,0:T(8,128)(2,1)} collective-permute-done((bf16[512,1024]{1,0:T(8,128)(2,1)}, bf16[512,1024]{1,0:T(8,128)(2,1)}, u32[]{:S(2)}, u32[]{:S(2)}) %collective-permute-start.62) | collective-permute-done | bytes 1048608 | tf_op jit(solution)/shard_map/ppermute | solution.py:145
  609.0 10.2 %collective-permute-done.67 = bf16[512,640]{1,0:T(8,128)(2,1)S(1)} collective-permute-done((bf16[512,640]{1,0:T(8,128)(2,1)S(1)}, bf16[512,640]{1,0:T(8,128)(2,1)S(1)}, u32[]{:S(2)}, u32[]{:S(2)}) %collective-permute-start.67) | collective-permute-done | bytes 655392 | tf_op jit(solution)/shard_map/ppermute | solution.py:145
  622.1 9.7 %collective-permute-done.65 = bf16[528,640]{1,0:T(8,128)(2,1)} collective-permute-done((bf16[528,640]{1,0:T(8,128)(2,1)}, bf16[528,640]{1,0:T(8,128)(2,1)}, u32[]{:S(2)}, u32[]{:S(2)}) %collective-permute-start.65) | collective-permute-done | bytes 675872 | tf_op jit(solution)/shard_map/ppermute | solution.py:145
  636.9 5.8 shard_map.259
  642.7 5.2 shard_map.250
  647.9 5.8 shard_map.257
  653.7 5.8 shard_map.258
  661.1 4.8 shard_map.246
  (507 shorter events, 261.0 us)
Async XLA Ops:
  7.2 128.6 %all-gather.6.cloned.1.call-start = ((), (), s32[]{:S(2)}) async-start(), calls=%async_computation.3 | async-start | bytes 1966080 | tf_op jit(solution)/shard_map/all_gather | solution.py:730
  11.6 31.9 %collective-permute-start.1 = (bf16[1024,640]{1,0:T(8,128)(2,1)S(1)}, bf16[1024,640]{1,0:T(8,128)(2,1)}, u32[]{:S(2)}, u32[]{:S(2)}) collective-permute-start(bf16[1024,640]{1,0:T(8,128)(2,1)S(1)} %constant_dynamic-update-slice_fusion.refs_0_.refs_1_), channel_id=1, source_target_pairs={{0,16},{16,0},{1,17},{17,1},{2,18},{18,2},{3,19},{19,3},{4,20},{20... | collective-permute-start | bytes 3932168 | tf_op jit(solution)/shard_map/ppermute | solution.py:43
  23.7 62.0 %collective-permute-start.5 = (bf16[512,1024]{1,0:T(8,128)(2,1)}, bf16[512,1024]{1,0:T(8,128)(2,1)}, u32[]{:S(2)}, u32[]{:S(2)}) collective-permute-start(bf16[512,1024]{1,0:T(8,128)(2,1)} %shard_map.197), channel_id=1, source_target_pairs={{0,16},{16,0},{1,17},{17,1},{2,18},{18,2},{3,19},{19,3},{4,20},{20... | collective-permute-start | bytes 3145736 | tf_op jit(solution)/shard_map/ppermute | solution.py:43
  57.4 21.9 %collective-permute-start.12 = (bf16[256,768]{1,0:T(8,128)(2,1)}, bf16[256,768]{1,0:T(8,128)(2,1)S(1)}, u32[]{:S(2)}, u32[]{:S(2)}) collective-permute-start(bf16[256,768]{1,0:T(8,128)(2,1)} %shard_map.199), channel_id=1, source_target_pairs={{0,16},{16,0},{1,17},{17,1},{2,18},{18,2},{3,19},{19,3},{4,20},{20... | collective-permute-start | bytes 1179656 | tf_op jit(solution)/shard_map/ppermute | solution.py:43
  57.9 24.8 %collective-permute-start.13 = (bf16[256,768]{1,0:T(8,128)(2,1)}, bf16[256,768]{1,0:T(8,128)(2,1)S(1)}, u32[]{:S(2)}, u32[]{:S(2)}) collective-permute-start(bf16[256,768]{1,0:T(8,128)(2,1)} %shard_map.200), channel_id=1, source_target_pairs={{0,16},{16,0},{1,17},{17,1},{2,18},{18,2},{3,19},{19,3},{4,20},{20... | collective-permute-start | bytes 1179656 | tf_op jit(solution)/shard_map/ppermute | solution.py:43
  65.4 28.3 %collective-permute-start.8 = (bf16[128,2048]{1,0:T(8,128)(2,1)S(1)}, bf16[128,2048]{1,0:T(8,128)(2,1)}, u32[]{:S(2)}, u32[]{:S(2)}) collective-permute-start(bf16[128,2048]{1,0:T(8,128)(2,1)S(1)} %copy-done.42), channel_id=1, source_target_pairs={{0,16},{16,0},{1,17},{17,1},{2,18},{18,2},{3,19},{19,3},{4,20},{20... | collective-permute-start | bytes 1572872 | tf_op jit(solution)/shard_map/ppermute | solution.py:43
  83.5 79.4 %all-gather.8.cloned.1.call-start = ((), (), s32[]{:S(2)}) async-start(), calls=%async_computation.4 | async-start | bytes 1966080 | tf_op jit(solution)/shard_map/all_gather | solution.py:730
  99.1 36.7 %collective-permute-start.11 = (bf16[768,1024]{1,0:T(8,128)(2,1)}, bf16[768,1024]{1,0:T(8,128)(2,1)S(1)}, u32[]{:S(2)}, u32[]{:S(2)}) collective-permute-start(bf16[768,1024]{1,0:T(8,128)(2,1)} %get-tuple-element.76), channel_id=1, source_target_pairs={{0,16},{16,0},{1,17},{17,1},{2,18},{18,2},{3,19},{19,3},{4,20},{20... | collective-permute-start | bytes 4718600 | tf_op jit(solution)/shard_map/ppermute | solution.py:43
  118.6 119.9 %reduce-scatter.8.cloned.1.call-start = ((), (), s32[]{:S(2)}) async-start(), calls=%async_computation.7 | async-start | bytes 1966080 | tf_op jit(solution)/shard_map/reduce_scatter | solution.py:825
  202.5 102.0 %reduce-scatter.4.cloned.1.call-start = ((), (), s32[]{:S(2)}) async-start(), calls=%async_computation.5 | async-start | bytes 1966080 | tf_op jit(solution)/shard_map/reduce_scatter | solution.py:825
  223.4 144.8 %all-gather.10.cloned.1.call-start = ((), (), s32[]{:S(2)}) async-start(), calls=%async_computation.8 | async-start | bytes 1966080 | tf_op jit(solution)/shard_map/all_gather | solution.py:831
  238.5 134.0 %reduce-scatter.6.cloned.1.call-start = ((), (), s32[]{:S(2)}) async-start(), calls=%async_computation.6 | async-start | bytes 1966080 | tf_op jit(solution)/shard_map/reduce_scatter | solution.py:825
  266.5 31.9 %collective-permute-start.26 = (bf16[640,1024]{1,0:T(8,128)(2,1)S(1)}, bf16[640,1024]{1,0:T(8,128)(2,1)}, u32[]{:S(2)}, u32[]{:S(2)}) collective-permute-start(bf16[640,1024]{1,0:T(8,128)(2,1)S(1)} %copy-done.11), channel_id=1, source_target_pairs={{0,16},{16,0},{1,17},{17,1},{2,18},{18,2},{3,19},{19,3},{4,20},{20... | collective-permute-start | bytes 3932168 | tf_op jit(solution)/shard_map/ppermute | solution.py:43
  281.3 18.4 %collective-permute-start.25 = (bf16[256,2048]{1,0:T(8,128)(2,1)}, bf16[256,2048]{1,0:T(8,128)(2,1)}, u32[]{:S(2)}, u32[]{:S(2)}) collective-permute-start(bf16[256,2048]{1,0:T(8,128)(2,1)} %pad_maximum_fusion.6.refs_0_), channel_id=1, source_target_pairs={{0,1},{1,0},{2,3},{3,2},{4,5},{5,4},{6,7},{7,6},{8,9},{9,8},{10,11... | collective-permute-start | bytes 3145736 | tf_op jit(solution)/shard_map/ppermute | solution.py:43
  287.4 65.9 %collective-permute-start.30 = (bf16[1024,640]{1,0:T(8,128)(2,1)}, bf16[1024,640]{1,0:T(8,128)(2,1)}, u32[]{:S(2)}, u32[]{:S(2)}) collective-permute-start(bf16[1024,640]{1,0:T(8,128)(2,1)} %shard_map.226.refs_1_), channel_id=1, source_target_pairs={{0,16},{16,0},{1,17},{17,1},{2,18},{18,2},{3,19},{19,3},{4,20},{20... | collective-permute-start | bytes 3932168 | tf_op jit(solution)/shard_map/ppermute | solution.py:43
  298.4 54.9 %collective-permute-start.31 = (bf16[640,1024]{1,0:T(8,128)(2,1)}, bf16[640,1024]{1,0:T(8,128)(2,1)S(1)}, u32[]{:S(2)}, u32[]{:S(2)}) collective-permute-start(bf16[640,1024]{1,0:T(8,128)(2,1)} %collective-permute-done.26.refs_1_), channel_id=1, source_target_pairs={{0,4},{12,8},{1,5},{13,9},{2,6},{14,10},{3,7},{15,11},{16,20},{28,... | collective-permute-start | bytes 3932168 | tf_op jit(solution)/shard_map/ppermute | solution.py:140
  304.5 137.2 %all-gather.12.cloned.1.call-start = ((), (), s32[]{:S(2)}) async-start(), calls=%async_computation.9 | async-start | bytes 1966080 | tf_op jit(solution)/shard_map/all_gather | solution.py:831
  337.2 18.6 %collective-permute-start.27 = (bf16[4,128,128]{2,1,0:T(8,128)(2,1)}, bf16[4,128,128]{2,1,0:T(8,128)(2,1)S(1)}, u32[]{:S(2)}, u32[]{:S(2)}) collective-permute-start(bf16[4,128,128]{2,1,0:T(8,128)(2,1)} %get-tuple-element.92.refs_1_), channel_id=1, source_target_pairs={{0,12},{4,0},{8,4},{12,8},{1,13},{5,1},{9,5},{13,9},{2,14},{6,2},{... | collective-permute-start | bytes 393224 | tf_op jit(solution)/shard_map/ppermute | solution.py:48
  337.2 22.8 %collective-permute-start.28 = (bf16[4,128,128]{2,1,0:T(8,128)(2,1)}, bf16[4,128,128]{2,1,0:T(8,128)(2,1)}, u32[]{:S(2)}, u32[]{:S(2)}) collective-permute-start(bf16[4,128,128]{2,1,0:T(8,128)(2,1)} %get-tuple-element.91.refs_2_), channel_id=1, source_target_pairs={{0,8},{4,12},{8,0},{12,4},{1,9},{5,13},{9,1},{13,5},{2,10},{6,14},... | collective-permute-start | bytes 393224 | tf_op jit(solution)/shard_map/ppermute | solution.py:48
  346.9 21.3 %collective-permute-start.29 = (bf16[4,128,128]{2,1,0:T(8,128)(2,1)}, bf16[4,128,128]{2,1,0:T(8,128)(2,1)}, u32[]{:S(2)}, u32[]{:S(2)}) collective-permute-start(bf16[4,128,128]{2,1,0:T(8,128)(2,1)} %get-tuple-element.90.refs_3_), channel_id=1, source_target_pairs={{0,4},{4,8},{8,12},{12,0},{1,5},{5,9},{9,13},{13,1},{2,6},{6,10},{... | collective-permute-start | bytes 393224 | tf_op jit(solution)/shard_map/ppermute | solution.py:48
  383.8 141.1 %all-gather.14.cloned.1.call-start = ((), (), s32[]{:S(2)}) async-start(), calls=%async_computation.10 | async-start | bytes 1966080 | tf_op jit(solution)/shard_map/all_gather | solution.py:831
  383.9 31.8 %collective-permute-start.42 = (bf16[1024,640]{1,0:T(8,128)(2,1)}, bf16[1024,640]{1,0:T(8,128)(2,1)S(1)}, u32[]{:S(2)}, u32[]{:S(2)}) collective-permute-start(bf16[1024,640]{1,0:T(8,128)(2,1)} %shard_map.232.refs_1_.refs_3_), channel_id=1, source_target_pairs={{0,16},{16,0},{1,17},{17,1},{2,18},{18,2},{3,19},{19,3},{4,20},{20... | collective-permute-start | bytes 3932168 | tf_op jit(solution)/shard_map/ppermute | solution.py:43
  388.8 28.0 %collective-permute-start.33 = (bf16[128,2048]{1,0:T(8,128)(2,1)S(1)}, bf16[128,2048]{1,0:T(8,128)(2,1)}, u32[]{:S(2)}, u32[]{:S(2)}) collective-permute-start(bf16[128,2048]{1,0:T(8,128)(2,1)S(1)} %slice_bitcast_fusion.2.refs_1_), channel_id=1, source_target_pairs={{0,2},{1,3},{2,0},{3,1},{4,6},{5,7},{6,4},{7,5},{8,10},{9,11},{10,... | collective-permute-start | bytes 1572872 | tf_op jit(solution)/shard_map/ppermute | solution.py:43
  393.4 54.9 %collective-permute-start.43 = (bf16[1024,640]{1,0:T(8,128)(2,1)}, bf16[1024,640]{1,0:T(8,128)(2,1)}, u32[]{:S(2)}, u32[]{:S(2)}) collective-permute-start(bf16[1024,640]{1,0:T(8,128)(2,1)} %shard_map.234.refs_4_), channel_id=1, source_target_pairs={{0,4},{12,8},{1,5},{13,9},{2,6},{14,10},{3,7},{15,11},{16,20},{28,... | collective-permute-start | bytes 3932168 | tf_op jit(solution)/shard_map/ppermute | solution.py:140
  399.0 53.8 %collective-permute-start.44 = (bf16[640,1024]{1,0:T(8,128)(2,1)}, bf16[640,1024]{1,0:T(8,128)(2,1)}, u32[]{:S(2)}, u32[]{:S(2)}) collective-permute-start(bf16[640,1024]{1,0:T(8,128)(2,1)} %add.301), channel_id=1, source_target_pairs={{4,8},{8,4},{5,9},{9,5},{6,10},{10,6},{7,11},{11,7},{20,24},{24,20... | collective-permute-start | bytes 3932168 | tf_op jit(solution)/shard_map/ppermute | solution.py:145
  404.6 54.1 %collective-permute-start.48 = (bf16[640,512]{1,0:T(8,128)(2,1)}, bf16[640,512]{1,0:T(8,128)(2,1)}, u32[]{:S(2)}, u32[]{:S(2)}) collective-permute-start(bf16[640,512]{1,0:T(8,128)(2,1)} %pad_maximum_fusion.10.refs_0_), channel_id=1, source_target_pairs={{0,16},{16,0},{1,17},{17,1},{2,18},{18,2},{3,19},{19,3},{4,20},{20... | collective-permute-start | bytes 1966088 | tf_op jit(solution)/shard_map/ppermute | solution.py:43
  423.3 43.9 %collective-permute-start.52 = (bf16[512,512]{1,0:T(8,128)(2,1)}, bf16[512,512]{1,0:T(8,128)(2,1)}, u32[]{:S(2)}, u32[]{:S(2)}) collective-permute-start(bf16[512,512]{1,0:T(8,128)(2,1)} %get-tuple-element.62), channel_id=1, source_target_pairs={{0,16},{16,0},{1,17},{17,1},{2,18},{18,2},{3,19},{19,3},{4,20},{20... | collective-permute-start | bytes 1572872 | tf_op jit(solution)/shard_map/ppermute | solution.py:43
  448.2 83.0 %collective-permute-start.34 = (bf16[2,256,2048]{2,1,0:T(8,128)(2,1)}, bf16[2,256,2048]{2,1,0:T(8,128)(2,1)}, u32[]{:S(2)}, u32[]{:S(2)}) collective-permute-start(bf16[2,256,2048]{2,1,0:T(8,128)(2,1)} %bitcast.122), channel_id=1, source_target_pairs={{0,1},{1,0},{2,3},{3,2},{4,5},{5,4},{6,7},{7,6},{8,9},{9,8},{10,11... | collective-permute-start | bytes 6291464 | tf_op jit(solution)/shard_map/ppermute | solution.py:43
  452.8 20.1 %collective-permute-start.53 = (bf16[256,1024]{1,0:T(8,128)(2,1)}, bf16[256,1024]{1,0:T(8,128)(2,1)}, u32[]{:S(2)}, u32[]{:S(2)}) collective-permute-start(bf16[256,1024]{1,0:T(8,128)(2,1)} %slice.126), channel_id=1, source_target_pairs={{0,16},{16,0},{1,17},{17,1},{2,18},{18,2},{3,19},{19,3},{4,20},{20... | collective-permute-start | bytes 1572872 | tf_op jit(solution)/shard_map/ppermute | solution.py:43
  454.5 54.7 %collective-permute-start.56 = (bf16[1024,640]{1,0:T(8,128)(2,1)}, bf16[1024,640]{1,0:T(8,128)(2,1)}, u32[]{:S(2)}, u32[]{:S(2)}) collective-permute-start(bf16[1024,640]{1,0:T(8,128)(2,1)} %add.310), channel_id=1, source_target_pairs={{4,8},{8,4},{5,9},{9,5},{6,10},{10,6},{7,11},{11,7},{20,24},{24,20... | collective-permute-start | bytes 3932168 | tf_op jit(solution)/shard_map/ppermute | solution.py:145
  464.5 50.9 %collective-permute-start.57 = (bf16[640,1024]{1,0:T(8,128)(2,1)}, bf16[640,1024]{1,0:T(8,128)(2,1)}, u32[]{:S(2)}, u32[]{:S(2)}) collective-permute-start(bf16[640,1024]{1,0:T(8,128)(2,1)} %add.302.refs_2_.refs_0_), channel_id=1, source_target_pairs={{4,0},{8,12},{5,1},{9,13},{6,2},{10,14},{7,3},{11,15},{20,16},{24,... | collective-permute-start | bytes 3932168 | tf_op jit(solution)/shard_map/ppermute | solution.py:146
  467.2 50.7 %collective-permute-start.55 = (bf16[1024,640]{1,0:T(8,128)(2,1)}, bf16[1024,640]{1,0:T(8,128)(2,1)}, u32[]{:S(2)}, u32[]{:S(2)}) collective-permute-start(bf16[1024,640]{1,0:T(8,128)(2,1)} %shard_map.248.refs_1_), channel_id=1, source_target_pairs={{0,4},{12,8},{1,5},{13,9},{2,6},{14,10},{3,7},{15,11},{16,20},{28,... | collective-permute-start | bytes 3932168 | tf_op jit(solution)/shard_map/ppermute | solution.py:140
  475.0 49.8 %collective-permute-start.46 = (bf16[256,1024]{1,0:T(8,128)(2,1)}, bf16[256,1024]{1,0:T(8,128)(2,1)}, u32[]{:S(2)}, u32[]{:S(2)}) collective-permute-start(bf16[256,1024]{1,0:T(8,128)(2,1)} %slice.125), channel_id=1, source_target_pairs={{0,16},{16,0},{1,17},{17,1},{2,18},{18,2},{3,19},{19,3},{4,20},{20... | collective-permute-start | bytes 1572872 | tf_op jit(solution)/shard_map/ppermute | solution.py:43
  515.4 44.9 %collective-permute-start.60 = (bf16[1024,640]{1,0:T(8,128)(2,1)}, bf16[1024,640]{1,0:T(8,128)(2,1)}, u32[]{:S(2)}, u32[]{:S(2)}) collective-permute-start(bf16[1024,640]{1,0:T(8,128)(2,1)} %add.311.refs_2_.refs_0_), channel_id=1, source_target_pairs={{4,0},{8,12},{5,1},{9,13},{6,2},{10,14},{7,3},{11,15},{20,16},{24,... | collective-permute-start | bytes 3932168 | tf_op jit(solution)/shard_map/ppermute | solution.py:146
  517.9 27.0 %collective-permute-start.58 = (bf16[512,1024]{1,0:T(8,128)(2,1)}, bf16[512,1024]{1,0:T(8,128)(2,1)S(1)}, u32[]{:S(2)}, u32[]{:S(2)}) collective-permute-start(bf16[512,1024]{1,0:T(8,128)(2,1)} %shard_map.254), channel_id=1, source_target_pairs={{0,4},{12,8},{1,5},{13,9},{2,6},{14,10},{3,7},{15,11},{16,20},{28,... | collective-permute-start | bytes 3145736 | tf_op jit(solution)/shard_map/ppermute | solution.py:140
  521.9 33.9 %collective-permute-start.59 = (bf16[1024,640]{1,0:T(8,128)(2,1)}, bf16[1024,640]{1,0:T(8,128)(2,1)}, u32[]{:S(2)}, u32[]{:S(2)}) collective-permute-start(bf16[1024,640]{1,0:T(8,128)(2,1)} %add.312), channel_id=1, source_target_pairs={{4,8},{8,4},{5,9},{9,5},{6,10},{10,6},{7,11},{11,7},{20,24},{24,20... | collective-permute-start | bytes 3932168 | tf_op jit(solution)/shard_map/ppermute | solution.py:145
  534.4 27.4 %collective-permute-start.37 = (bf16[2,128,1024]{2,1,0:T(8,128)(2,1)S(1)}, bf16[2,128,1024]{2,1,0:T(8,128)(2,1)}, u32[]{:S(2)}, u32[]{:S(2)}) collective-permute-start(bf16[2,128,1024]{2,1,0:T(8,128)(2,1)S(1)} %split.155), channel_id=1, source_target_pairs={{0,2},{1,3},{2,0},{3,1},{4,6},{5,7},{6,4},{7,5},{8,10},{9,11},{10,... | collective-permute-start | bytes 1572872 | tf_op jit(solution)/shard_map/ppermute | solution.py:43
  546.3 30.8 %collective-permute-start.62 = (bf16[512,1024]{1,0:T(8,128)(2,1)}, bf16[512,1024]{1,0:T(8,128)(2,1)}, u32[]{:S(2)}, u32[]{:S(2)}) collective-permute-start(bf16[512,1024]{1,0:T(8,128)(2,1)} %add.314), channel_id=1, source_target_pairs={{4,8},{8,4},{5,9},{9,5},{6,10},{10,6},{7,11},{11,7},{20,24},{24,20... | collective-permute-start | bytes 3145736 | tf_op jit(solution)/shard_map/ppermute | solution.py:145
  557.8 27.6 %collective-permute-start.63 = (bf16[1024,640]{1,0:T(8,128)(2,1)S(1)}, bf16[1024,640]{1,0:T(8,128)(2,1)}, u32[]{:S(2)}, u32[]{:S(2)}) collective-permute-start(bf16[1024,640]{1,0:T(8,128)(2,1)S(1)} %add.313.refs_2_.refs_0_), channel_id=1, source_target_pairs={{4,0},{8,12},{5,1},{9,13},{6,2},{10,14},{7,3},{11,15},{20,16},{24,... | collective-permute-start | bytes 3932168 | tf_op jit(solution)/shard_map/ppermute | solution.py:146
  560.3 21.9 %collective-permute-start.61 = (bf16[512,640]{1,0:T(8,128)(2,1)}, bf16[512,640]{1,0:T(8,128)(2,1)}, u32[]{:S(2)}, u32[]{:S(2)}) collective-permute-start(bf16[512,640]{1,0:T(8,128)(2,1)} %shard_map.255), channel_id=1, source_target_pairs={{0,4},{12,8},{1,5},{13,9},{2,6},{14,10},{3,7},{15,11},{16,20},{28,... | collective-permute-start | bytes 1966088 | tf_op jit(solution)/shard_map/ppermute | solution.py:140
  587.7 19.9 %collective-permute-start.39 = (bf16[128,2048]{1,0:T(8,128)(2,1)}, bf16[128,2048]{1,0:T(8,128)(2,1)}, u32[]{:S(2)}, u32[]{:S(2)}) collective-permute-start(bf16[128,2048]{1,0:T(8,128)(2,1)} %fusion.1), channel_id=1, source_target_pairs={{0,2},{1,3},{2,0},{3,1},{4,6},{5,7},{6,4},{7,5},{8,10},{9,11},{10,... | collective-permute-start | bytes 1572872 | tf_op jit(solution)/shard_map/ppermute | solution.py:43
  594.2 48.5 %collective-permute-start.45 = (bf16[256,2048]{1,0:T(8,128)(2,1)}, bf16[256,2048]{1,0:T(8,128)(2,1)}, u32[]{:S(2)}, u32[]{:S(2)}) collective-permute-start(bf16[256,2048]{1,0:T(8,128)(2,1)} %shard_map.249.first), channel_id=1, source_target_pairs={{0,1},{1,0},{2,3},{3,2},{4,5},{5,4},{6,7},{7,6},{8,9},{9,8},{10,11... | collective-permute-start | bytes 3145736 | tf_op jit(solution)/shard_map/ppermute | solution.py:43
  595.4 64.0 %collective-permute-start.69 = (bf16[512,1024]{1,0:T(8,128)(2,1)S(1)}, bf16[512,1024]{1,0:T(8,128)(2,1)}, u32[]{:S(2)}, u32[]{:S(2)}) collective-permute-start(bf16[512,1024]{1,0:T(8,128)(2,1)S(1)} %copy-done.15), channel_id=1, source_target_pairs={{4,0},{8,12},{5,1},{9,13},{6,2},{10,14},{7,3},{11,15},{20,16},{24,... | collective-permute-start | bytes 3145736 | tf_op jit(solution)/shard_map/ppermute | solution.py:146
  599.6 19.6 %collective-permute-start.67 = (bf16[512,640]{1,0:T(8,128)(2,1)S(1)}, bf16[512,640]{1,0:T(8,128)(2,1)S(1)}, u32[]{:S(2)}, u32[]{:S(2)}) collective-permute-start(bf16[512,640]{1,0:T(8,128)(2,1)S(1)} %add.318), channel_id=1, source_target_pairs={{4,8},{8,4},{5,9},{9,5},{6,10},{10,6},{7,11},{11,7},{20,24},{24,20... | collective-permute-start | bytes 1966088 | tf_op jit(solution)/shard_map/ppermute | solution.py:145
  604.3 27.5 %collective-permute-start.65 = (bf16[528,640]{1,0:T(8,128)(2,1)}, bf16[528,640]{1,0:T(8,128)(2,1)}, u32[]{:S(2)}, u32[]{:S(2)}) collective-permute-start(bf16[528,640]{1,0:T(8,128)(2,1)} %add.316), channel_id=1, source_target_pairs={{4,8},{8,4},{5,9},{9,5},{6,10},{10,6},{7,11},{11,7},{20,24},{24,20... | collective-permute-start | bytes 2027528 | tf_op jit(solution)/shard_map/ppermute | solution.py:145
  608.9 52.2 %collective-permute-start.40 = (bf16[256,2048]{1,0:T(8,128)(2,1)S(1)}, bf16[256,2048]{1,0:T(8,128)(2,1)}, u32[]{:S(2)}, u32[]{:S(2)}) collective-permute-start(bf16[256,2048]{1,0:T(8,128)(2,1)S(1)} %pad_maximum_fusion.7.first), channel_id=1, source_target_pairs={{0,1},{1,0},{2,3},{3,2},{4,5},{5,4},{6,7},{7,6},{8,9},{9,8},{10,11... | collective-permute-start | bytes 3145736 | tf_op jit(solution)/shard_map/ppermute | solution.py:43
  619.4 41.5 %collective-permute-start.68 = (bf16[512,640]{1,0:T(8,128)(2,1)S(1)}, bf16[512,640]{1,0:T(8,128)(2,1)}, u32[]{:S(2)}, u32[]{:S(2)}) collective-permute-start(bf16[512,640]{1,0:T(8,128)(2,1)S(1)} %add.319), channel_id=1, source_target_pairs={{4,0},{8,12},{5,1},{9,13},{6,2},{10,14},{7,3},{11,15},{20,16},{24,... | collective-permute-start | bytes 1966088 | tf_op jit(solution)/shard_map/ppermute | solution.py:146
  634.1 31.7 %collective-permute-start.66 = (bf16[528,640]{1,0:T(8,128)(2,1)}, bf16[528,640]{1,0:T(8,128)(2,1)}, u32[]{:S(2)}, u32[]{:S(2)}) collective-permute-start(bf16[528,640]{1,0:T(8,128)(2,1)} %add.317), channel_id=1, source_target_pairs={{4,0},{8,12},{5,1},{9,13},{6,2},{10,14},{7,3},{11,15},{20,16},{24,... | collective-permute-start | bytes 2027528 | tf_op jit(solution)/shard_map/ppermute | solution.py:146
  (119 other events, 927.3 us)
Sparse Core Ops, SparseCore 0:
  83.6 36.3 all-gather.5
  121.6 35.9 all-gather.7
  202.6 34.4 reduce-scatter.7
  239.9 34.2 reduce-scatter.3
  275.6 45.8 all-gather.9
  324.2 48.2 reduce-scatter.5
  383.9 57.7 all-gather.11
  443.3 47.5 all-gather.13

commit v5 on v4

--- a/solution.py
+++ b/solution.py
@@ -234,18 +234,19 @@
         values = kv[tile, HD:]
         key_code = k_code[tile]
         allowed = (key_code <= code) & (key_code >= base)
-        key_term = dkv[tile, :HD]
-        value_term = dkv[tile, HD:]
+        all_probs, all_scores = [], []
         for h in range(heads):
             scores = dot(keys, q[h], 0, 0) - lse[h : h + 1]
             probs = jnp.exp(jnp.where(allowed, scores, NEGATIVE))
             grad_probs = dot(values, upstream[h], 0, 0)
             grad_scores = (probs * (grad_probs - centre[h : h + 1])).astype(jnp.bfloat16)
-            value_term = value_term + dot(upstream[h], probs.astype(jnp.bfloat16), 1, 1)
-            key_term = key_term + dot(q[h], grad_scores, 1, 1)
+            all_probs.append(probs.astype(jnp.bfloat16))
+            all_scores.append(grad_scores)
             dq[h] += dot(keys, grad_scores, 1, 0)
-        dkv[tile, :HD] = key_term
-        dkv[tile, HD:] = value_term
+        join = lambda parts: jnp.concatenate(parts, axis=1)
+        every = range(heads)
+        dkv[tile, :HD] += dot(join([q[h] for h in every]), join(all_scores), 1, 1)
+        dkv[tile, HD:] += dot(join([upstream[h] for h in every]), join(all_probs), 1, 1)
         return carry
 
     lax.fori_loop(0, count[step], body, 0)
@@ -358,7 +359,7 @@
     parts = len(gate_w)
     count, width = rows.shape
     units = gate_w[0].shape[1]
-    block = 256
+    block = 384 if units % 384 == 0 else 256
     out = pl.BlockSpec((count, block), lambda i, *_: (0, i))
     tall = [pl.BlockSpec((w.shape[0], block), lambda i, *_: (0, i)) for w in gate_w]
     return pl.pallas_call(
@@ -475,6 +476,8 @@
     parts = len(lefts)
     count = lefts[0].shape[0]
     block = TILE if tall % 256 or lefts[0].shape[1] % 256 else 256
+    if tall % 512 == 0 and lefts[0].shape[1] % 512 == 0:
+        block = 512
     return pl.pallas_call(
         functools.partial(weigh_kernel, parts, at_left, at_right, wide),
         grid_spec=pltpu.PrefetchScalarGridSpec(

time: 688 us -> 691 us (level)
  Pallas kernels: 193 us -> 180 us
  starting transfers between devices: 99.1 us -> 108 us
  waiting for transfers between devices: 205 us -> 213 us
    pallas_call x1, Pallas kernels: 30.5 us -> 20.7 us  [attend_back(): pl.pallas_call(functools.partial(attend_back_kernel, heads), grid_spec=pl...]
    ppermute x6, starting transfers between devices: 14.5 us -> 22.8 us  [shift(): return lax.ppermute(value, axis, pairs)]
  transfers between devices with their start and end apart: 78 -> 78, of which waited for: 33 -> 33; matrix products, arithmetic and copies ran while one was open for 21% -> 21% of each run, Pallas kernels for 23% -> 20%
where the time goes in v5:
time: 691 us; the launch traced here: 682 us
  waiting for transfers between devices  213 us (31%)
  Pallas kernels  180 us (26%)
  starting transfers between devices  108 us (16%)
  other arithmetic  102 us (15%)
  local copies, waits for them, and re-layouts  52.5 us (8%)
  between operations  16.1 us (2%)
  matrix products  9.48 us (1%)
    ppermute x46, waiting for transfers between devices, swap(): return lax.ppermute(value, axis, pairs)  93.4 us
    ppermute x6, waiting for transfers between devices, land(): self.total.append(inward + lax.ppermute(inward, 'ctx', [(1, 2), (2, 1)]))  66.5 us
    pallas_call x6, Pallas kernels, project(): pl.pallas_call(functools.partial(project_kernel, parts, factors, steps, o...  41.9 us
    ppermute x46, starting transfers between devices, swap(): return lax.ppermute(value, axis, pairs)  41.7 us
    pallas_call x6, Pallas kernels, weigh(): pl.pallas_call(functools.partial(weigh_kernel, parts, at_left, at_right,...  36 us
    ppermute x6, starting transfers between devices, shift(): return lax.ppermute(value, axis, pairs)  22.8 us
    pallas_call x1, Pallas kernels, attend_back(): pl.pallas_call(functools.partial(attend_back_kernel, heads), grid_spec=pl...  20.7 us
    pallas_call x2, Pallas kernels, middle(): pl.pallas_call(functools.partial(middle_kernel, parts), grid_spec=pltpu.P...  20 us
  transfers between devices with their start and end apart: 78, of which 33 were waited for; matrix products, arithmetic and copies ran while one was open for 21% of the time, Pallas kernels for 20%

profile of v5, /device:TPU:8, one launch (start us, length us, event | category | flops | bytes accessed | tf_op | source)
XLA Modules:
  0.0 681.5 jit_solution(1259346037007428821)
XLA Ops:
  26.0 4.1 multiply_convert_fusion.rows
  30.1 13.4 %collective-permute-done.1.refs_1_.refs_2_ = bf16[1024,640]{1,0:T(8,128)(2,1)} collective-permute-done((bf16[1024,640]{1,0:T(8,128)(2,1)S(1)}, bf16[1024,640]{1,0:T(8,128)(2,1)}, u32[]{:S(2)}, u32[]{:S(2)}) %collective-permute-start.1) | collective-permute-done | bytes 1310752 | tf_op jit(solution)/shard_map/ppermute | solution.py:43
  43.5 8.0 %shard_map.195 = (bf16[512,512]{1,0:T(8,128)(2,1)}, bf16[4,128,128]{2,1,0:T(8,128)(2,1)}) custom-call(s32[5]{0:T(128)} %stack.87.places.refs_0_, bf16[512,2048]{1,0:T(8,128)(2,1)} %multiply_convert_fusion.rows, f32[32,512]{1,0:T(8,128)} %get-tuple-element.118.cosine, f32[32,512]{1,0:T(8,128)} %get-tuple-element.117.sine, bf16[1024,640]{1,0:T(8,128)(2,1)} %copy-done.13, ...), custom_call_target="tpu_custom_call" | custom-call | flops 1000000 | bytes 100000 | tf_op jit(solution)/shard_map/pallas_call | solution.py:557
  68.4 8.9 %shard_map.196 = (f32[8,64,512]{2,1,0:T(8,128)}, f32[8,512]{1,0:T(8,128)}) custom-call(s32[4]{0:T(128)} %convert_reduce_fusion.count, s32[4,16]{1,0:T(4,128)} %select_reduce_fusion.tiles, bf16[8,64,512]{2,1,0:T(8,128)(2,1)} %bitcast.132, bf16[16,128,128]{2,1,0:T(8,128)(2,1)} %copy-done.54, s32[1,512]{1,0:T(1,128)} %copy-done.79, s32[1,512]{1,0:T(1,128)} %copy-done.80, ...), custom_call_target="tpu_custom_call" | custom-call | flops 1000000 | bytes 100000 | tf_op jit(solution)/shard_map/pallas_call | solution.py:193
  77.3 5.4 collective-permute-done.13.refs_1_
  85.7 5.7 shard_map.198
  102.1 6.2 collective-permute-done.9
  122.0 6.8 collective-permute-done.7
  131.5 4.4 collective-permute-done.11.refs_3_.refs_1_.refs_2_
  139.4 6.4 shard_map.203.refs_2_.grads
  150.4 6.3 shard_map.205.refs_1_.grads
  168.8 10.0 %shard_map.207 = (bf16[512,768]{1,0:T(8,128)(2,1)}, bf16[512,768]{1,0:T(8,128)(2,1)}, bf16[512,768]{1,0:T(8,128)(2,1)}) custom-call(s32[5]{0:T(128)} %stack.87.places.refs_0_, bf16[512,2048]{1,0:T(8,128)(2,1)} %bitcast.109, f32[512,768]{1,0:T(8,128)} %shard_map.205.refs_1_.grads, bf16[1024,768]{1,0:T(8,128)(2,1)} %constant_dynamic-slice_fusion.7.refs_0_.refs_2_, ...), custom_call_target="tpu_custom_call" | custom-call | flops 1000000 | bytes 16605000 | tf_op jit(solution)/shard_map/pallas_call | solution.py:365
  178.8 8.6 %shard_map.209 = bf16[512,2048]{1,0:T(8,128)(2,1)} custom-call(s32[5]{0:T(128)} %shard_map.208.places.refs_0_, bf16[512,768]{1,0:T(8,128)(2,1)} %get-tuple-element.46.refs_0_.refs_3_, bf16[512,768]{1,0:T(8,128)(2,1)} %get-tuple-element.47.refs_1_.refs_3_, bf16[1024,768]{1,0:T(8,128)(2,1)} %constant_dynamic-slice_fusion.7.refs_0_.refs_2_, ...), custom_call_target="tpu_custom_call" | custom-call | flops 1000000 | bytes 11070000 | tf_op jit(solution)/shard_map/pallas_call | solution.py:416
  187.4 10.0 %shard_map.211 = (bf16[512,768]{1,0:T(8,128)(2,1)}, bf16[512,768]{1,0:T(8,128)(2,1)}, bf16[512,768]{1,0:T(8,128)(2,1)}) custom-call(s32[5]{0:T(128)} %shard_map.210.places.refs_0_, bf16[512,2048]{1,0:T(8,128)(2,1)} %bitcast.104, f32[512,768]{1,0:T(8,128)} %shard_map.203.refs_2_.grads, bf16[1024,768]{1,0:T(8,128)(2,1)} %constant_dynamic-slice_fusion.7.refs_0_.refs_2_, ...), custom_call_target="tpu_custom_call" | custom-call | flops 1000000 | bytes 16605000 | tf_op jit(solution)/shard_map/pallas_call | solution.py:365
  197.4 6.7 shard_map.213.refs_1_
  205.8 8.6 %shard_map.215 = bf16[512,2048]{1,0:T(8,128)(2,1)} custom-call(s32[5]{0:T(128)} %shard_map.214.places.refs_0_, bf16[512,768]{1,0:T(8,128)(2,1)} %get-tuple-element.49.refs_0_.refs_2_, bf16[512,768]{1,0:T(8,128)(2,1)} %get-tuple-element.50.refs_1_.refs_2_, bf16[1024,768]{1,0:T(8,128)(2,1)} %constant_dynamic-slice_fusion.7.refs_0_.refs_2_, ...), custom_call_target="tpu_custom_call" | custom-call | flops 1000000 | bytes 11070000 | tf_op jit(solution)/shard_map/pallas_call | solution.py:416
  219.1 5.3 shard_map.217.refs_2_.refs_1_
  226.6 12.6 %collective-permute-done.20.refs_0_ = bf16[1,256,1024]{2,1,0:T(8,128)(2,1)} collective-permute-done((bf16[1,256,1024]{2,1,0:T(8,128)(2,1)}, bf16[1,256,1024]{2,1,0:T(8,128)(2,1)}, u32[]{:S(2)}, u32[]{:S(2)}) %collective-permute-start.20) | collective-permute-done | bytes 524320 | tf_op jit(solution)/shard_map/ppermute | solution.py:43
  247.1 7.8 %shard_map.220.refs_1_ = bf16[640,1024]{1,0:T(8,128)(2,1)} custom-call(s32[5]{0:T(128)} %shard_map.219.places.refs_0_, bf16[512,768]{1,0:T(8,128)(2,1)} %get-tuple-element.48.refs_1_.refs_0_, bf16[512,768]{1,0:T(8,128)(2,1)} %get-tuple-element.45.refs_1_.refs_0_, bf16[512,2048]{1,0:T(8,128)(2,1)} %pad_maximum_fusion.refs_1_.upstream.refs_2_, ...), custom_call_target="tpu_custom_call" | custom-call | flops 1000000 | bytes 11070000 | tf_op jit(solution)/shard_map/pallas_call | solution.py:481
  262.1 5.5 shard_map.224.refs_1_
  268.6 11.4 %collective-permute-done.24 = bf16[128,2048]{1,0:T(8,128)(2,1)S(1)} collective-permute-done((bf16[128,2048]{1,0:T(8,128)(2,1)S(1)}, bf16[128,2048]{1,0:T(8,128)(2,1)S(1)}, u32[]{:S(2)}, u32[]{:S(2)}) %collective-permute-start.24) | collective-permute-done | bytes 524320 | tf_op jit(solution)/shard_map/ppermute | solution.py:43
  281.9 5.3 shard_map.226.refs_1_
  288.7 10.8 %collective-permute-done.26.refs_1_ = bf16[640,1024]{1,0:T(8,128)(2,1)} collective-permute-done((bf16[640,1024]{1,0:T(8,128)(2,1)S(1)}, bf16[640,1024]{1,0:T(8,128)(2,1)}, u32[]{:S(2)}, u32[]{:S(2)}) %collective-permute-start.26) | collective-permute-done | bytes 1310752 | tf_op jit(solution)/shard_map/ppermute | solution.py:43
  300.8 4.8 shard_map.228
  305.6 20.7 %shard_map.230 = (f32[8,64,512]{2,1,0:T(8,128)}, f32[16,128,128]{2,1,0:T(8,128)}) custom-call(s32[4]{0:T(128)} %convert_reduce_fusion.count, s32[4,16]{1,0:T(4,128)} %select_reduce_fusion.tiles, bf16[8,64,512]{2,1,0:T(8,128)(2,1)} %bitcast.133, bf16[16,128,128]{2,1,0:T(8,128)(2,1)} %copy-done.54, s32[1,512]{1,0:T(1,128)} %copy-done.79, s32[1,512]{1,0:T(1,128)} %copy-done.80, ...), custom_call_target="tpu_custom_call" | custom-call | flops 1000000 | bytes 44280000 | tf_op jit(solution)/shard_map/pallas_call | solution.py:261
  328.5 16.4 %collective-permute-start.27 = (bf16[4,128,128]{2,1,0:T(8,128)(2,1)}, bf16[4,128,128]{2,1,0:T(8,128)(2,1)S(1)}, u32[]{:S(2)}, u32[]{:S(2)}) collective-permute-start(bf16[4,128,128]{2,1,0:T(8,128)(2,1)} %get-tuple-element.92.refs_1_), channel_id=1, source_target_pairs={{0,12},{4,0},{8,4},{12,8},{1,13},{5,1},{9,5},{13,9},{2,14},{6,2},{... | collective-permute-start | bytes 393224 | tf_op jit(solution)/shard_map/ppermute | solution.py:48
  346.9 5.3 shard_map.232.refs_1_.refs_3_
  355.0 5.2 collective-permute-done.28.refs_1_
  360.2 7.1 %collective-permute-done.29.refs_2_ = bf16[4,128,128]{2,1,0:T(8,128)(2,1)} collective-permute-done((bf16[4,128,128]{2,1,0:T(8,128)(2,1)}, bf16[4,128,128]{2,1,0:T(8,128)(2,1)}, u32[]{:S(2)}, u32[]{:S(2)}) %collective-permute-start.29) | collective-permute-done | bytes 131104 | tf_op jit(solution)/shard_map/ppermute | solution.py:48
  367.3 8.8 %reduce-scatter.6.cloned.1.call-done.refs_5_.refs_1_.refs_0_ = bf16[256,768]{1,0:T(8,128)(2,1)} async-done(((bf16[1024,768]{1,0:T(8,128)(2,1)}), bf16[256,768]{1,0:T(8,128)(2,1)}) %reduce-scatter.6.cloned.1.call-update) | async-done | bytes 393232 | tf_op jit(solution)/shard_map/reduce_scatter | solution.py:828
  378.7 6.2 shard_map.236.refs_1_
  402.4 5.3 collective-permute-start.44
  409.3 11.4 %collective-permute-done.42.refs_0_.refs_3_ = bf16[1024,640]{1,0:T(8,128)(2,1)S(1)} collective-permute-done((bf16[1024,640]{1,0:T(8,128)(2,1)}, bf16[1024,640]{1,0:T(8,128)(2,1)S(1)}, u32[]{:S(2)}, u32[]{:S(2)}) %collective-permute-start.42) | collective-permute-done | bytes 1310752 | tf_op jit(solution)/shard_map/ppermute | solution.py:43
  430.2 15.0 %all-gather.12.cloned.1.call-done.refs_1_.kept = bf16[1024,768]{1,0:T(8,128)(2,1)} async-done(((bf16[256,768]{1,0:T(8,128)(2,1)}), bf16[1024,768]{1,0:T(8,128)(2,1)}) %all-gather.12.cloned.1.call-update) | async-done | bytes 1572880 | tf_op jit(solution)/shard_map/all_gather | solution.py:834
  445.1 6.5 shard_map.242
  457.7 4.4 collective-permute-start.56
  481.0 31.6 %collective-permute-done.56 = bf16[1024,640]{1,0:T(8,128)(2,1)} collective-permute-done((bf16[1024,640]{1,0:T(8,128)(2,1)}, bf16[1024,640]{1,0:T(8,128)(2,1)}, u32[]{:S(2)}, u32[]{:S(2)}) %collective-permute-start.56) | collective-permute-done | bytes 1310752 | tf_op jit(solution)/shard_map/ppermute | solution.py:145
  528.5 6.3 shard_map.245
  541.9 6.4 collective-permute-done.58.refs_1_
  554.0 5.4 collective-permute-done.59
  571.2 9.6 %collective-permute-done.62 = bf16[512,1024]{1,0:T(8,128)(2,1)} collective-permute-done((bf16[512,1024]{1,0:T(8,128)(2,1)}, bf16[512,1024]{1,0:T(8,128)(2,1)}, u32[]{:S(2)}, u32[]{:S(2)}) %collective-permute-start.62) | collective-permute-done | bytes 1048608 | tf_op jit(solution)/shard_map/ppermute | solution.py:145
  612.6 10.2 %collective-permute-done.67 = bf16[512,640]{1,0:T(8,128)(2,1)S(1)} collective-permute-done((bf16[512,640]{1,0:T(8,128)(2,1)S(1)}, bf16[512,640]{1,0:T(8,128)(2,1)S(1)}, u32[]{:S(2)}, u32[]{:S(2)}) %collective-permute-start.67) | collective-permute-done | bytes 655392 | tf_op jit(solution)/shard_map/ppermute | solution.py:145
  625.8 9.7 %collective-permute-done.65 = bf16[528,640]{1,0:T(8,128)(2,1)} collective-permute-done((bf16[528,640]{1,0:T(8,128)(2,1)}, bf16[528,640]{1,0:T(8,128)(2,1)}, u32[]{:S(2)}, u32[]{:S(2)}) %collective-permute-start.65) | collective-permute-done | bytes 675872 | tf_op jit(solution)/shard_map/ppermute | solution.py:145
  640.5 5.8 shard_map.259
  646.3 5.2 shard_map.250
  651.5 5.8 shard_map.257
  657.3 5.8 shard_map.258
  664.7 4.8 shard_map.246
  (507 shorter events, 263.7 us)
Async XLA Ops:
  7.2 128.6 %all-gather.6.cloned.1.call-start = ((), (), s32[]{:S(2)}) async-start(), calls=%async_computation.3 | async-start | bytes 1966080 | tf_op jit(solution)/shard_map/all_gather | solution.py:733
  11.6 31.9 %collective-permute-start.1 = (bf16[1024,640]{1,0:T(8,128)(2,1)S(1)}, bf16[1024,640]{1,0:T(8,128)(2,1)}, u32[]{:S(2)}, u32[]{:S(2)}) collective-permute-start(bf16[1024,640]{1,0:T(8,128)(2,1)S(1)} %constant_dynamic-update-slice_fusion.refs_0_.refs_1_), channel_id=1, source_target_pairs={{0,16},{16,0},{1,17},{17,1},{2,18},{18,2},{3,19},{19,3},{4,20},{20... | collective-permute-start | bytes 3932168 | tf_op jit(solution)/shard_map/ppermute | solution.py:43
  23.7 62.0 %collective-permute-start.5 = (bf16[512,1024]{1,0:T(8,128)(2,1)}, bf16[512,1024]{1,0:T(8,128)(2,1)}, u32[]{:S(2)}, u32[]{:S(2)}) collective-permute-start(bf16[512,1024]{1,0:T(8,128)(2,1)} %shard_map.197), channel_id=1, source_target_pairs={{0,16},{16,0},{1,17},{17,1},{2,18},{18,2},{3,19},{19,3},{4,20},{20... | collective-permute-start | bytes 3145736 | tf_op jit(solution)/shard_map/ppermute | solution.py:43
  57.4 20.0 %collective-permute-start.12 = (bf16[256,768]{1,0:T(8,128)(2,1)}, bf16[256,768]{1,0:T(8,128)(2,1)S(1)}, u32[]{:S(2)}, u32[]{:S(2)}) collective-permute-start(bf16[256,768]{1,0:T(8,128)(2,1)} %shard_map.199), channel_id=1, source_target_pairs={{0,16},{16,0},{1,17},{17,1},{2,18},{18,2},{3,19},{19,3},{4,20},{20... | collective-permute-start | bytes 1179656 | tf_op jit(solution)/shard_map/ppermute | solution.py:43
  57.9 24.8 %collective-permute-start.13 = (bf16[256,768]{1,0:T(8,128)(2,1)}, bf16[256,768]{1,0:T(8,128)(2,1)S(1)}, u32[]{:S(2)}, u32[]{:S(2)}) collective-permute-start(bf16[256,768]{1,0:T(8,128)(2,1)} %shard_map.200), channel_id=1, source_target_pairs={{0,16},{16,0},{1,17},{17,1},{2,18},{18,2},{3,19},{19,3},{4,20},{20... | collective-permute-start | bytes 1179656 | tf_op jit(solution)/shard_map/ppermute | solution.py:43
  65.4 28.3 %collective-permute-start.8 = (bf16[128,2048]{1,0:T(8,128)(2,1)S(1)}, bf16[128,2048]{1,0:T(8,128)(2,1)}, u32[]{:S(2)}, u32[]{:S(2)}) collective-permute-start(bf16[128,2048]{1,0:T(8,128)(2,1)S(1)} %copy-done.42), channel_id=1, source_target_pairs={{0,16},{16,0},{1,17},{17,1},{2,18},{18,2},{3,19},{19,3},{4,20},{20... | collective-permute-start | bytes 1572872 | tf_op jit(solution)/shard_map/ppermute | solution.py:43
  83.5 79.5 %all-gather.8.cloned.1.call-start = ((), (), s32[]{:S(2)}) async-start(), calls=%async_computation.4 | async-start | bytes 1966080 | tf_op jit(solution)/shard_map/all_gather | solution.py:733
  99.1 36.7 %collective-permute-start.11 = (bf16[768,1024]{1,0:T(8,128)(2,1)}, bf16[768,1024]{1,0:T(8,128)(2,1)S(1)}, u32[]{:S(2)}, u32[]{:S(2)}) collective-permute-start(bf16[768,1024]{1,0:T(8,128)(2,1)} %get-tuple-element.76), channel_id=1, source_target_pairs={{0,16},{16,0},{1,17},{17,1},{2,18},{18,2},{3,19},{19,3},{4,20},{20... | collective-permute-start | bytes 4718600 | tf_op jit(solution)/shard_map/ppermute | solution.py:43
  118.6 121.9 %reduce-scatter.8.cloned.1.call-start = ((), (), s32[]{:S(2)}) async-start(), calls=%async_computation.7 | async-start | bytes 1966080 | tf_op jit(solution)/shard_map/reduce_scatter | solution.py:828
  204.2 101.4 %reduce-scatter.4.cloned.1.call-start = ((), (), s32[]{:S(2)}) async-start(), calls=%async_computation.5 | async-start | bytes 1966080 | tf_op jit(solution)/shard_map/reduce_scatter | solution.py:828
  224.5 142.8 %all-gather.10.cloned.1.call-start = ((), (), s32[]{:S(2)}) async-start(), calls=%async_computation.8 | async-start | bytes 1966080 | tf_op jit(solution)/shard_map/all_gather | solution.py:834
  240.5 135.5 %reduce-scatter.6.cloned.1.call-start = ((), (), s32[]{:S(2)}) async-start(), calls=%async_computation.6 | async-start | bytes 1966080 | tf_op jit(solution)/shard_map/reduce_scatter | solution.py:828
  267.6 31.9 %collective-permute-start.26 = (bf16[640,1024]{1,0:T(8,128)(2,1)S(1)}, bf16[640,1024]{1,0:T(8,128)(2,1)}, u32[]{:S(2)}, u32[]{:S(2)}) collective-permute-start(bf16[640,1024]{1,0:T(8,128)(2,1)S(1)} %copy-done.11), channel_id=1, source_target_pairs={{0,16},{16,0},{1,17},{17,1},{2,18},{18,2},{3,19},{19,3},{4,20},{20... | collective-permute-start | bytes 3932168 | tf_op jit(solution)/shard_map/ppermute | solution.py:43
  281.9 18.9 %collective-permute-start.25 = (bf16[256,2048]{1,0:T(8,128)(2,1)}, bf16[256,2048]{1,0:T(8,128)(2,1)}, u32[]{:S(2)}, u32[]{:S(2)}) collective-permute-start(bf16[256,2048]{1,0:T(8,128)(2,1)} %pad_maximum_fusion.6.refs_0_), channel_id=1, source_target_pairs={{0,1},{1,0},{2,3},{3,2},{4,5},{5,4},{6,7},{7,6},{8,9},{9,8},{10,11... | collective-permute-start | bytes 3145736 | tf_op jit(solution)/shard_map/ppermute | solution.py:43
  287.2 65.0 %collective-permute-start.30 = (bf16[1024,640]{1,0:T(8,128)(2,1)}, bf16[1024,640]{1,0:T(8,128)(2,1)}, u32[]{:S(2)}, u32[]{:S(2)}) collective-permute-start(bf16[1024,640]{1,0:T(8,128)(2,1)} %shard_map.226.refs_1_), channel_id=1, source_target_pairs={{0,16},{16,0},{1,17},{17,1},{2,18},{18,2},{3,19},{19,3},{4,20},{20... | collective-permute-start | bytes 3932168 | tf_op jit(solution)/shard_map/ppermute | solution.py:43
  299.5 52.7 %collective-permute-start.31 = (bf16[640,1024]{1,0:T(8,128)(2,1)}, bf16[640,1024]{1,0:T(8,128)(2,1)S(1)}, u32[]{:S(2)}, u32[]{:S(2)}) collective-permute-start(bf16[640,1024]{1,0:T(8,128)(2,1)} %collective-permute-done.26.refs_1_), channel_id=1, source_target_pairs={{0,4},{12,8},{1,5},{13,9},{2,6},{14,10},{3,7},{15,11},{16,20},{28,... | collective-permute-start | bytes 3932168 | tf_op jit(solution)/shard_map/ppermute | solution.py:140
  305.6 139.6 %all-gather.12.cloned.1.call-start = ((), (), s32[]{:S(2)}) async-start(), calls=%async_computation.9 | async-start | bytes 1966080 | tf_op jit(solution)/shard_map/all_gather | solution.py:834
  328.5 26.5 %collective-permute-start.27 = (bf16[4,128,128]{2,1,0:T(8,128)(2,1)}, bf16[4,128,128]{2,1,0:T(8,128)(2,1)S(1)}, u32[]{:S(2)}, u32[]{:S(2)}) collective-permute-start(bf16[4,128,128]{2,1,0:T(8,128)(2,1)} %get-tuple-element.92.refs_1_), channel_id=1, source_target_pairs={{0,12},{4,0},{8,4},{12,8},{1,13},{5,1},{9,5},{13,9},{2,14},{6,2},{... | collective-permute-start | bytes 393224 | tf_op jit(solution)/shard_map/ppermute | solution.py:48
  344.9 22.4 %collective-permute-start.29 = (bf16[4,128,128]{2,1,0:T(8,128)(2,1)}, bf16[4,128,128]{2,1,0:T(8,128)(2,1)}, u32[]{:S(2)}, u32[]{:S(2)}) collective-permute-start(bf16[4,128,128]{2,1,0:T(8,128)(2,1)} %get-tuple-element.90.refs_3_), channel_id=1, source_target_pairs={{0,4},{4,8},{8,12},{12,0},{1,5},{5,9},{9,13},{13,1},{2,6},{6,10},{... | collective-permute-start | bytes 393224 | tf_op jit(solution)/shard_map/ppermute | solution.py:48
  387.3 141.2 %all-gather.14.cloned.1.call-start = ((), (), s32[]{:S(2)}) async-start(), calls=%async_computation.10 | async-start | bytes 1966080 | tf_op jit(solution)/shard_map/all_gather | solution.py:834
  387.4 33.3 %collective-permute-start.42 = (bf16[1024,640]{1,0:T(8,128)(2,1)}, bf16[1024,640]{1,0:T(8,128)(2,1)S(1)}, u32[]{:S(2)}, u32[]{:S(2)}) collective-permute-start(bf16[1024,640]{1,0:T(8,128)(2,1)} %shard_map.232.refs_1_.refs_3_), channel_id=1, source_target_pairs={{0,16},{16,0},{1,17},{17,1},{2,18},{18,2},{3,19},{19,3},{4,20},{20... | collective-permute-start | bytes 3932168 | tf_op jit(solution)/shard_map/ppermute | solution.py:43
  392.9 28.9 %collective-permute-start.33 = (bf16[128,2048]{1,0:T(8,128)(2,1)S(1)}, bf16[128,2048]{1,0:T(8,128)(2,1)}, u32[]{:S(2)}, u32[]{:S(2)}) collective-permute-start(bf16[128,2048]{1,0:T(8,128)(2,1)S(1)} %slice_bitcast_fusion.2.refs_1_), channel_id=1, source_target_pairs={{0,2},{1,3},{2,0},{3,1},{4,6},{5,7},{6,4},{7,5},{8,10},{9,11},{10,... | collective-permute-start | bytes 1572872 | tf_op jit(solution)/shard_map/ppermute | solution.py:43
  396.9 54.9 %collective-permute-start.43 = (bf16[1024,640]{1,0:T(8,128)(2,1)}, bf16[1024,640]{1,0:T(8,128)(2,1)}, u32[]{:S(2)}, u32[]{:S(2)}) collective-permute-start(bf16[1024,640]{1,0:T(8,128)(2,1)} %shard_map.234.refs_4_), channel_id=1, source_target_pairs={{0,4},{12,8},{1,5},{13,9},{2,6},{14,10},{3,7},{15,11},{16,20},{28,... | collective-permute-start | bytes 3932168 | tf_op jit(solution)/shard_map/ppermute | solution.py:140
  402.4 53.7 %collective-permute-start.44 = (bf16[640,1024]{1,0:T(8,128)(2,1)}, bf16[640,1024]{1,0:T(8,128)(2,1)}, u32[]{:S(2)}, u32[]{:S(2)}) collective-permute-start(bf16[640,1024]{1,0:T(8,128)(2,1)} %add.301), channel_id=1, source_target_pairs={{4,8},{8,4},{5,9},{9,5},{6,10},{10,6},{7,11},{11,7},{20,24},{24,20... | collective-permute-start | bytes 3932168 | tf_op jit(solution)/shard_map/ppermute | solution.py:145
  407.8 54.3 %collective-permute-start.48 = (bf16[640,512]{1,0:T(8,128)(2,1)}, bf16[640,512]{1,0:T(8,128)(2,1)}, u32[]{:S(2)}, u32[]{:S(2)}) collective-permute-start(bf16[640,512]{1,0:T(8,128)(2,1)} %pad_maximum_fusion.10.refs_0_), channel_id=1, source_target_pairs={{0,16},{16,0},{1,17},{17,1},{2,18},{18,2},{3,19},{19,3},{4,20},{20... | collective-permute-start | bytes 1966088 | tf_op jit(solution)/shard_map/ppermute | solution.py:43
  428.2 42.4 %collective-permute-start.52 = (bf16[512,512]{1,0:T(8,128)(2,1)}, bf16[512,512]{1,0:T(8,128)(2,1)}, u32[]{:S(2)}, u32[]{:S(2)}) collective-permute-start(bf16[512,512]{1,0:T(8,128)(2,1)} %get-tuple-element.62), channel_id=1, source_target_pairs={{0,16},{16,0},{1,17},{17,1},{2,18},{18,2},{3,19},{19,3},{4,20},{20... | collective-permute-start | bytes 1572872 | tf_op jit(solution)/shard_map/ppermute | solution.py:43
  451.6 83.2 %collective-permute-start.34 = (bf16[2,256,2048]{2,1,0:T(8,128)(2,1)}, bf16[2,256,2048]{2,1,0:T(8,128)(2,1)}, u32[]{:S(2)}, u32[]{:S(2)}) collective-permute-start(bf16[2,256,2048]{2,1,0:T(8,128)(2,1)} %bitcast.122), channel_id=1, source_target_pairs={{0,1},{1,0},{2,3},{3,2},{4,5},{5,4},{6,7},{7,6},{8,9},{9,8},{10,11... | collective-permute-start | bytes 6291464 | tf_op jit(solution)/shard_map/ppermute | solution.py:43
  456.2 20.1 %collective-permute-start.53 = (bf16[256,1024]{1,0:T(8,128)(2,1)}, bf16[256,1024]{1,0:T(8,128)(2,1)}, u32[]{:S(2)}, u32[]{:S(2)}) collective-permute-start(bf16[256,1024]{1,0:T(8,128)(2,1)} %slice.126), channel_id=1, source_target_pairs={{0,16},{16,0},{1,17},{17,1},{2,18},{18,2},{3,19},{19,3},{4,20},{20... | collective-permute-start | bytes 1572872 | tf_op jit(solution)/shard_map/ppermute | solution.py:43
  457.7 54.9 %collective-permute-start.56 = (bf16[1024,640]{1,0:T(8,128)(2,1)}, bf16[1024,640]{1,0:T(8,128)(2,1)}, u32[]{:S(2)}, u32[]{:S(2)}) collective-permute-start(bf16[1024,640]{1,0:T(8,128)(2,1)} %add.310), channel_id=1, source_target_pairs={{4,8},{8,4},{5,9},{9,5},{6,10},{10,6},{7,11},{11,7},{20,24},{24,20... | collective-permute-start | bytes 3932168 | tf_op jit(solution)/shard_map/ppermute | solution.py:145
  467.9 50.9 %collective-permute-start.57 = (bf16[640,1024]{1,0:T(8,128)(2,1)}, bf16[640,1024]{1,0:T(8,128)(2,1)}, u32[]{:S(2)}, u32[]{:S(2)}) collective-permute-start(bf16[640,1024]{1,0:T(8,128)(2,1)} %add.302.refs_2_.refs_0_), channel_id=1, source_target_pairs={{4,0},{8,12},{5,1},{9,13},{6,2},{10,14},{7,3},{11,15},{20,16},{24,... | collective-permute-start | bytes 3932168 | tf_op jit(solution)/shard_map/ppermute | solution.py:146
  470.6 50.7 %collective-permute-start.55 = (bf16[1024,640]{1,0:T(8,128)(2,1)}, bf16[1024,640]{1,0:T(8,128)(2,1)}, u32[]{:S(2)}, u32[]{:S(2)}) collective-permute-start(bf16[1024,640]{1,0:T(8,128)(2,1)} %shard_map.248.refs_1_), channel_id=1, source_target_pairs={{0,4},{12,8},{1,5},{13,9},{2,6},{14,10},{3,7},{15,11},{16,20},{28,... | collective-permute-start | bytes 3932168 | tf_op jit(solution)/shard_map/ppermute | solution.py:140
  478.4 50.1 %collective-permute-start.46 = (bf16[256,1024]{1,0:T(8,128)(2,1)}, bf16[256,1024]{1,0:T(8,128)(2,1)}, u32[]{:S(2)}, u32[]{:S(2)}) collective-permute-start(bf16[256,1024]{1,0:T(8,128)(2,1)} %slice.125), channel_id=1, source_target_pairs={{0,16},{16,0},{1,17},{17,1},{2,18},{18,2},{3,19},{19,3},{4,20},{20... | collective-permute-start | bytes 1572872 | tf_op jit(solution)/shard_map/ppermute | solution.py:43
  518.8 45.1 %collective-permute-start.60 = (bf16[1024,640]{1,0:T(8,128)(2,1)}, bf16[1024,640]{1,0:T(8,128)(2,1)}, u32[]{:S(2)}, u32[]{:S(2)}) collective-permute-start(bf16[1024,640]{1,0:T(8,128)(2,1)} %add.311.refs_2_.refs_0_), channel_id=1, source_target_pairs={{4,0},{8,12},{5,1},{9,13},{6,2},{10,14},{7,3},{11,15},{20,16},{24,... | collective-permute-start | bytes 3932168 | tf_op jit(solution)/shard_map/ppermute | solution.py:146
  521.3 27.0 %collective-permute-start.58 = (bf16[512,1024]{1,0:T(8,128)(2,1)}, bf16[512,1024]{1,0:T(8,128)(2,1)S(1)}, u32[]{:S(2)}, u32[]{:S(2)}) collective-permute-start(bf16[512,1024]{1,0:T(8,128)(2,1)} %shard_map.254), channel_id=1, source_target_pairs={{0,4},{12,8},{1,5},{13,9},{2,6},{14,10},{3,7},{15,11},{16,20},{28,... | collective-permute-start | bytes 3145736 | tf_op jit(solution)/shard_map/ppermute | solution.py:140
  525.6 33.9 %collective-permute-start.59 = (bf16[1024,640]{1,0:T(8,128)(2,1)}, bf16[1024,640]{1,0:T(8,128)(2,1)}, u32[]{:S(2)}, u32[]{:S(2)}) collective-permute-start(bf16[1024,640]{1,0:T(8,128)(2,1)} %add.312), channel_id=1, source_target_pairs={{4,8},{8,4},{5,9},{9,5},{6,10},{10,6},{7,11},{11,7},{20,24},{24,20... | collective-permute-start | bytes 3932168 | tf_op jit(solution)/shard_map/ppermute | solution.py:145
  538.1 27.2 %collective-permute-start.37 = (bf16[2,128,1024]{2,1,0:T(8,128)(2,1)S(1)}, bf16[2,128,1024]{2,1,0:T(8,128)(2,1)}, u32[]{:S(2)}, u32[]{:S(2)}) collective-permute-start(bf16[2,128,1024]{2,1,0:T(8,128)(2,1)S(1)} %split.155), channel_id=1, source_target_pairs={{0,2},{1,3},{2,0},{3,1},{4,6},{5,7},{6,4},{7,5},{8,10},{9,11},{10,... | collective-permute-start | bytes 1572872 | tf_op jit(solution)/shard_map/ppermute | solution.py:43
  549.7 31.1 %collective-permute-start.62 = (bf16[512,1024]{1,0:T(8,128)(2,1)}, bf16[512,1024]{1,0:T(8,128)(2,1)}, u32[]{:S(2)}, u32[]{:S(2)}) collective-permute-start(bf16[512,1024]{1,0:T(8,128)(2,1)} %add.314), channel_id=1, source_target_pairs={{4,8},{8,4},{5,9},{9,5},{6,10},{10,6},{7,11},{11,7},{20,24},{24,20... | collective-permute-start | bytes 3145736 | tf_op jit(solution)/shard_map/ppermute | solution.py:145
  561.5 27.6 %collective-permute-start.63 = (bf16[1024,640]{1,0:T(8,128)(2,1)S(1)}, bf16[1024,640]{1,0:T(8,128)(2,1)}, u32[]{:S(2)}, u32[]{:S(2)}) collective-permute-start(bf16[1024,640]{1,0:T(8,128)(2,1)S(1)} %add.313.refs_2_.refs_0_), channel_id=1, source_target_pairs={{4,0},{8,12},{5,1},{9,13},{6,2},{10,14},{7,3},{11,15},{20,16},{24,... | collective-permute-start | bytes 3932168 | tf_op jit(solution)/shard_map/ppermute | solution.py:146
  564.0 21.9 %collective-permute-start.61 = (bf16[512,640]{1,0:T(8,128)(2,1)}, bf16[512,640]{1,0:T(8,128)(2,1)}, u32[]{:S(2)}, u32[]{:S(2)}) collective-permute-start(bf16[512,640]{1,0:T(8,128)(2,1)} %shard_map.255), channel_id=1, source_target_pairs={{0,4},{12,8},{1,5},{13,9},{2,6},{14,10},{3,7},{15,11},{16,20},{28,... | collective-permute-start | bytes 1966088 | tf_op jit(solution)/shard_map/ppermute | solution.py:140
  566.7 18.2 %collective-permute-start.38 = (bf16[1,128,1024]{2,1,0:T(8,128)(2,1)S(1)}, bf16[1,128,1024]{2,1,0:T(8,128)(2,1)S(1)}, u32[]{:S(2)}, u32[]{:S(2)}) collective-permute-start(bf16[1,128,1024]{2,1,0:T(8,128)(2,1)S(1)} %split.201), channel_id=1, source_target_pairs={{0,16},{16,0},{1,17},{17,1},{2,18},{18,2},{3,19},{19,3},{4,20},{20... | collective-permute-start | bytes 786440 | tf_op jit(solution)/shard_map/ppermute | solution.py:43
  591.4 19.8 %collective-permute-start.39 = (bf16[128,2048]{1,0:T(8,128)(2,1)}, bf16[128,2048]{1,0:T(8,128)(2,1)}, u32[]{:S(2)}, u32[]{:S(2)}) collective-permute-start(bf16[128,2048]{1,0:T(8,128)(2,1)} %fusion.1), channel_id=1, source_target_pairs={{0,2},{1,3},{2,0},{3,1},{4,6},{5,7},{6,4},{7,5},{8,10},{9,11},{10,... | collective-permute-start | bytes 1572872 | tf_op jit(solution)/shard_map/ppermute | solution.py:43
  597.9 48.5 %collective-permute-start.45 = (bf16[256,2048]{1,0:T(8,128)(2,1)}, bf16[256,2048]{1,0:T(8,128)(2,1)}, u32[]{:S(2)}, u32[]{:S(2)}) collective-permute-start(bf16[256,2048]{1,0:T(8,128)(2,1)} %shard_map.249.first), channel_id=1, source_target_pairs={{0,1},{1,0},{2,3},{3,2},{4,5},{5,4},{6,7},{7,6},{8,9},{9,8},{10,11... | collective-permute-start | bytes 3145736 | tf_op jit(solution)/shard_map/ppermute | solution.py:43
  599.1 64.0 %collective-permute-start.69 = (bf16[512,1024]{1,0:T(8,128)(2,1)S(1)}, bf16[512,1024]{1,0:T(8,128)(2,1)}, u32[]{:S(2)}, u32[]{:S(2)}) collective-permute-start(bf16[512,1024]{1,0:T(8,128)(2,1)S(1)} %copy-done.15), channel_id=1, source_target_pairs={{4,0},{8,12},{5,1},{9,13},{6,2},{10,14},{7,3},{11,15},{20,16},{24,... | collective-permute-start | bytes 3145736 | tf_op jit(solution)/shard_map/ppermute | solution.py:146
  603.3 19.6 %collective-permute-start.67 = (bf16[512,640]{1,0:T(8,128)(2,1)S(1)}, bf16[512,640]{1,0:T(8,128)(2,1)S(1)}, u32[]{:S(2)}, u32[]{:S(2)}) collective-permute-start(bf16[512,640]{1,0:T(8,128)(2,1)S(1)} %add.318), channel_id=1, source_target_pairs={{4,8},{8,4},{5,9},{9,5},{6,10},{10,6},{7,11},{11,7},{20,24},{24,20... | collective-permute-start | bytes 1966088 | tf_op jit(solution)/shard_map/ppermute | solution.py:145
  608.0 27.5 %collective-permute-start.65 = (bf16[528,640]{1,0:T(8,128)(2,1)}, bf16[528,640]{1,0:T(8,128)(2,1)}, u32[]{:S(2)}, u32[]{:S(2)}) collective-permute-start(bf16[528,640]{1,0:T(8,128)(2,1)} %add.316), channel_id=1, source_target_pairs={{4,8},{8,4},{5,9},{9,5},{6,10},{10,6},{7,11},{11,7},{20,24},{24,20... | collective-permute-start | bytes 2027528 | tf_op jit(solution)/shard_map/ppermute | solution.py:145
  612.5 52.2 %collective-permute-start.40 = (bf16[256,2048]{1,0:T(8,128)(2,1)S(1)}, bf16[256,2048]{1,0:T(8,128)(2,1)}, u32[]{:S(2)}, u32[]{:S(2)}) collective-permute-start(bf16[256,2048]{1,0:T(8,128)(2,1)S(1)} %pad_maximum_fusion.7.first), channel_id=1, source_target_pairs={{0,1},{1,0},{2,3},{3,2},{4,5},{5,4},{6,7},{7,6},{8,9},{9,8},{10,11... | collective-permute-start | bytes 3145736 | tf_op jit(solution)/shard_map/ppermute | solution.py:43
  623.0 41.5 %collective-permute-start.68 = (bf16[512,640]{1,0:T(8,128)(2,1)S(1)}, bf16[512,640]{1,0:T(8,128)(2,1)}, u32[]{:S(2)}, u32[]{:S(2)}) collective-permute-start(bf16[512,640]{1,0:T(8,128)(2,1)S(1)} %add.319), channel_id=1, source_target_pairs={{4,0},{8,12},{5,1},{9,13},{6,2},{10,14},{7,3},{11,15},{20,16},{24,... | collective-permute-start | bytes 1966088 | tf_op jit(solution)/shard_map/ppermute | solution.py:146
  637.8 31.7 %collective-permute-start.66 = (bf16[528,640]{1,0:T(8,128)(2,1)}, bf16[528,640]{1,0:T(8,128)(2,1)}, u32[]{:S(2)}, u32[]{:S(2)}) collective-permute-start(bf16[528,640]{1,0:T(8,128)(2,1)} %add.317), channel_id=1, source_target_pairs={{4,0},{8,12},{5,1},{9,13},{6,2},{10,14},{7,3},{11,15},{20,16},{24,... | collective-permute-start | bytes 2027528 | tf_op jit(solution)/shard_map/ppermute | solution.py:146
  (119 other events, 967.9 us)
Sparse Core Ops, SparseCore 0:
  83.6 37.9 all-gather.5
  123.2 35.9 all-gather.7
  204.3 36.1 reduce-scatter.7
  243.2 34.2 reduce-scatter.3
  278.9 47.8 all-gather.9
  329.5 46.4 reduce-scatter.5
  387.4 57.6 all-gather.11
  446.7 47.4 all-gather.13
